TPU v7x, 256 devices: a whole 4x4x8 slice. The times are simulated.
256 devices in a mesh: row: 8 (over z_lo, core), col: 32 (over x, z_hi, y).
Axes of the slice: x: 4, y: 4, z: 8 (z_hi: 2, z_lo: 4; z = z_hi * 4 + z_lo), core: 2. Of those that a mesh axis runs over, the one named last changes fastest.
Arguments:
- alignment: bfloat16 [512, 1024, 256], P('col', 'row'), may hold values from -8 to 8, as said below
- column_mask: int32 [512, 1024], replicated, may hold values from 0 to 1, as said below
- chain_index: int32 [1024], replicated, may hold values from 0 to 3, never falling along the last dimension, each value on 1 to 512 neighbouring positions
- attention_norm_gain: float32 [256], replicated, may hold values from 0.1 to 1.9
- query_weight: bfloat16 [256, 256], replicated, may hold values from -2 to 2
- key_weight: bfloat16 [256, 256], replicated, may hold values from -2 to 2
- value_matrix: bfloat16 [256, 256], replicated, may hold values from -0.375 to 0.375
- gate_matrix: bfloat16 [256, 256], replicated, may hold values from -0.375 to 0.375
- gate_bias: float32 [256], replicated, may hold values from -4 to 4
- attention_output_weight: bfloat16 [256, 256], replicated, may hold values from -0.375 to 0.375
- attention_output_bias: float32 [256], replicated, may hold values from -3 to 3
- outer_norm_gain: float32 [256], replicated, may hold values from 0.1 to 1.9
- left_factor_weight: bfloat16 [256, 32], replicated, may hold values from -0.375 to 0.375
- right_factor_weight: bfloat16 [256, 32], replicated, may hold values from -0.375 to 0.375
- pair_weight: bfloat16 [1024, 128], replicated, may hold values from -0.1875 to 0.1875
- chain_bias: float32 [128], replicated, may hold values from -4 to 4
Outputs:
- updated_alignment: bfloat16 [512, 1024, 256], P(None, ('row', 'col'))
- pair_update: bfloat16 [1024, 1024, 128], P('row', 'col')
Inputs may be any that keep to these rules, and one draw needn't show every extreme that they name: `alignment`: aligned features: a per-residue profile shared by all sequences plus per-sequence variation. `column_mask`: row 0 (the query sequence) is 1 at every residue.
All inputs are finite; a program needn't handle non-finite values.
Results may differ from a plain program's by a relative error of at most 0.0089.
Values may be sent and summed in bfloat16 or wider, within the bound.
No kernel may reach another device: no remote copies, remote signals or barrier semaphores. Data moves between devices by JAX's collectives and lax.ppermute only.
A program may use at most 64 MiB of HBM per device.

v0:
```python
import math

import jax
import jax.numpy as jnp
from jax import lax
from jax.sharding import PartitionSpec as P

HEAD_COUNT = 8
HEAD_FEATURES = 32


def from_root(value, axis, source):
    kept = jnp.where(lax.axis_index(axis) == source, value, 0).astype(value.dtype)
    return lax.psum(kept, axis)


def layer_normalize(value_rows, gain):
    value_rows = value_rows.astype(jnp.float32)
    average = jnp.mean(value_rows, -1, keepdims=True)
    centred = value_rows - average
    variance = jnp.mean(centred * centred, -1, keepdims=True)
    return centred * lax.rsqrt(variance + 1e-05) * gain


def column_attention(
    block_row_count,
    mask_rows,
    attention_norm_gain,
    query_weight,
    key_weight,
    value_matrix,
    gate_matrix,
    gate_bias,
    attention_output_weight,
    attention_output_bias,
):
    sequence_total, residue_count, alignment_width = block_row_count.shape
    normed_alignment = (
        layer_normalize(block_row_count, attention_norm_gain)
        .astype(jnp.bfloat16)
        .reshape(sequence_total * residue_count, alignment_width)
    )

    def project(weight):
        product = jnp.dot(normed_alignment, weight, preferred_element_type=jnp.float32)
        return product.astype(jnp.bfloat16).reshape(
            sequence_total, residue_count, HEAD_COUNT, HEAD_FEATURES
        )

    queries = project(query_weight)
    keys_all = project(key_weight)
    values_all = project(value_matrix)
    gates = jax.nn.sigmoid(
        jnp.dot(normed_alignment, gate_matrix, preferred_element_type=jnp.float32) + gate_bias
    )
    gates = gates.reshape(sequence_total, residue_count, HEAD_COUNT * HEAD_FEATURES)

    def attend_one(residue):
        query_col = lax.dynamic_index_in_dim(queries, residue, 1, keepdims=False)
        key_col = lax.dynamic_index_in_dim(keys_all, residue, 1, keepdims=False)
        value_col = lax.dynamic_index_in_dim(values_all, residue, 1, keepdims=False)
        scores = jnp.einsum(
            "shd,thd->hst", query_col, key_col, preferred_element_type=jnp.float32
        ) * HEAD_FEATURES ** (-0.5)
        live = lax.dynamic_index_in_dim(mask_rows, residue, 1, keepdims=False)
        scores = jnp.where(live[None, None, :] > 0, scores, jnp.float32(-1000000000.0))
        weights = jax.nn.softmax(scores, axis=-1).astype(jnp.bfloat16)
        mixed = jnp.einsum("hst,thd->shd", weights, value_col, preferred_element_type=jnp.float32)
        gate_col = lax.dynamic_index_in_dim(gates, residue, 1, keepdims=False)
        return (mixed.reshape(sequence_total, HEAD_COUNT * HEAD_FEATURES) * gate_col).astype(
            jnp.bfloat16
        )

    gated_output = lax.map(attend_one, jnp.arange(residue_count, dtype=jnp.int32))
    gated_output = jnp.swapaxes(gated_output, 0, 1).reshape(
        sequence_total * residue_count, HEAD_COUNT * HEAD_FEATURES
    )
    projected_output = jnp.dot(
        gated_output, attention_output_weight, preferred_element_type=jnp.float32
    ).reshape(sequence_total, residue_count, alignment_width)
    return (projected_output + attention_output_bias + block_row_count.astype(jnp.float32)).astype(
        jnp.bfloat16
    )


def body(
    alignment,
    column_mask,
    chain_index,
    attention_norm_gain,
    query_weight,
    key_weight,
    value_matrix,
    gate_matrix,
    gate_bias,
    attention_output_weight,
    attention_output_bias,
    outer_norm_gain,
    left_factor_weight,
    right_factor_weight,
    pair_weight,
    chain_bias,
):
    col_devices = lax.axis_size("col")
    row_devices = lax.axis_size("row")
    col_place = lax.axis_index("col")
    row_place = lax.axis_index("row")
    regrouped_heads = lax.all_to_all(alignment, "col", split_axis=1, concat_axis=0, tiled=True)
    sequence_total, residues_per_device, alignment_width = regrouped_heads.shape
    own_first = (row_place * col_devices + col_place) * residues_per_device
    own_mask = lax.dynamic_slice_in_dim(column_mask, own_first, residues_per_device, 1)
    updated_rows = column_attention(
        regrouped_heads,
        own_mask,
        attention_norm_gain,
        query_weight,
        key_weight,
        value_matrix,
        gate_matrix,
        gate_bias,
        attention_output_weight,
        attention_output_bias,
    )
    outer_normed_alignment = (
        layer_normalize(updated_rows, outer_norm_gain)
        .astype(jnp.bfloat16)
        .reshape(sequence_total * residues_per_device, alignment_width)
    )
    mask_float = own_mask.astype(jnp.float32)[:, :, None]
    left = (
        jnp.dot(
            outer_normed_alignment, left_factor_weight, preferred_element_type=jnp.float32
        ).reshape(sequence_total, residues_per_device, -1)
        * mask_float
    ).astype(jnp.bfloat16)
    right = (
        jnp.dot(
            outer_normed_alignment, right_factor_weight, preferred_element_type=jnp.float32
        ).reshape(sequence_total, residues_per_device, -1)
        * mask_float
    ).astype(jnp.bfloat16)
    factor_width = left.shape[2]
    band_rows = residues_per_device * row_devices
    row_band = residues_per_device * col_devices
    col_per_row = col_devices // row_devices
    within = col_place % col_per_row
    row_block = lax.all_gather(right, "col", axis=1, tiled=True)
    own_part = lax.dynamic_slice_in_dim(row_block, within * band_rows, band_rows, 1)
    right_cols = from_root(own_part, "row", col_place // col_per_row)
    col_first = col_place * band_rows
    row_first = row_place * row_band
    mask_cols = lax.dynamic_slice_in_dim(column_mask, col_first, band_rows, 1).astype(jnp.float32)
    chain_cols = lax.dynamic_slice_in_dim(chain_index, col_first, band_rows, 0)

    def make_rows(shard_rows, first_row):
        row_count = shard_rows.shape[1]
        outer_product = jnp.einsum(
            "sip,sjq->ijpq", shard_rows, right_cols, preferred_element_type=jnp.float32
        )
        outer_product = outer_product.astype(jnp.bfloat16).reshape(
            row_count * band_rows, factor_width * factor_width
        )
        projected_output = jnp.dot(
            outer_product, pair_weight, preferred_element_type=jnp.float32
        ).reshape(row_count, band_rows, -1)
        mask_rows = lax.dynamic_slice_in_dim(
            column_mask, row_first + first_row, row_count, 1
        ).astype(jnp.float32)
        counts = jnp.dot(mask_rows.T, mask_cols, precision=lax.Precision.HIGHEST)
        chain_rows = lax.dynamic_slice_in_dim(chain_index, row_first + first_row, row_count, 0)
        same_chain = (chain_rows[:, None] == chain_cols[None, :]).astype(jnp.float32)
        result = (
            projected_output / (counts + 0.001)[:, :, None] + same_chain[:, :, None] * chain_bias
        )
        return result.astype(jnp.bfloat16)

    left_rows = lax.all_gather(left, "col", axis=1, tiled=True)
    block_size = math.gcd(32, row_band)

    def pair_block_rows(block_index):
        first_row = block_index * block_size
        shard_rows = lax.dynamic_slice_in_dim(left_rows, first_row, block_size, 1)
        return make_rows(shard_rows, first_row)

    pair_update = lax.map(pair_block_rows, jnp.arange(row_band // block_size, dtype=jnp.int32))
    pair_update = pair_update.reshape(row_band, band_rows, -1)
    return (updated_rows, pair_update)


def solution(mesh):
    return jax.shard_map(
        body,
        mesh=mesh,
        in_specs=(
            P("col", "row", None),
            P(),
            P(),
            P(),
            P(),
            P(),
            P(),
            P(),
            P(),
            P(),
            P(),
            P(),
            P(),
            P(),
            P(),
            P(),
        ),
        out_specs=(P(None, ("row", "col"), None), P("row", "col", None)),
        check_vma=False,
    )
```

profile of v0, /device:TPU:38, one launch (start us, length us, event | category | flops | bytes accessed | tf_op | source)
XLA Modules:
  0.0 561.7 jit_solution(12102542404875830417)
XLA Ops:
  7.2 2.8 copy.78
  10.0 13.3 %all-to-all-start = ((bf16[16,128,256]{2,0,1:T(8,128)(2,1)}), bf16[16,128,256]{2,0,1:T(8,128)(2,1)S(1)}, u32[]{:S(2)}, u32[]{:S(2)}) async-start(bf16[16,128,256]{2,0,1:T(8,128)(2,1)} %copy.78), calls=%async_computation | async-start | bytes 2097152 | tf_op jit(solution)/shard_map/all_to_all | solution.py:108
  23.4 1.1 constant_dynamic-slice_fusion.1
  25.2 28.1 %all-to-all-done = bf16[16,128,256]{2,0,1:T(8,128)(2,1)S(1)} async-done(((bf16[16,128,256]{2,0,1:T(8,128)(2,1)}), bf16[16,128,256]{2,0,1:T(8,128)(2,1)S(1)}, u32[]{:S(2)}, u32[]{:S(2)}) %all-to-all-start) | async-done | bytes 1048608 | tf_op jit(solution)/shard_map/all_to_all | solution.py:108
  53.8 3.1 copy.79
  58.7 1.0 copy.81
  59.7 1.9 copy.93
  61.6 2.0 reshape.168
  63.5 2.1 multiply_reduce_fusion
  65.7 0.9 copy.83
  67.0 0.8 div.42
  67.7 1.4 multiply_convert_fusion
  69.1 1.3 convolution_convert_fusion.2
  70.5 3.3 reshape.163
  73.8 5.3 copy.86
  79.6 3.3 reshape.164
  82.9 5.3 copy.87
  88.6 3.3 reshape.165
  92.0 5.3 copy.88
  97.2 2.1 fusion.52
  99.3 1.9 reshape.166
  101.2 65.2 %while.20 = (s32[]{:T(128)}, bf16[4,512,256]{1,2,0:T(8,128)(2,1)}, s32[4]{0:T(128)S(1)}, bf16[512,4,8,32]{0,3,2,1:T(8,128)(2,1)}, s32[512,4]{0,1:T(4,128)S(1)}, ...) while((s32[]{:T(128)}, bf16[4,512,256]{1,2,0:T(8,128)(2,1)}, ...), condition=%wide.region_5.6_spmd, body=%wide.region_2.5_spmd.sunk | while | flops 281281536 | bytes 21532852 | solution.py:74
  104.8 7.7 %fusion.101 = (f32[8,512]{1,0:T(8,128)S(1)}, f32[8,512,512]{1,2,0:T(8,128)}) fusion(pred[512]{0:T(512)(128)(4,1)S(1)} %compare_reduce_fusion.2, bf16[512,4,8,32]{0,3,2,1:T(8,128)(2,1)} %get-tuple-element.356, s32[]{:T(128)S(6)} %select_n.74, bf16[512,4,8,32]{0,3,2,1:T(8,128)(2,1)} %get-tuple-element.355), kind=kOutput, calls=%fused_computation.82.clone.1 | convolution fusion | flops 142606848 | bytes 8930816 | tf_op jit(solution)/shard_map/while/body/eval_jaxpr/sub | solution.py:67
  112.5 4.3 fusion.102
  116.8 0.8 constant_dynamic-update-slice_fusion.2
  121.1 7.7 %fusion.101 = (f32[8,512]{1,0:T(8,128)S(1)}, f32[8,512,512]{1,2,0:T(8,128)}) fusion(pred[512]{0:T(512)(128)(4,1)S(1)} %compare_reduce_fusion.2, bf16[512,4,8,32]{0,3,2,1:T(8,128)(2,1)} %get-tuple-element.356, s32[]{:T(128)S(6)} %select_n.74, bf16[512,4,8,32]{0,3,2,1:T(8,128)(2,1)} %get-tuple-element.355), kind=kOutput, calls=%fused_computation.82.clone.1 | convolution fusion | flops 142606848 | bytes 8930816 | tf_op jit(solution)/shard_map/while/body/eval_jaxpr/sub | solution.py:67
  128.8 4.3 fusion.102
  133.1 0.8 constant_dynamic-update-slice_fusion.2
  137.3 7.7 %fusion.101 = (f32[8,512]{1,0:T(8,128)S(1)}, f32[8,512,512]{1,2,0:T(8,128)}) fusion(pred[512]{0:T(512)(128)(4,1)S(1)} %compare_reduce_fusion.2, bf16[512,4,8,32]{0,3,2,1:T(8,128)(2,1)} %get-tuple-element.356, s32[]{:T(128)S(6)} %select_n.74, bf16[512,4,8,32]{0,3,2,1:T(8,128)(2,1)} %get-tuple-element.355), kind=kOutput, calls=%fused_computation.82.clone.1 | convolution fusion | flops 142606848 | bytes 8930816 | tf_op jit(solution)/shard_map/while/body/eval_jaxpr/sub | solution.py:67
  145.0 4.3 fusion.102
  149.3 0.8 constant_dynamic-update-slice_fusion.2
  153.6 7.7 %fusion.101 = (f32[8,512]{1,0:T(8,128)S(1)}, f32[8,512,512]{1,2,0:T(8,128)}) fusion(pred[512]{0:T(512)(128)(4,1)S(1)} %compare_reduce_fusion.2, bf16[512,4,8,32]{0,3,2,1:T(8,128)(2,1)} %get-tuple-element.356, s32[]{:T(128)S(6)} %select_n.74, bf16[512,4,8,32]{0,3,2,1:T(8,128)(2,1)} %get-tuple-element.355), kind=kOutput, calls=%fused_computation.82.clone.1 | convolution fusion | flops 142606848 | bytes 8930816 | tf_op jit(solution)/shard_map/while/body/eval_jaxpr/sub | solution.py:67
  161.3 4.3 fusion.102
  165.6 0.8 constant_dynamic-update-slice_fusion.2
  166.4 2.5 convert_reduce_fusion
  169.3 1.1 fusion.59
  170.5 1.1 fusion.58
  171.8 104.7 %all-gather.5.cloned.1.call-done = bf16[512,128,32]{0,2,1:T(8,128)(2,1)} async-done(((bf16[512,4,32]{0,2,1:T(8,128)(2,1)}), bf16[512,128,32]{0,2,1:T(8,128)(2,1)}) %all-gather.5.cloned.1.call-update) | async-done | bytes 4194320 | tf_op jit(solution)/shard_map/all_gather | solution.py:147
  276.4 2.3 dynamic-slice_select_fusion
  278.7 0.8 dynamic_slice.49
  279.5 1.1 dynamic-slice_convert_fusion
  280.6 1.4 copy.96
  282.0 103.7 %all-gather.3.cloned.1.call-done = bf16[512,128,32]{0,2,1:T(8,128)(2,1)} async-done(((bf16[512,4,32]{0,2,1:T(8,128)(2,1)}), bf16[512,128,32]{0,2,1:T(8,128)(2,1)}) %all-gather.3.cloned.1.call-update) | async-done | bytes 4194320 | tf_op jit(solution)/shard_map/all_gather | solution.py:177
  385.7 70.4 %all-reduce.2.cloned.1.call-done = bf16[512,32,32]{0,2,1:T(8,128)(2,1)} async-done(((bf16[512,32,32]{0,2,1:T(8,128)(2,1)}), bf16[512,32,32]{0,2,1:T(8,128)(2,1)}) %all-reduce.2.cloned.1.call-update) | async-done | bytes 1048592 | tf_op jit(solution)/shard_map/psum | solution.py:14
  456.1 98.1 %while.21 = (s32[]{:T(128)}, bf16[4,32,32,128]{3,2,1,0:T(8,128)(2,1)}, s32[4]{0:T(128)S(1)}, bf16[512,128,32]{0,2,1:T(8,128)(2,1)}, bf16[512,32,32]{0,2,1:T(8,12...) while((s32[]{:T(128)}, ...), condition=%wide.region_10.11_spmd, body=%wide.region_9.10_spmd.sunk | while | flops 1350061056 | bytes 11355421 | solution.py:185
  457.4 8.1 %convert_bitcast_fusion.3 = bf16[32,32,32,32]{3,2,1,0:T(8,128)(2,1)} fusion(bf16[512,32,32]{0,2,1:T(8,128)(2,1)} %get-tuple-element.399, bf16[512,128,32]{0,2,1:T(8,128)(2,1)} %get-tuple-element.398, s32[]{:T(128)S(6)} %select_n.75), kind=kOutput, calls=%fused_computation.clone.1 | convolution fusion | flops 1074790400 | bytes 4194308 | tf_op jit(solution)/shard_map/while/body/eval_jaxpr/sip,sjq->ijpq/dot_general | solution.py:157
  465.4 11.3 %dot_general.46 = bf16[32,32,1024]{2,1,0:T(8,128)(2,1)S(1)} reshape(bf16[32,32,32,32]{3,2,1,0:T(8,128)(2,1)} %convert_bitcast_fusion.3) | data formatting | bytes 4194304 | tf_op jit(solution)/shard_map/while/body/eval_jaxpr/dot_general | solution.py:163
  476.8 0.8 dynamic_slice.118
  477.6 1.6 convolution_add_fusion.3
  479.2 1.4 fusion.109
  481.9 8.1 %convert_bitcast_fusion.3 = bf16[32,32,32,32]{3,2,1,0:T(8,128)(2,1)} fusion(bf16[512,32,32]{0,2,1:T(8,128)(2,1)} %get-tuple-element.399, bf16[512,128,32]{0,2,1:T(8,128)(2,1)} %get-tuple-element.398, s32[]{:T(128)S(6)} %select_n.75), kind=kOutput, calls=%fused_computation.clone.1 | convolution fusion | flops 1074790400 | bytes 4194308 | tf_op jit(solution)/shard_map/while/body/eval_jaxpr/sip,sjq->ijpq/dot_general | solution.py:157
  490.0 11.3 %dot_general.46 = bf16[32,32,1024]{2,1,0:T(8,128)(2,1)S(1)} reshape(bf16[32,32,32,32]{3,2,1,0:T(8,128)(2,1)} %convert_bitcast_fusion.3) | data formatting | bytes 4194304 | tf_op jit(solution)/shard_map/while/body/eval_jaxpr/dot_general | solution.py:163
  502.1 1.6 convolution_add_fusion.3
  503.8 1.4 fusion.109
  506.4 8.1 %convert_bitcast_fusion.3 = bf16[32,32,32,32]{3,2,1,0:T(8,128)(2,1)} fusion(bf16[512,32,32]{0,2,1:T(8,128)(2,1)} %get-tuple-element.399, bf16[512,128,32]{0,2,1:T(8,128)(2,1)} %get-tuple-element.398, s32[]{:T(128)S(6)} %select_n.75), kind=kOutput, calls=%fused_computation.clone.1 | convolution fusion | flops 1074790400 | bytes 4194308 | tf_op jit(solution)/shard_map/while/body/eval_jaxpr/sip,sjq->ijpq/dot_general | solution.py:157
  514.5 11.3 %dot_general.46 = bf16[32,32,1024]{2,1,0:T(8,128)(2,1)S(1)} reshape(bf16[32,32,32,32]{3,2,1,0:T(8,128)(2,1)} %convert_bitcast_fusion.3) | data formatting | bytes 4194304 | tf_op jit(solution)/shard_map/while/body/eval_jaxpr/dot_general | solution.py:163
  526.7 1.6 convolution_add_fusion.3
  528.3 1.4 fusion.109
  531.0 8.1 %convert_bitcast_fusion.3 = bf16[32,32,32,32]{3,2,1,0:T(8,128)(2,1)} fusion(bf16[512,32,32]{0,2,1:T(8,128)(2,1)} %get-tuple-element.399, bf16[512,128,32]{0,2,1:T(8,128)(2,1)} %get-tuple-element.398, s32[]{:T(128)S(6)} %select_n.75), kind=kOutput, calls=%fused_computation.clone.1 | convolution fusion | flops 1074790400 | bytes 4194308 | tf_op jit(solution)/shard_map/while/body/eval_jaxpr/sip,sjq->ijpq/dot_general | solution.py:157
  539.0 11.3 %dot_general.46 = bf16[32,32,1024]{2,1,0:T(8,128)(2,1)S(1)} reshape(bf16[32,32,32,32]{3,2,1,0:T(8,128)(2,1)} %convert_bitcast_fusion.3) | data formatting | bytes 4194304 | tf_op jit(solution)/shard_map/while/body/eval_jaxpr/dot_general | solution.py:163
  550.4 0.8 dynamic_slice.118
  551.2 1.6 convolution_add_fusion.3
  552.8 1.4 fusion.109
  554.3 0.9 copy-done.1
  (79 shorter events, 16.0 us)
Async XLA Ops:
  7.2 159.3 %copy-start = (bf16[256,256]{1,0:T(8,128)(2,1)S(1)}, bf16[256,256]{1,0:T(8,128)(2,1)}, u32[]{:S(2)}) copy-start(bf16[256,256]{1,0:T(8,128)(2,1)} %param.29) | copy-start | bytes 393220
  10.0 43.3 %all-to-all-start = ((bf16[16,128,256]{2,0,1:T(8,128)(2,1)}), bf16[16,128,256]{2,0,1:T(8,128)(2,1)S(1)}, u32[]{:S(2)}, u32[]{:S(2)}) async-start(bf16[16,128,256]{2,0,1:T(8,128)(2,1)} %copy.78), calls=%async_computation | async-start | bytes 2097152 | tf_op jit(solution)/shard_map/all_to_all | solution.py:108
  23.3 253.1 %all-gather.5.cloned.1.call-start = ((), (), s32[]{:S(2)}) async-start(), calls=%async_computation.2 | async-start | bytes 4325376 | tf_op jit(solution)/shard_map/all_gather | solution.py:147
  57.4 0.6 copy-start.2
  73.8 5.3 copy-start.3
  82.9 5.3 copy-start.4
  91.9 5.3 copy-start.8
  91.9 5.3 copy-start.11
  101.2 65.2 %copy-start.6 = (f32[256]{0:T(256)S(1)}, f32[256]{0:T(256)}, u32[]{:S(2)}) copy-start(f32[256]{0:T(256)} %param.30) | copy-start | bytes 3076
  166.4 2.9 copy-start.5
  166.4 2.9 copy-start.9
  166.4 2.9 copy-start.12
  169.0 1.6 copy-start.10
  170.5 215.2 %all-gather.3.cloned.1.call-start = ((), (), s32[]{:S(2)}) async-start(), calls=%async_computation.1 | async-start | bytes 4325376 | tf_op jit(solution)/shard_map/all_gather | solution.py:177
  171.7 284.4 %all-reduce.2.cloned.1.call-start = ((), (), s32[]{:S(2)}) async-start(), calls=%async_computation.3 | async-start | bytes 2097152 | tf_op jit(solution)/shard_map/psum | solution.py:14
  278.7 177.4 %copy-start.7 = (bf16[1024,128]{1,0:T(8,128)(2,1)S(1)}, bf16[1024,128]{1,0:T(8,128)(2,1)}, u32[]{:S(2)}) copy-start(bf16[1024,128]{1,0:T(8,128)(2,1)} %param.34) | copy-start | bytes 786436
  278.7 177.4 %copy-start.13 = (f32[128]{0:T(128)S(1)}, f32[128]{0:T(128)}, u32[]{:S(2)}) copy-start(f32[128]{0:T(128)} %param.35) | copy-start | bytes 1540
  554.3 0.9 copy-start.1
Sparse Core Ops, SparseCore 0:
  170.6 105.7 all-gather.4
  279.9 105.7 all-gather.2
  388.4 67.7 all-reduce.1
where the time goes:
time: 567 us; the launch traced here: 562 us
  waiting for transfers between devices  307 us (54%)
  local copies, waits for them, and re-layouts  104 us (18%)
  matrix products  101 us (18%)
  between operations  14 us (2%)
  starting transfers between devices  13.5 us (2%)
  other arithmetic  12.2 us (2%)
  loops' own time  9.67 us (2%)
    all_gather x1, waiting for transfers between devices, body(): row_block = lax.all_gather(right, 'col', axis=1, tiled=True)  105 us
    all_gather x1, waiting for transfers between devices, body(): left_rows = lax.all_gather(left, 'col', axis=1, tiled=True)  104 us
    psum x1, waiting for transfers between devices, from_root(): return lax.psum(kept, axis)  70.4 us
    dot_general x4, local copies, waits for them, and re-layouts, make_rows(): jnp.dot(outer_product, pair_weight, preferred_element_type=jnp.float32)  45.3 us
    dot_general x4, matrix products, make_rows(): jnp.einsum('sip,sjq->ijpq', shard_rows, right_cols, preferred_element_typ...  32.2 us
    sub x4, matrix products, attend_one(): weights = jax.nn.softmax(scores, axis=-1).astype(jnp.bfloat16)  30.8 us
    all_to_all x1, waiting for transfers between devices, body(): lax.all_to_all(alignment, 'col', split_axis=1, concat_axis=0, tiled=True)  28.1 us
    dot_general x4, matrix products, attend_one(): jnp.einsum('hst,thd->shd', weights, value_col, preferred_element_type=jnp...  17.3 us
  transfers between devices with their start and end apart: 4, of which 4 were waited for; matrix products, arithmetic and copies ran while one was open for 2% of the time, Pallas kernels for 0%

commit v1 on v0

v1 whole, which is shorter than its diff:
```python
import functools
import math

import jax
import jax.numpy as jnp
import numpy as np
from jax import lax
from jax.experimental import pallas as pl
from jax.experimental.pallas import tpu as pltpu
from jax.sharding import PartitionSpec as P

HEAD_COUNT = 8
HEAD_FEATURES = 32
NT = (((1,), (1,)), ((), ()))
F32, BF16 = jnp.float32, jnp.bfloat16
SB = 128

def norm_rows(x, gain):
    average = jnp.mean(x, -1, keepdims=True)
    centred = x - average
    variance = jnp.mean(centred * centred, -1, keepdims=True)
    return centred * lax.rsqrt(variance + 1e-05) * gain

def dot(a, b):
    return jnp.dot(a, b, preferred_element_type=F32)

def dot_nt(a, b):
    return lax.dot_general(a, b, NT, preferred_element_type=F32)

def attend_kernel(x_ref, kbias_ref, mask_ref, gain1_ref, wqkvg_ref, gbias_ref, wo_ref, obias_ref, gain2_ref, wlr_ref,
                  up_ref, left_ref, right_ref, qa_ref, ka_ref, va_ref, gated_ref):
    rows, width = qa_ref.shape[1], x_ref.shape[-1]
    x = x_ref[...].reshape(rows, width).astype(F32)
    normed = norm_rows(x, gain1_ref[...]).astype(BF16)
    scale = math.log2(math.e) * HEAD_FEATURES ** (-0.5)
    lane = lax.broadcasted_iota(jnp.int32, (1, 128), 1)
    first = jnp.broadcast_to(jnp.where(lane == 0, 1.0, 0.0).astype(BF16), (rows, 128))
    kbias = kbias_ref[...].reshape(rows, 128)
    queries = (dot(normed, wqkvg_ref[:, 0:256]) * scale).astype(BF16)
    keys = dot(normed, wqkvg_ref[:, 256:512]).astype(BF16)
    values = dot(normed, wqkvg_ref[:, 512:768]).astype(BF16)
    for g in range(2):
        qa_ref[g] = jnp.concatenate([queries[:, g * 128:(g + 1) * 128], first], axis=1)
        for h in range(4):
            on = (lane // 32 == h)
            kept = jnp.where(on, 1.0, 0.0).astype(BF16)
            ka_ref[g * 4 + h] = jnp.concatenate([keys[:, g * 128:(g + 1) * 128] * kept, kbias], axis=1)
            va_ref[g, h * rows:(h + 1) * rows, :] = jnp.concatenate(
                [values[:, g * 128:(g + 1) * 128] * kept, jnp.broadcast_to(kept, (rows, 128))], axis=1)
    gates = jax.nn.sigmoid(dot(normed, wqkvg_ref[:, 768:1024]) + gbias_ref[...])
    gated_ref[...] = gates
    for g in range(2):
        for b in range(rows // SB):
            q = qa_ref[g, b * SB:(b + 1) * SB, :]
            total = None
            for h in range(4):
                s = dot_nt(q, ka_ref[g * 4 + h])
                m = jnp.max(s, axis=-1, keepdims=True)
                p = jnp.exp2(s - m).astype(BF16)
                part = dot(p, va_ref[g, h * rows:(h + 1) * rows, :])
                total = part if total is None else total + part
            out = total[:, :128] / total[:, 128:]
            sl = (slice(b * SB, (b + 1) * SB), slice(g * 128, (g + 1) * 128))
            gated_ref[sl] = gated_ref[sl] * out
    gated = gated_ref[...].astype(BF16)
    updated = (dot(gated, wo_ref[...]) + obias_ref[...] + x).astype(BF16)
    up_ref[...] = updated.reshape(up_ref.shape)
    again = norm_rows(updated.astype(F32), gain2_ref[...]).astype(BF16)
    factors = dot_nt(wlr_ref[...], again) * mask_ref[...].reshape(1, rows)
    left_ref[...] = factors[:32].astype(BF16).reshape(left_ref.shape)
    right_ref[...] = factors[32:].astype(BF16).reshape(right_ref.shape)

def attend(x, kbias, mask, gain1, wqkvg, gbias, wo, obias, gain2, wlr_t):
    groups, count, per, width = x.shape
    rows = groups * per
    whole = lambda a: pl.BlockSpec(a.shape, lambda k: (0,) * a.ndim)
    return pl.pallas_call(
        attend_kernel,
        grid=(count,),
        in_specs=[
            pl.BlockSpec((groups, 1, per, width), lambda k: (0, k, 0, 0)),
            pl.BlockSpec((1, rows, 128), lambda k: (k, 0, 0)),
            pl.BlockSpec((1, 1, rows), lambda k: (k, 0, 0)),
            whole(gain1), whole(wqkvg), whole(gbias), whole(wo), whole(obias), whole(gain2), whole(wlr_t),
        ],
        out_specs=[
            pl.BlockSpec((1, rows, width), lambda k: (k, 0, 0)),
            pl.BlockSpec((1, 32, rows), lambda k: (k, 0, 0)),
            pl.BlockSpec((1, 32, rows), lambda k: (k, 0, 0)),
        ],
        out_shape=[
            jax.ShapeDtypeStruct((count, rows, width), BF16),
            jax.ShapeDtypeStruct((count, 32, rows), BF16),
            jax.ShapeDtypeStruct((count, 32, rows), BF16),
        ],
        scratch_shapes=[
            pltpu.VMEM((2, rows, 256), BF16),
            pltpu.VMEM((8, rows, 256), BF16),
            pltpu.VMEM((2, 4 * rows, 256), BF16),
            pltpu.VMEM((rows, 256), F32),
        ],
        compiler_params=pltpu.CompilerParams(vmem_limit_bytes=48 * 1024 * 1024),
        cost_estimate=pl.CostEstimate(flops=count * 4 * 10**9, bytes_accessed=count * 10**6, transcendentals=count * 2 * 10**6),
    )(x, kbias, mask, gain1, wqkvg, gbias, wo, obias, gain2, wlr_t)


def rearrange_kernel(order_ref, r_ref, out_ref, f_ref):
    for n in range(8):
        first = pl.multiple_of(order_ref[n] * 128, 128)
        r = r_ref[n].reshape(128, 512).astype(F32)
        for c in range(4):
            f_ref[c, pl.ds(first, 128), :] = r[:, c * 128:(c + 1) * 128]
    for b in range(8):
        for c in range(4):
            part = jnp.concatenate(
                [f_ref[c, pl.ds(b * 4 + a, 32, stride=32), :] for a in range(4)], axis=0
            )
            out_ref[c * 128:(c + 1) * 128, b * 128:(b + 1) * 128] = part.T.astype(BF16)


def rearrange(order, right):
    return pl.pallas_call(
        rearrange_kernel,
        in_specs=[pl.BlockSpec(memory_space=pltpu.SMEM), pl.BlockSpec(memory_space=pltpu.VMEM)],
        out_shape=jax.ShapeDtypeStruct((512, 1024), BF16),
        scratch_shapes=[pltpu.VMEM((4, 1024, 128), F32)],
        compiler_params=pltpu.CompilerParams(vmem_limit_bytes=48 * 1024 * 1024),
        cost_estimate=pl.CostEstimate(flops=10**6, bytes_accessed=2 * 10**6, transcendentals=0),
    )(order, right)


def pair_kernel(count, place_ref, *refs):
    parts = refs[:count]
    r_ref, w_ref, inv_ref, bias_ref, old_ref, out_ref, x_ref = refs[count:]
    out_ref[...] = old_ref[...]
    slot = 0
    for part in parts:
        sources, per = part.shape[0], part.shape[1]
        group = 256 // (32 * per)
        for s0 in range(0, sources, group):
            outer = dot(part[s0:s0 + group].reshape(256, 512), r_ref[...]).astype(BF16)
            for n in range(8):
                a = jnp.concatenate(
                    [outer[n * 32:(n + 1) * 32, b * 128:(b + 1) * 128] for b in range(8)], axis=0
                )
                t = a.T
                for q in range(4):
                    x_ref[n * 32:(n + 1) * 32, q * 256:(q + 1) * 256] = t[q * 32:(q + 1) * 32, :]
            y = dot(x_ref[...], w_ref[...])
            rows = 32 * per
            for g in range(group):
                at = place_ref[slot]
                slot += 1
                first = pl.multiple_of(at * per, per)
                part_y = y[g * rows:(g + 1) * rows].reshape(per, 32, 128)
                result = part_y * inv_ref[pl.ds(first, per)] + bias_ref[pl.ds(first, per)]
                out_ref[pl.ds(first, per)] = result.astype(BF16)


def pair(place, parts, r, w, inv, bias, old):
    count = len(parts)
    whole = pl.BlockSpec(memory_space=pltpu.VMEM)
    n = sum(p.shape[0] * p.shape[1] for p in parts)
    return pl.pallas_call(
        functools.partial(pair_kernel, count),
        in_specs=[pl.BlockSpec(memory_space=pltpu.SMEM)] + [whole] * (count + 5),
        out_specs=whole,
        out_shape=jax.ShapeDtypeStruct(old.shape, BF16),
        scratch_shapes=[pltpu.VMEM((256, 1024), BF16)],
        input_output_aliases={count + 5: 0},
        compiler_params=pltpu.CompilerParams(vmem_limit_bytes=48 * 1024 * 1024),
        cost_estimate=pl.CostEstimate(flops=n * 6 * 10**7, bytes_accessed=n * 10**4 * 4, transcendentals=0),
    )(place, *parts, r, w, inv, bias, old)


def body(
    alignment, column_mask, chain_index, attention_norm_gain, query_weight, key_weight, value_matrix,
    gate_matrix, gate_bias, attention_output_weight, attention_output_bias, outer_norm_gain,
    left_factor_weight, right_factor_weight, pair_weight, chain_bias,
):
    row = lax.axis_index("row")
    col = lax.axis_index("col")
    moved = alignment.reshape(16, 32, 4, 256).transpose(1, 2, 0, 3)
    regrouped = lax.all_to_all(moved, "col", split_axis=0, concat_axis=0, tiled=True)

    own_mask = lax.dynamic_slice_in_dim(column_mask, row * 128 + col * 4, 4, 1).T
    kbias = jnp.pad(((own_mask - 1).astype(F32) * 1e9).astype(BF16)[:, :, None], ((0, 0), (0, 0), (0, 127)))
    mask_rows = own_mask.astype(F32).reshape(4, 1, 512)
    row_mask = lax.dynamic_slice_in_dim(column_mask, row * 128, 128, 1).astype(BF16)
    col_mask = lax.dynamic_slice_in_dim(column_mask, col * 32, 32, 1).astype(BF16)
    counts = lax.dot_general(row_mask, col_mask, (((0,), (0,)), ((), ())), preferred_element_type=F32)
    inverse = jnp.broadcast_to((1.0 / (counts + 0.001))[:, :, None], (128, 32, 128))
    row_chain = lax.dynamic_slice_in_dim(chain_index, row * 128, 128, 0)
    col_chain = lax.dynamic_slice_in_dim(chain_index, col * 32, 32, 0)
    same = (row_chain[:, None] == col_chain[None, :]).astype(F32)
    bias = same[:, :, None] * chain_bias
    wqkvg = jnp.concatenate([query_weight, key_weight, value_matrix, gate_matrix], axis=1)
    wlr = jnp.concatenate([left_factor_weight, right_factor_weight], axis=1).T
    wpair = pair_weight.reshape(32, 8, 4, 128).transpose(2, 1, 0, 3).reshape(1024, 128)

    up, left, right = attend(
        regrouped, kbias, mask_rows, attention_norm_gain[None], wqkvg, gate_bias[None],
        attention_output_weight, attention_output_bias[None], outer_norm_gain[None], wlr,
    )
    updated = up.transpose(1, 0, 2)

    moves = []
    for source in range(256):
        zl, co, x, zh, y = np.unravel_index(source, (4, 2, 4, 2, 4))
        moves.append((source, int(np.ravel_multi_index((y, zh, zl, co, x), (4, 2, 4, 2, 4)))))
    r0 = lax.ppermute(right, ("row", "col"), moves)

    def row_flip(value, bit):
        return lax.ppermute(value, "row", [(i, i ^ bit) for i in range(8)])

    def xy(value, axis, shift):
        perm = []
        for c in range(32):
            x, zh, y = c // 8, (c // 4) % 2, c % 4
            if axis == "x":
                x = (x + shift) % 4
            else:
                y = (y + shift) % 4
            perm.append((c, x * 8 + zh * 4 + y))
        return lax.ppermute(value, "col", perm)

    zp = lax.ppermute(left, "col", [(c, c ^ 4) for c in range(32)])
    both = jnp.stack([left, zp])
    h0, h1 = both[:, :2], both[:, 2:]
    b0 = jnp.concatenate([h0] + [xy(h0, "y", s) for s in (1, 2, 3)])
    b1 = jnp.concatenate([h1] + [xy(h1, "x", s) for s in (1, 2, 3)])
    c0 = [xy(b0, "x", s) for s in (1, 3, 2)]
    c1 = [xy(b1, "y", s) for s in (1, 3, 2)]

    ra = row_flip(r0, 2)
    rb = row_flip(jnp.stack([r0, ra]), 4)
    rc = jnp.concatenate([jnp.stack([r0, ra]), rb])
    rd = row_flip(rc, 1)
    gathered = jnp.stack([rc, rd])
    z_lo, core = row // 2, row % 2
    order = jnp.stack([(core ^ (n // 4)) * 4 + (z_lo ^ (n % 4)) for n in range(8)])
    r = rearrange(order.astype(jnp.int32), gathered.reshape(8, 4, 32, 512))

    x, zh, y = col // 8, (col // 4) % 2, col % 4
    shifts = (0, 1, 3, 2)

    def places(half, s):
        result = []
        for t in range(4):
            for z in range(2):
                if half == 0:
                    source = ((x - s) % 4) * 8 + (zh ^ z) * 4 + (y - t) % 4
                else:
                    source = ((x - t) % 4) * 8 + (zh ^ z) * 4 + (y - s) % 4
                result.append(source * 2 + half)
        return result

    out = jnp.zeros((128, 32, 128), BF16)
    for n, s in enumerate(shifts):
        p0, p1 = (b0, b1) if n == 0 else (c0[n - 1], c1[n - 1])
        place = jnp.stack(places(0, s) + places(1, s)).astype(jnp.int32)
        out = pair(place, [p0, p1], r, wpair, inverse, bias, out)
    return updated, out


def solution(mesh):
    return jax.shard_map(
        body,
        mesh=mesh,
        in_specs=(P("col", "row", None),) + (P(),) * 15,
        out_specs=(P(None, ("row", "col"), None), P("row", "col", None)),
        check_vma=False,
    )
```

time: 567 us -> 160 us (0.28)
  waiting for transfers between devices: 307 us -> 44.6 us
  matrix products: 101 us -> 1.33 us
  local copies, waits for them, and re-layouts: 104 us -> 11.3 us
  Pallas kernels: 0 us -> 54.3 us
  starting transfers between devices: 13.5 us -> 39.5 us
  between operations: 14 us -> 1.3 us
  loops' own time: 9.67 us -> 0 us
  other arithmetic: 12.2 us -> 4.47 us
    all_gather x2 -> x0, waiting for transfers between devices: 208 us -> none  [the longest x1 105 us: body(): row_block = lax.all_gather(right, 'col', axis=1, tiled=True)]
    psum x1 -> x0, waiting for transfers between devices: 70.4 us -> none  [from_root(): return lax.psum(kept, axis)]
    dot_general x23 -> x1, matrix products: 70.7 us -> 1.33 us  [body(): lax.dot_general(row_mask, col_mask, (((0,), (0,)), ((), ())), preferred_e...]
    pallas_call x0 -> x6, Pallas kernels: none -> 54.3 us  [the longest x1 29.9 us: attend(): pl.pallas_call(attend_kernel, grid=(count,), in_specs=[pl.BlockSpec((grou...]
    dot_general x4 -> x0, local copies, waits for them, and re-layouts: 45.3 us -> none  [make_rows(): jnp.dot(outer_product, pair_weight, preferred_element_type=jnp.float32)]
    sub x4 -> x0, matrix products: 30.8 us -> none  [attend_one(): weights = jax.nn.softmax(scores, axis=-1).astype(jnp.bfloat16)]
    ppermute x0 -> x17, starting transfers between devices: none -> 26 us  [the longest x12 20.2 us: xy(): return lax.ppermute(value, 'col', perm)]
    ppermute x0 -> x17, waiting for transfers between devices: none -> 16.6 us  [the longest x1 12.2 us: body(): r0 = lax.ppermute(right, ('row', 'col'), moves)]
  transfers between devices with their start and end apart: 4 -> 18, of which waited for: 4 -> 4; matrix products, arithmetic and copies ran while one was open for 2% -> 9% of each run, Pallas kernels for 0% -> 12%
where the time goes in v1:
time: 160 us; the launch traced here: 157 us
  Pallas kernels  54.3 us (34%)
  waiting for transfers between devices  44.6 us (28%)
  starting transfers between devices  39.5 us (25%)
  local copies, waits for them, and re-layouts  11.3 us (7%)
  other arithmetic  4.47 us (3%)
    pallas_call x1, Pallas kernels, attend(): pl.pallas_call(attend_kernel, grid=(count,), in_specs=[pl.BlockSpec((grou...  29.9 us
    all_to_all x1, waiting for transfers between devices, body(): lax.all_to_all(moved, 'col', split_axis=0, concat_axis=0, tiled=True)  28 us
    pallas_call x4, Pallas kernels, pair(): pl.pallas_call(functools.partial(pair_kernel, count), in_specs=[pl.BlockS...  21.9 us
    ppermute x12, starting transfers between devices, xy(): return lax.ppermute(value, 'col', perm)  20.2 us
    all_to_all x1, starting transfers between devices, body(): lax.all_to_all(moved, 'col', split_axis=0, concat_axis=0, tiled=True)  13.5 us
    ppermute x1, waiting for transfers between devices, body(): r0 = lax.ppermute(right, ('row', 'col'), moves)  12.2 us
    unnamed x30, local copies, waits for them, and re-layouts  5.06 us
    ppermute x3, waiting for transfers between devices, row_flip(): return lax.ppermute(value, 'row', [(i, i ^ bit) for i in range(8)])  3.46 us
  transfers between devices with their start and end apart: 18, of which 4 were waited for; matrix products, arithmetic and copies ran while one was open for 9% of the time, Pallas kernels for 12%

profile of v1, /device:TPU:38, one launch (start us, length us, event | category | flops | bytes accessed | tf_op | source)
XLA Modules:
  0.0 156.8 jit_solution(11148484159100301445)
XLA Ops:
  0.6 2.8 %copy.28 = bf16[16,128,256]{2,0,1:T(8,128)(2,1)} copy(bf16[16,128,256]{2,1,0:T(8,128)(2,1)} %param.16) | data formatting | bytes 2097152 | tf_op args[0]
  3.4 0.0 copy-start.8
  3.4 0.0 copy-start.9
  3.4 13.5 %all-to-all-start = ((bf16[32,4,16,256]{3,2,1,0:T(8,128)(2,1)}), bf16[32,4,16,256]{3,2,1,0:T(8,128)(2,1)S(1)}, u32[]{:S(2)}, u32[]{:S(2)}) async-start(bf16[32,4,16,256]{3,2,1,0:T(8,128)(2,1)} %bitcast.1), calls=%async_computation | async-start | bytes 2097152 | tf_op jit(solution)/shard_map/all_to_all | solution.py:184
  16.9 0.0 copy-start
  16.9 0.0 copy-start.1
  17.0 0.0 copy-start.2
  17.0 0.0 copy-start.3
  17.0 0.0 copy-start.4
  17.0 1.1 constant_dynamic-slice_fusion
  18.1 0.1 copy.35
  18.3 0.3 copy.36
  18.6 0.1 pad.4.clone.kbias_ref
  18.8 0.1 pad_maximum_fusion.1.wqkvg_ref
  18.9 28.0 %all-to-all-done.x_ref = bf16[32,4,16,256]{3,2,1,0:T(8,128)(2,1)S(1)} async-done(((bf16[32,4,16,256]{3,2,1,0:T(8,128)(2,1)}), bf16[32,4,16,256]{3,2,1,0:T(8,128)(2,1)S(1)}, u32[]{:S(2)}, u32[]{:S(2)}) %all-to-all-start) | async-done | bytes 1048608 | tf_op jit(solution)/shard_map/all_to_all | solution.py:184
  46.9 29.9 %shard_map.167 = (bf16[4,512,256]{2,1,0:T(8,128)(2,1)S(1)}, bf16[4,32,512]{2,1,0:T(8,128)(2,1)S(1)}, bf16[4,32,512]{2,1,0:T(8,128)(2,1)S(1)}) custom-call(bf16[32,4,16,256]{3,2,1,0:T(8,128)(2,1)S(1)} %all-to-all-done.x_ref, bf16[4,512,128]{2,1,0:T(8,128)(2,1)S(1)} %pad.4.clone.kbias_ref, f32[4,1,512]{2,1,0:T(1,128)S(1)} %reshape.50.mask_ref, ...), custom_call_target="tpu_custom_call" | custom-call | flops 16000000000 | bytes 4000000 | tf_op jit(solution)/shard_map/pallas_call | solution.py:77
  76.9 1.9 %collective-permute-start.9 = (bf16[4,32,512]{2,1,0:T(8,128)(2,1)S(1)}, bf16[4,32,512]{2,1,0:T(8,128)(2,1)S(1)}, u32[]{:S(2)}, u32[]{:S(2)}) collective-permute-start(bf16[4,32,512]{2,1,0:T(8,128)(2,1)S(1)} %get-tuple-element.7), channel_id=1, source_target_pairs={{0,0},{1,64},{2,128},{3,192},{4,32},{5,96},{6,160},{7,224},{8,1},{... | collective-permute-start | bytes 393224 | tf_op jit(solution)/shard_map/ppermute | solution.py:211
  78.8 1.1 collective-permute-start
  79.8 12.2 %collective-permute-done.9 = bf16[4,32,512]{2,1,0:T(8,128)(2,1)S(1)} collective-permute-done((bf16[4,32,512]{2,1,0:T(8,128)(2,1)S(1)}, bf16[4,32,512]{2,1,0:T(8,128)(2,1)S(1)}, u32[]{:S(2)}, u32[]{:S(2)}) %collective-permute-start.9) | collective-permute-done | bytes 131104 | tf_op jit(solution)/shard_map/ppermute | solution.py:211
  92.0 0.8 dynamic_slice.18
  92.8 0.8 dynamic_slice.19
  93.6 0.1 collective-permute-start.5
  93.7 6.9 %collective-permute-start.6 = (bf16[2,2,32,512]{3,2,1,0:T(8,128)(2,1)S(1)}, bf16[2,2,32,512]{3,2,1,0:T(8,128)(2,1)S(1)}, u32[]{:S(2)}, u32[]{:S(2)}) collective-permute-start(bf16[2,2,32,512]{3,2,1,0:T(8,128)(2,1)S(1)} %get-tuple-element.14), channel_id=1, source_target_pairs={{0,16},{1,17},{2,18},{3,19},{4,20},{5,21},{6,22},{7,23},{8,24},{9,... | collective-permute-start | bytes 393224 | tf_op jit(solution)/shard_map/ppermute | solution.py:225
  100.6 0.0 collective-permute-start.7
  100.6 2.8 %collective-permute-start.11 = (bf16[2,4,32,512]{3,2,1,0:T(8,128)(2,1)S(1)}, bf16[2,4,32,512]{3,2,1,0:T(8,128)(2,1)S(1)}, u32[]{:S(2)}, u32[]{:S(2)}) collective-permute-start(bf16[2,4,32,512]{3,2,1,0:T(8,128)(2,1)S(1)} %pad_maximum_fusion.5), channel_id=1, source_target_pairs={{0,128},{32,160},{64,192},{96,224},{128,0},{160,32},{192,64},{224,... | collective-permute-start | bytes 786440 | tf_op jit(solution)/shard_map/ppermute | solution.py:214
  103.5 0.1 compare_convert_fusion
  103.5 0.1 copy.33
  103.6 0.1 collective-permute-start.1
  103.7 3.4 %collective-permute-start.2 = (bf16[2,2,32,512]{3,2,1,0:T(8,128)(2,1)S(1)}, bf16[2,2,32,512]{3,2,1,0:T(8,128)(2,1)S(1)}, u32[]{:S(2)}, u32[]{:S(2)}) collective-permute-start(bf16[2,2,32,512]{3,2,1,0:T(8,128)(2,1)S(1)} %get-tuple-element.15), channel_id=1, source_target_pairs={{0,2},{1,3},{2,0},{3,1},{4,6},{5,7},{6,4},{7,5},{8,10},{9,11},{10,... | collective-permute-start | bytes 393224 | tf_op jit(solution)/shard_map/ppermute | solution.py:225
  107.1 0.0 collective-permute-done.6
  107.1 0.0 collective-permute-start.3
  107.1 0.0 collective-permute-done.7
  107.1 0.1 pad_maximum_fusion.3.refs_1_
  107.2 2.1 %collective-permute-start.16 = (bf16[8,2,32,512]{3,2,1,0:T(8,128)(2,1)S(1)}, bf16[8,2,32,512]{3,2,1,0:T(8,128)(2,1)S(1)}, u32[]{:S(2)}, u32[]{:S(2)}) collective-permute-start(bf16[8,2,32,512]{3,2,1,0:T(8,128)(2,1)S(1)} %pad_maximum_fusion.3.refs_1_), channel_id=1, source_target_pairs={{0,1},{1,2},{2,3},{3,0},{4,5},{5,6},{6,7},{7,4},{8,9},{9,10},{10,1... | collective-permute-start | bytes 1572872 | tf_op jit(solution)/shard_map/ppermute | solution.py:225
  109.3 3.5 %collective-permute-done.11 = bf16[2,4,32,512]{3,2,1,0:T(8,128)(2,1)S(1)} collective-permute-done((bf16[2,4,32,512]{3,2,1,0:T(8,128)(2,1)S(1)}, bf16[2,4,32,512]{3,2,1,0:T(8,128)(2,1)S(1)}, u32[]{:S(2)}, u32[]{:S(2)}) %collective-permute-start.11) | collective-permute-done | bytes 262176 | tf_op jit(solution)/shard_map/ppermute | solution.py:214
  112.7 1.0 fusion.4
  113.8 0.0 collective-permute-start.12
  113.8 0.0 collective-permute-done.1
  113.8 0.0 collective-permute-done.2
  113.8 0.1 pad_maximum_fusion.2.refs_0_
  113.9 2.1 %collective-permute-start.15 = (bf16[8,2,32,512]{3,2,1,0:T(8,128)(2,1)S(1)}, bf16[8,2,32,512]{3,2,1,0:T(8,128)(2,1)}, u32[]{:S(2)}, u32[]{:S(2)}) collective-permute-start(bf16[8,2,32,512]{3,2,1,0:T(8,128)(2,1)S(1)} %pad_maximum_fusion.2.refs_0_), channel_id=1, source_target_pairs={{0,8},{1,9},{2,10},{3,11},{4,12},{5,13},{6,14},{7,15},{8,16},{9,17... | collective-permute-start | bytes 1572872 | tf_op jit(solution)/shard_map/ppermute | solution.py:225
  116.0 2.0 %broadcast_multiply_fusion.refs_5_ = f32[128,32,128]{2,1,0:T(8,128)} fusion(f32[128]{0:T(128)S(1)} %copy-done.12, f32[128,32]{1,0:T(8,128)S(1)} %copy.33), kind=kLoop, calls=%fused_computation.3 | loop fusion | flops 524288 | bytes 2114048 | tf_op jit(solution)/shard_map/mul | solution.py:196
  118.0 2.3 %collective-permute-start.14 = (bf16[8,2,32,512]{3,2,1,0:T(8,128)(2,1)S(1)}, bf16[8,2,32,512]{3,2,1,0:T(8,128)(2,1)S(1)}, u32[]{:S(2)}, u32[]{:S(2)}) collective-permute-start(bf16[8,2,32,512]{3,2,1,0:T(8,128)(2,1)S(1)} %pad_maximum_fusion.3.refs_1_), channel_id=1, source_target_pairs={{0,3},{1,0},{2,1},{3,2},{4,7},{5,4},{6,5},{7,6},{8,11},{9,8},{10,9... | collective-permute-start | bytes 1572872 | tf_op jit(solution)/shard_map/ppermute | solution.py:225
  120.3 1.3 fusion
  121.9 0.1 copy.32
  122.0 1.1 copy.31
  123.1 0.1 stack.288.order_ref
  123.2 0.1 stack.345.place_ref
  123.3 0.1 stack.328.place_ref
  123.4 0.1 stack.311.place_ref
  123.5 0.1 stack.276.place_ref
  123.6 0.0 copy-start.5
  123.6 1.8 %copy.34 = bf16[512,4,256]{2,1,0:T(4,128)(2,1)} copy(bf16[512,4,256]{2,0,1:T(8,128)(2,1)S(1)} %bitcast.105) | data formatting | bytes 2097152
  125.4 0.0 collective-permute-start.8
  125.4 1.1 pad_maximum_fusion
  126.6 2.4 %shard_map.168.refs_2_ = bf16[512,1024]{1,0:T(8,128)(2,1)S(1)} custom-call(s32[8]{0:T(128)S(1)} %stack.288.order_ref, bf16[8,4,32,512]{3,2,1,0:T(8,128)(2,1)S(1)} %bitcast.104), custom_call_target="tpu_custom_call" | custom-call | flops 1000000 | bytes 2000000 | tf_op jit(solution)/shard_map/pallas_call | solution.py:122
  129.0 3.2 %collective-permute-start.4 = (bf16[8,2,32,512]{3,2,1,0:T(8,128)(2,1)S(1)}, bf16[8,2,32,512]{3,2,1,0:T(8,128)(2,1)S(1)}, u32[]{:S(2)}, u32[]{:S(2)}) collective-permute-start(bf16[8,2,32,512]{3,2,1,0:T(8,128)(2,1)S(1)} %pad_maximum_fusion.2.refs_0_), channel_id=1, source_target_pairs={{0,16},{1,17},{2,18},{3,19},{4,20},{5,21},{6,22},{7,23},{8,24},{9,... | collective-permute-start | bytes 1572872 | tf_op jit(solution)/shard_map/ppermute | solution.py:225
  132.2 0.6 broadcast_in_dim.33.refs_4_
  132.8 1.1 broadcast_in_dim.34.refs_6_
  133.9 5.4 %shard_map.169.refs_6_ = bf16[128,32,128]{2,1,0:T(8,128)(2,1)} custom-call(s32[16]{0:T(128)S(1)} %stack.345.place_ref, bf16[8,2,32,512]{3,2,1,0:T(8,128)(2,1)S(1)} %pad_maximum_fusion.2.refs_0_, bf16[8,2,32,512]{3,2,1,0:T(8,128)(2,1)S(1)} %pad_maximum_fusion.3.refs_1_, bf16[512,1024]{1,0:T(8,128)(2,1)S(1)} %shard_map.168.refs_2_, ...), custom_call_target="tpu_custom_call", output_to_operand_aliasing={{}: (7, {})} | custom-call | flops 1920000000 | bytes 1280000 | tf_op jit(solution)/shard_map/pallas_call | solution.py:164
  139.3 5.6 %shard_map.170.refs_6_ = bf16[128,32,128]{2,1,0:T(8,128)(2,1)} custom-call(s32[16]{0:T(128)S(1)} %stack.328.place_ref, bf16[8,2,32,512]{3,2,1,0:T(8,128)(2,1)} %collective-permute-done.15.refs_0_, bf16[8,2,32,512]{3,2,1,0:T(8,128)(2,1)S(1)} %collective-permute-done.16.refs_1_, ...), custom_call_target="tpu_custom_call", output_to_operand_aliasing={{}: (7, {})} | custom-call | flops 1920000000 | bytes 1280000 | tf_op jit(solution)/shard_map/pallas_call | solution.py:164
  144.9 0.9 collective-permute-done.13.refs_0_
  145.8 5.6 %shard_map.171.refs_6_ = bf16[128,32,128]{2,1,0:T(8,128)(2,1)} custom-call(s32[16]{0:T(128)S(1)} %stack.311.place_ref, bf16[8,2,32,512]{3,2,1,0:T(8,128)(2,1)} %collective-permute-done.13.refs_0_, bf16[8,2,32,512]{3,2,1,0:T(8,128)(2,1)S(1)} %collective-permute-done.14.refs_1_, ...), custom_call_target="tpu_custom_call", output_to_operand_aliasing={{}: (7, {})} | custom-call | flops 1920000000 | bytes 1280000 | tf_op jit(solution)/shard_map/pallas_call | solution.py:164
  151.4 5.4 %shard_map.172 = bf16[128,32,128]{2,1,0:T(8,128)(2,1)} custom-call(s32[16]{0:T(128)S(1)} %stack.276.place_ref, bf16[8,2,32,512]{3,2,1,0:T(8,128)(2,1)S(1)} %collective-permute-done.4.refs_0_, bf16[8,2,32,512]{3,2,1,0:T(8,128)(2,1)S(1)} %collective-permute-done.8.refs_1_, bf16[512,1024]{1,0:T(8,128)(2,1)S(1)} %shard_map.168.refs_2_, ...), custom_call_target="tpu_custom_call", output_to_operand_aliasing={{}: (7, {})} | custom-call | flops 1920000000 | bytes 1280000 | tf_op jit(solution)/shard_map/pallas_call | solution.py:164
  (36 shorter events, 0.1 us)
Async XLA Ops:
  3.4 15.3 %copy-start.10 = (bf16[256,32]{0,1:T(8,128)(2,1)S(1)}, bf16[256,32]{0,1:T(8,128)(2,1)}, u32[]{:S(2)}) copy-start(bf16[256,32]{0,1:T(8,128)(2,1)} %param.29) | copy-start | bytes 49156
  3.4 15.3 %copy-start.11 = (bf16[256,32]{0,1:T(8,128)(2,1)S(1)}, bf16[256,32]{0,1:T(8,128)(2,1)}, u32[]{:S(2)}) copy-start(bf16[256,32]{0,1:T(8,128)(2,1)} %param.28) | copy-start | bytes 49156
  3.4 15.4 %copy-start.6 = (bf16[256,256]{1,0:T(8,128)(2,1)S(1)}, bf16[256,256]{1,0:T(8,128)(2,1)}, u32[]{:S(2)}) copy-start(bf16[256,256]{1,0:T(8,128)(2,1)} %param.23) | copy-start | bytes 393220
  3.4 15.4 %copy-start.7 = (bf16[256,256]{1,0:T(8,128)(2,1)S(1)}, bf16[256,256]{1,0:T(8,128)(2,1)}, u32[]{:S(2)}) copy-start(bf16[256,256]{1,0:T(8,128)(2,1)} %param.22) | copy-start | bytes 393220
  3.4 15.4 %copy-start.8 = (bf16[256,256]{1,0:T(8,128)(2,1)S(1)}, bf16[256,256]{1,0:T(8,128)(2,1)}, u32[]{:S(2)}) copy-start(bf16[256,256]{1,0:T(8,128)(2,1)} %param.21) | copy-start | bytes 393220
  3.4 15.4 %copy-start.9 = (bf16[256,256]{1,0:T(8,128)(2,1)S(1)}, bf16[256,256]{1,0:T(8,128)(2,1)}, u32[]{:S(2)}) copy-start(bf16[256,256]{1,0:T(8,128)(2,1)} %param.20) | copy-start | bytes 393220
  3.4 43.5 %all-to-all-start = ((bf16[32,4,16,256]{3,2,1,0:T(8,128)(2,1)}), bf16[32,4,16,256]{3,2,1,0:T(8,128)(2,1)S(1)}, u32[]{:S(2)}, u32[]{:S(2)}) async-start(bf16[32,4,16,256]{3,2,1,0:T(8,128)(2,1)} %bitcast.1), calls=%async_computation | async-start | bytes 2097152 | tf_op jit(solution)/shard_map/all_to_all | solution.py:184
  16.9 30.0 %copy-start = (bf16[256,256]{1,0:T(8,128)(2,1)S(1)}, bf16[256,256]{1,0:T(8,128)(2,1)}, u32[]{:S(2)}) copy-start(bf16[256,256]{1,0:T(8,128)(2,1)} %wo_ref.1) | copy-start | bytes 393220
  16.9 30.0 %copy-start.1 = (f32[256]{0:T(256)S(1)}, f32[256]{0:T(256)}, u32[]{:S(2)}) copy-start(f32[256]{0:T(256)} %param.19) | copy-start | bytes 3076
  17.0 30.0 %copy-start.2 = (f32[256]{0:T(256)S(1)}, f32[256]{0:T(256)}, u32[]{:S(2)}) copy-start(f32[256]{0:T(256)} %param.24) | copy-start | bytes 3076
  17.0 30.0 %copy-start.3 = (f32[256]{0:T(256)S(1)}, f32[256]{0:T(256)}, u32[]{:S(2)}) copy-start(f32[256]{0:T(256)} %param.26) | copy-start | bytes 3076
  17.0 30.0 %copy-start.4 = (f32[256]{0:T(256)S(1)}, f32[256]{0:T(256)}, u32[]{:S(2)}) copy-start(f32[256]{0:T(256)} %param.27) | copy-start | bytes 3076
  76.9 15.2 %collective-permute-start.9 = (bf16[4,32,512]{2,1,0:T(8,128)(2,1)S(1)}, bf16[4,32,512]{2,1,0:T(8,128)(2,1)S(1)}, u32[]{:S(2)}, u32[]{:S(2)}) collective-permute-start(bf16[4,32,512]{2,1,0:T(8,128)(2,1)S(1)} %get-tuple-element.7), channel_id=1, source_target_pairs={{0,0},{1,64},{2,128},{3,192},{4,32},{5,96},{6,160},{7,224},{8,1},{... | collective-permute-start | bytes 393224 | tf_op jit(solution)/shard_map/ppermute | solution.py:211
  78.8 14.8 %collective-permute-start = (bf16[4,32,512]{2,1,0:T(8,128)(2,1)S(1)}, bf16[4,32,512]{2,1,0:T(8,128)(2,1)S(1)}, u32[]{:S(2)}, u32[]{:S(2)}) collective-permute-start(bf16[4,32,512]{2,1,0:T(8,128)(2,1)S(1)} %get-tuple-element.6), channel_id=1, source_target_pairs={{0,4},{1,5},{2,6},{3,7},{4,0},{5,1},{6,2},{7,3},{8,12},{9,13},{10,... | collective-permute-start | bytes 393224 | tf_op jit(solution)/shard_map/ppermute | solution.py:227
  92.0 8.5 %collective-permute-start.10 = (bf16[4,32,512]{2,1,0:T(8,128)(2,1)S(1)}, bf16[4,32,512]{2,1,0:T(8,128)(2,1)S(1)}, u32[]{:S(2)}, u32[]{:S(2)}) collective-permute-start(bf16[4,32,512]{2,1,0:T(8,128)(2,1)S(1)} %collective-permute-done.9), channel_id=1, source_target_pairs={{0,64},{32,96},{64,0},{96,32},{128,192},{160,224},{192,128},{224,1... | collective-permute-start | bytes 393224 | tf_op jit(solution)/shard_map/ppermute | solution.py:214
  93.6 10.1 %collective-permute-start.5 = (bf16[2,2,32,512]{3,2,1,0:T(8,128)(2,1)S(1)}, bf16[2,2,32,512]{3,2,1,0:T(8,128)(2,1)S(1)}, u32[]{:S(2)}, u32[]{:S(2)}) collective-permute-start(bf16[2,2,32,512]{3,2,1,0:T(8,128)(2,1)S(1)} %get-tuple-element.14), channel_id=1, source_target_pairs={{0,8},{1,9},{2,10},{3,11},{4,12},{5,13},{6,14},{7,15},{8,16},{9,17... | collective-permute-start | bytes 393224 | tf_op jit(solution)/shard_map/ppermute | solution.py:225
  93.7 13.4 %collective-permute-start.6 = (bf16[2,2,32,512]{3,2,1,0:T(8,128)(2,1)S(1)}, bf16[2,2,32,512]{3,2,1,0:T(8,128)(2,1)S(1)}, u32[]{:S(2)}, u32[]{:S(2)}) collective-permute-start(bf16[2,2,32,512]{3,2,1,0:T(8,128)(2,1)S(1)} %get-tuple-element.14), channel_id=1, source_target_pairs={{0,16},{1,17},{2,18},{3,19},{4,20},{5,21},{6,22},{7,23},{8,24},{9,... | collective-permute-start | bytes 393224 | tf_op jit(solution)/shard_map/ppermute | solution.py:225
  100.6 6.5 %collective-permute-start.7 = (bf16[2,2,32,512]{3,2,1,0:T(8,128)(2,1)S(1)}, bf16[2,2,32,512]{3,2,1,0:T(8,128)(2,1)S(1)}, u32[]{:S(2)}, u32[]{:S(2)}) collective-permute-start(bf16[2,2,32,512]{3,2,1,0:T(8,128)(2,1)S(1)} %get-tuple-element.14), channel_id=1, source_target_pairs={{0,24},{1,25},{2,26},{3,27},{4,28},{5,29},{6,30},{7,31},{8,0},{9,1... | collective-permute-start | bytes 393224 | tf_op jit(solution)/shard_map/ppermute | solution.py:225
  100.6 15.4 %copy-start.12 = (f32[128]{0:T(128)S(1)}, f32[128]{0:T(128)}, u32[]{:S(2)}) copy-start(f32[128]{0:T(128)} %param.31) | copy-start | bytes 1540
  100.6 12.1 %collective-permute-start.11 = (bf16[2,4,32,512]{3,2,1,0:T(8,128)(2,1)S(1)}, bf16[2,4,32,512]{3,2,1,0:T(8,128)(2,1)S(1)}, u32[]{:S(2)}, u32[]{:S(2)}) collective-permute-start(bf16[2,4,32,512]{3,2,1,0:T(8,128)(2,1)S(1)} %pad_maximum_fusion.5), channel_id=1, source_target_pairs={{0,128},{32,160},{64,192},{96,224},{128,0},{160,32},{192,64},{224,... | collective-permute-start | bytes 786440 | tf_op jit(solution)/shard_map/ppermute | solution.py:214
  103.6 10.1 %collective-permute-start.1 = (bf16[2,2,32,512]{3,2,1,0:T(8,128)(2,1)S(1)}, bf16[2,2,32,512]{3,2,1,0:T(8,128)(2,1)S(1)}, u32[]{:S(2)}, u32[]{:S(2)}) collective-permute-start(bf16[2,2,32,512]{3,2,1,0:T(8,128)(2,1)S(1)} %get-tuple-element.15), channel_id=1, source_target_pairs={{0,1},{1,2},{2,3},{3,0},{4,5},{5,6},{6,7},{7,4},{8,9},{9,10},{10,1... | collective-permute-start | bytes 393224 | tf_op jit(solution)/shard_map/ppermute | solution.py:225
  103.7 10.0 %collective-permute-start.2 = (bf16[2,2,32,512]{3,2,1,0:T(8,128)(2,1)S(1)}, bf16[2,2,32,512]{3,2,1,0:T(8,128)(2,1)S(1)}, u32[]{:S(2)}, u32[]{:S(2)}) collective-permute-start(bf16[2,2,32,512]{3,2,1,0:T(8,128)(2,1)S(1)} %get-tuple-element.15), channel_id=1, source_target_pairs={{0,2},{1,3},{2,0},{3,1},{4,6},{5,7},{6,4},{7,5},{8,10},{9,11},{10,... | collective-permute-start | bytes 393224 | tf_op jit(solution)/shard_map/ppermute | solution.py:225
  107.1 6.7 %collective-permute-start.3 = (bf16[2,2,32,512]{3,2,1,0:T(8,128)(2,1)S(1)}, bf16[2,2,32,512]{3,2,1,0:T(8,128)(2,1)S(1)}, u32[]{:S(2)}, u32[]{:S(2)}) collective-permute-start(bf16[2,2,32,512]{3,2,1,0:T(8,128)(2,1)S(1)} %get-tuple-element.15), channel_id=1, source_target_pairs={{0,3},{1,0},{2,1},{3,2},{4,7},{5,4},{6,5},{7,6},{8,11},{9,8},{10,9... | collective-permute-start | bytes 393224 | tf_op jit(solution)/shard_map/ppermute | solution.py:225
  107.2 21.8 %collective-permute-start.16 = (bf16[8,2,32,512]{3,2,1,0:T(8,128)(2,1)S(1)}, bf16[8,2,32,512]{3,2,1,0:T(8,128)(2,1)S(1)}, u32[]{:S(2)}, u32[]{:S(2)}) collective-permute-start(bf16[8,2,32,512]{3,2,1,0:T(8,128)(2,1)S(1)} %pad_maximum_fusion.3.refs_1_), channel_id=1, source_target_pairs={{0,1},{1,2},{2,3},{3,0},{4,5},{5,6},{6,7},{7,4},{8,9},{9,10},{10,1... | collective-permute-start | bytes 1572872 | tf_op jit(solution)/shard_map/ppermute | solution.py:225
  113.8 11.6 %collective-permute-start.12 = (bf16[4,4,32,512]{3,2,1,0:T(8,128)(2,1)}, bf16[4,4,32,512]{3,2,1,0:T(8,128)(2,1)}, u32[]{:S(2)}, u32[]{:S(2)}) collective-permute-start(bf16[4,4,32,512]{3,2,1,0:T(8,128)(2,1)} %get-tuple-element.13), channel_id=1, source_target_pairs={{0,32},{32,0},{64,96},{96,64},{128,160},{160,128},{192,224},{224,1... | collective-permute-start | bytes 1572872 | tf_op jit(solution)/shard_map/ppermute | solution.py:214
  113.9 25.4 %collective-permute-start.15 = (bf16[8,2,32,512]{3,2,1,0:T(8,128)(2,1)S(1)}, bf16[8,2,32,512]{3,2,1,0:T(8,128)(2,1)}, u32[]{:S(2)}, u32[]{:S(2)}) collective-permute-start(bf16[8,2,32,512]{3,2,1,0:T(8,128)(2,1)S(1)} %pad_maximum_fusion.2.refs_0_), channel_id=1, source_target_pairs={{0,8},{1,9},{2,10},{3,11},{4,12},{5,13},{6,14},{7,15},{8,16},{9,17... | collective-permute-start | bytes 1572872 | tf_op jit(solution)/shard_map/ppermute | solution.py:225
  118.0 26.9 %collective-permute-start.14 = (bf16[8,2,32,512]{3,2,1,0:T(8,128)(2,1)S(1)}, bf16[8,2,32,512]{3,2,1,0:T(8,128)(2,1)S(1)}, u32[]{:S(2)}, u32[]{:S(2)}) collective-permute-start(bf16[8,2,32,512]{3,2,1,0:T(8,128)(2,1)S(1)} %pad_maximum_fusion.3.refs_1_), channel_id=1, source_target_pairs={{0,3},{1,0},{2,1},{3,2},{4,7},{5,4},{6,5},{7,6},{8,11},{9,8},{10,9... | collective-permute-start | bytes 1572872 | tf_op jit(solution)/shard_map/ppermute | solution.py:225
  120.3 25.5 %collective-permute-start.13 = (bf16[8,2,32,512]{3,2,1,0:T(8,128)(2,1)S(1)}, bf16[8,2,32,512]{3,2,1,0:T(8,128)(2,1)}, u32[]{:S(2)}, u32[]{:S(2)}) collective-permute-start(bf16[8,2,32,512]{3,2,1,0:T(8,128)(2,1)S(1)} %pad_maximum_fusion.2.refs_0_), channel_id=1, source_target_pairs={{0,24},{1,25},{2,26},{3,27},{4,28},{5,29},{6,30},{7,31},{8,0},{9,1... | collective-permute-start | bytes 1572872 | tf_op jit(solution)/shard_map/ppermute | solution.py:225
  123.6 1.8 %copy-start.5 = (bf16[1,4,4,32,512]{4,3,2,1,0:T(8,128)(2,1)S(1)}, bf16[1,4,4,32,512]{4,3,2,1,0:T(8,128)(2,1)}, u32[]{:S(2)}) copy-start(bf16[1,4,4,32,512]{4,3,2,1,0:T(8,128)(2,1)} %get-tuple-element.12) | copy-start | bytes 1572868
  125.4 26.0 %collective-permute-start.8 = (bf16[8,2,32,512]{3,2,1,0:T(8,128)(2,1)S(1)}, bf16[8,2,32,512]{3,2,1,0:T(8,128)(2,1)S(1)}, u32[]{:S(2)}, u32[]{:S(2)}) collective-permute-start(bf16[8,2,32,512]{3,2,1,0:T(8,128)(2,1)S(1)} %pad_maximum_fusion.3.refs_1_), channel_id=1, source_target_pairs={{0,2},{1,3},{2,0},{3,1},{4,6},{5,7},{6,4},{7,5},{8,10},{9,11},{10,... | collective-permute-start | bytes 1572872 | tf_op jit(solution)/shard_map/ppermute | solution.py:225
  129.0 22.4 %collective-permute-start.4 = (bf16[8,2,32,512]{3,2,1,0:T(8,128)(2,1)S(1)}, bf16[8,2,32,512]{3,2,1,0:T(8,128)(2,1)S(1)}, u32[]{:S(2)}, u32[]{:S(2)}) collective-permute-start(bf16[8,2,32,512]{3,2,1,0:T(8,128)(2,1)S(1)} %pad_maximum_fusion.2.refs_0_), channel_id=1, source_target_pairs={{0,16},{1,17},{2,18},{3,19},{4,20},{5,21},{6,22},{7,23},{8,24},{9,... | collective-permute-start | bytes 1572872 | tf_op jit(solution)/shard_map/ppermute | solution.py:225

commit v2 on v1

v2 whole, which is shorter than its diff:
```python
import functools
import math

import jax
import jax.numpy as jnp
import numpy as np
from jax import lax
from jax.experimental import pallas as pl
from jax.experimental.pallas import tpu as pltpu
from jax.sharding import PartitionSpec as P

HEAD_FEATURES = 32
F32, BF16 = jnp.float32, jnp.bfloat16
SB = 256
VMEM_LIMIT = 40 * 1024 * 1024

def norm_rows(x, gain):
    average = jnp.mean(x, -1, keepdims=True)
    centred = x - average
    variance = jnp.mean(centred * centred, -1, keepdims=True)
    return centred * lax.rsqrt(variance + 1e-05) * gain

def dot(a, b):
    return jnp.dot(a, b, preferred_element_type=F32)

def dot_nt(a, b):
    return lax.dot_general(a, b, (((1,), (1,)), ((), ())), preferred_element_type=F32)

def attend_kernel(
    parts_ref, mask_ref, gain1_ref, wqkvg_ref, gbias_ref, wo_ref, obias_ref, gain2_ref, wlr_ref,
    up_ref, left_ref, right_ref, qa_ref, ka_ref, va_ref, gated_ref,
):
    rows = qa_ref.shape[1]
    lane = lax.broadcasted_iota(jnp.int32, (1, 128), 1)

    @pl.when(pl.program_id(0) == 0)
    def _():
        ka_ref[...] = jnp.zeros_like(ka_ref)
        va_ref[...] = jnp.zeros_like(va_ref)
        ones = jnp.broadcast_to(jnp.where(lane == 0, 1.0, 0.0).astype(BF16), (rows, 128))
        for g in range(2):
            qa_ref[g, :, 128:] = ones
            for h in range(4):
                va_ref[g, h * rows:(h + 1) * rows, 128:] = jnp.broadcast_to(
                    jnp.where(lane // 32 == h, 1.0, 0.0).astype(BF16), (rows, 128))

    x = parts_ref[...].reshape(rows, 256).astype(F32)
    normed = norm_rows(x, gain1_ref[...]).astype(BF16)
    scale = math.log2(math.e) * HEAD_FEATURES ** (-0.5)
    queries = (dot(normed, wqkvg_ref[:, 0:256]) * scale).astype(BF16)
    keys = dot(normed, wqkvg_ref[:, 256:512]).astype(BF16).T
    values = dot(normed, wqkvg_ref[:, 512:768]).astype(BF16)
    live = mask_ref[...].reshape(1, rows)
    dead = jnp.where(lax.broadcasted_iota(jnp.int32, (16, 1), 0) == 0, (live - 1.0) * 1e9, 0.0).astype(BF16)
    for g in range(2):
        qa_ref[g, :, :128] = queries[:, g * 128:(g + 1) * 128]
        for h in range(4):
            n = g * 4 + h
            ka_ref[n, h * 32:(h + 1) * 32, :] = keys[n * 32:(n + 1) * 32, :]
            ka_ref[n, 128:144, :] = dead
            kept = jnp.where(lane // 32 == h, 1.0, 0.0).astype(BF16)
            va_ref[g, h * rows:(h + 1) * rows, :128] = values[:, g * 128:(g + 1) * 128] * kept
    gated_ref[...] = jax.nn.sigmoid(dot(normed, wqkvg_ref[:, 768:1024]) + gbias_ref[...])
    for g in range(2):
        for b in range(rows // SB):
            q = qa_ref[g, b * SB:(b + 1) * SB, :]
            total = None
            for h in range(4):
                s = dot(q, ka_ref[g * 4 + h])
                m = jnp.max(s, axis=-1, keepdims=True)
                p = jnp.exp2(s - m).astype(BF16)
                part = dot(p, va_ref[g, h * rows:(h + 1) * rows, :])
                total = part if total is None else total + part
            out = total[:, :128] / total[:, 128:]
            sl = (slice(b * SB, (b + 1) * SB), slice(g * 128, (g + 1) * 128))
            gated_ref[sl] = gated_ref[sl] * out
    gated = gated_ref[...].astype(BF16)
    updated = (dot(gated, wo_ref[...]) + obias_ref[...] + x).astype(BF16)
    up_ref[...] = updated.reshape(up_ref.shape)
    again = norm_rows(updated.astype(F32), gain2_ref[...]).astype(BF16)
    factors = dot_nt(wlr_ref[...], again) * live
    left_ref[...] = factors[:32].astype(BF16).reshape(left_ref.shape)
    right_ref[...] = factors[32:].astype(BF16).reshape(right_ref.shape)

def attend(x, mask, gain1, wqkvg, gbias, wo, obias, gain2, wlr_t, first=0, count=4):
    groups, _, per, width = x.shape
    rows = groups * per
    whole = lambda a: pl.BlockSpec(a.shape, lambda k: (0,) * a.ndim)
    return pl.pallas_call(
        attend_kernel,
        grid=(count,),
        in_specs=[
            pl.BlockSpec((groups, 1, per, width), lambda k: (0, k + first, 0, 0)),
            pl.BlockSpec((1, 1, rows), lambda k: (k + first, 0, 0)),
            whole(gain1), whole(wqkvg), whole(gbias), whole(wo), whole(obias), whole(gain2), whole(wlr_t),
        ],
        out_specs=[
            pl.BlockSpec((1, rows, width), lambda k: (k, 0, 0)),
            pl.BlockSpec((1, 32, rows), lambda k: (k, 0, 0)),
            pl.BlockSpec((1, 32, rows), lambda k: (k, 0, 0)),
        ],
        out_shape=[
            jax.ShapeDtypeStruct((count, rows, width), BF16),
            jax.ShapeDtypeStruct((count, 32, rows), BF16),
            jax.ShapeDtypeStruct((count, 32, rows), BF16),
        ],
        scratch_shapes=[
            pltpu.VMEM((2, rows, 256), BF16),
            pltpu.VMEM((8, 256, rows), BF16),
            pltpu.VMEM((2, 4 * rows, 256), BF16),
            pltpu.VMEM((rows, 256), F32),
        ],
        compiler_params=pltpu.CompilerParams(vmem_limit_bytes=VMEM_LIMIT),
        cost_estimate=pl.CostEstimate(
            flops=count * 4 * 10**9, bytes_accessed=count * 10**6, transcendentals=count * 2 * 10**6
        ),
    )(x, mask, gain1, wqkvg, gbias, wo, obias, gain2, wlr_t)


def rearrange_kernel(order_ref, a_ref, b_ref, c_ref, out_ref, f_ref):
    pieces = [a_ref.at[0], a_ref.at[1], b_ref.at[0], b_ref.at[1]]
    pieces += [c_ref.at[n] for n in range(4)]
    for n in range(8):
        first = pl.multiple_of(order_ref[n] * 128, 128)
        r = pieces[n][...].reshape(128, 512).astype(F32)
        for c in range(4):
            f_ref[c, pl.ds(first, 128), :] = r[:, c * 128:(c + 1) * 128]
    for b in range(8):
        for c in range(4):
            part = jnp.concatenate(
                [f_ref[c, pl.ds(b * 4 + a, 32, stride=32), :] for a in range(4)], axis=0
            )
            out_ref[c * 128:(c + 1) * 128, b * 128:(b + 1) * 128] = part.T.astype(BF16)


def rearrange(order, a, b, c):
    return pl.pallas_call(
        rearrange_kernel,
        in_specs=[pl.BlockSpec(memory_space=pltpu.SMEM)] + [pl.BlockSpec(memory_space=pltpu.VMEM)] * 3,
        out_shape=jax.ShapeDtypeStruct((512, 1024), BF16),
        scratch_shapes=[pltpu.VMEM((4, 1024, 128), F32)],
        compiler_params=pltpu.CompilerParams(vmem_limit_bytes=VMEM_LIMIT),
        cost_estimate=pl.CostEstimate(flops=10**6, bytes_accessed=4 * 10**6, transcendentals=0),
    )(order, a, b, c)


def pair_kernel(first, count, has_old, place_ref, *refs):
    parts = refs[:count]
    r_ref, w_ref, inv_ref, same_ref, bias_ref = refs[count:count + 5]
    out_ref, x_ref, y_ref, sems = refs[count + 5 + has_old:]
    copies = []
    at = 0
    for part in parts:
        for half in range(part.shape[0] // 4):
            outer = dot(part[half * 4:half * 4 + 4].reshape(512, 512), r_ref[...]).astype(BF16)
            for n in range(16):
                a = jnp.concatenate(
                    [outer[n * 32:(n + 1) * 32, b * 128:(b + 1) * 128] for b in range(8)], axis=0
                )
                t = a.T
                for q in range(4):
                    x_ref[n * 32:(n + 1) * 32, q * 256:(q + 1) * 256] = t[q * 32:(q + 1) * 32, :]
            y = dot(x_ref[...], w_ref[...])
            for n in range(16):
                lane = (first + at) * 4 + n
                scale = jnp.broadcast_to(inv_ref[:, lane:lane + 1], (32, 128))
                same = jnp.broadcast_to(same_ref[:, lane:lane + 1], (32, 128))
                result = y[n * 32:(n + 1) * 32] * scale + same * bias_ref[...]
                y_ref[at + n // 4, n % 4] = result.astype(BF16)
            for s in range(at, at + 4):
                copy = pltpu.make_async_copy(y_ref.at[s], out_ref.at[place_ref[first + s]], sems.at[s])
                copy.start()
                copies.append(copy)
            at += 4
    for copy in copies:
        copy.wait()


def pair(first, place, parts, r, w, inv, same, bias, old=None):
    count = len(parts)
    sources = sum(part.shape[0] for part in parts)
    vmem = pl.BlockSpec(memory_space=pltpu.VMEM)
    anywhere = pl.BlockSpec(memory_space=pl.ANY)
    has_old = old is not None
    return pl.pallas_call(
        functools.partial(pair_kernel, first, count, has_old),
        in_specs=[pl.BlockSpec(memory_space=pltpu.SMEM)] + [vmem] * (count + 5) + [anywhere] * has_old,
        out_specs=anywhere,
        out_shape=jax.ShapeDtypeStruct((32, 4, 32, 128), BF16),
        scratch_shapes=[
            pltpu.VMEM((512, 1024), BF16),
            pltpu.VMEM((sources, 4, 32, 128), BF16),
            pltpu.SemaphoreType.DMA((sources,)),
        ],
        input_output_aliases={count + 6: 0} if has_old else {},
        compiler_params=pltpu.CompilerParams(vmem_limit_bytes=VMEM_LIMIT),
        cost_estimate=pl.CostEstimate(
            flops=sources * 25 * 10**7, bytes_accessed=sources * 4 * 10**5, transcendentals=0
        ),
    )(place, *parts, r, w, inv, same, bias, *([old] if has_old else []))


def coordinates(device):
    return [int(n) for n in np.unravel_index(device, (4, 2, 4, 2, 4))]


def permute_all(value, move):
    pairs = []
    for source in range(256):
        pairs.append((source, int(np.ravel_multi_index(move(*coordinates(source)), (4, 2, 4, 2, 4)))))
    return lax.ppermute(value, ("row", "col"), pairs)


def shifted(phase, shift):
    def move(zl, co, x, zh, y):
        if (co + phase) % 2 == 0:
            return zl, co, x, zh, (y + shift) % 4
        return zl, co, (x + shift) % 4, zh, y

    return move


SHIFTS = (0, 1, 3, 2)


def after(value, *others):
    anywhere = pl.BlockSpec(memory_space=pl.ANY)

    def nothing(*refs):
        pass

    return pl.pallas_call(
        nothing,
        in_specs=[anywhere] * (1 + len(others)),
        out_specs=anywhere,
        out_shape=jax.ShapeDtypeStruct(value.shape, value.dtype),
        input_output_aliases={0: 0},
        cost_estimate=pl.CostEstimate(flops=0, bytes_accessed=0, transcendentals=0),
    )(value, *others)


def body(
    alignment, column_mask, chain_index, attention_norm_gain, query_weight, key_weight, value_matrix,
    gate_matrix, gate_bias, attention_output_weight, attention_output_bias, outer_norm_gain,
    left_factor_weight, right_factor_weight, pair_weight, chain_bias,
):
    row = lax.axis_index("row")
    col = lax.axis_index("col")
    z_lo, core = row // 2, row % 2
    x, z_hi, y = col // 8, (col // 4) % 2, col % 4
    moved = alignment.reshape(16, 32, 4, 256).transpose(1, 2, 0, 3)
    regrouped = lax.all_to_all(moved, "col", split_axis=0, concat_axis=0, tiled=True)

    place = []
    for s in SHIFTS:
        for t in SHIFTS:
            for z in range(2):
                by_y = ((x - s) % 4) * 8 + (z_hi ^ z) * 4 + (y - t) % 4
                by_x = ((x - t) % 4) * 8 + (z_hi ^ z) * 4 + (y - s) % 4
                place.append(jnp.where(core == 0, by_y, by_x))
    place = jnp.stack(place).astype(jnp.int32)
    order = jnp.stack(
        [(core ^ c) * 4 + (z_lo ^ n) for c in range(2) for n in (0, 2, 1, 3)]
    ).astype(jnp.int32)

    own_mask = lax.dynamic_slice_in_dim(column_mask, row * 128 + col * 4, 4, 1).T
    live = own_mask.astype(F32).reshape(4, 1, 512)
    row_mask = lax.dynamic_slice_in_dim(column_mask, row * 128, 128, 1).astype(BF16)
    col_mask = lax.dynamic_slice_in_dim(column_mask, col * 32, 32, 1).astype(BF16)
    counts = lax.dot_general(col_mask, row_mask, (((0,), (0,)), ((), ())), preferred_element_type=F32)
    row_chain = lax.dynamic_slice_in_dim(chain_index, row * 128, 128, 0)
    col_chain = lax.dynamic_slice_in_dim(chain_index, col * 32, 32, 0)
    same = (col_chain[:, None] == row_chain[None, :]).astype(F32)
    residue = (place[:, None] * 4 + jnp.arange(4)[None, :]).reshape(128)
    chosen = (jnp.arange(128)[:, None] == residue[None, :]).astype(F32)
    arrived = jnp.dot(jnp.concatenate([1.0 / (counts + 0.001), same]), chosen, precision=lax.Precision.HIGHEST)
    inverse, same = arrived[:32], arrived[32:]
    wqkvg = jnp.concatenate([query_weight, key_weight, value_matrix, gate_matrix], axis=1)
    wlr = jnp.concatenate([left_factor_weight, right_factor_weight], axis=1).T
    wpair = pair_weight.reshape(32, 8, 4, 128).transpose(2, 1, 0, 3).reshape(1024, 128)
    prepared = (live, wqkvg, wlr, wpair, inverse, same, place, order)
    regrouped, prepared = lax.optimization_barrier((regrouped, prepared))
    live, wqkvg, wlr, wpair, inverse, same, place, order = prepared

    up, left, right = attend(
        regrouped, live, attention_norm_gain[None], wqkvg, gate_bias[None],
        attention_output_weight, attention_output_bias[None], outer_norm_gain[None], wlr,
    )
    updated = up.transpose(1, 0, 2)

    beside = permute_all(left, lambda zl, co, x, zh, y: (zl, co, x, 1 - zh, y))
    near = permute_all(right, lambda zl, co, x, zh, y: (y, zh, zl, co, x))
    far = permute_all(after(right, beside), lambda zl, co, x, zh, y: (y ^ 2, zh, zl, co, x))
    own = jnp.stack([left, beside])
    line = jnp.concatenate([own] + [permute_all(own, shifted(0, s)) for s in SHIFTS[1:]])
    right_a = jnp.stack([near, far])
    right_b = permute_all(right_a, lambda zl, co, x, zh, y: (zl ^ 1, co, x, zh, y))
    below, above = permute_all(line, shifted(1, 1)), permute_all(line, shifted(1, 3))
    parts = [line, below, above, permute_all(below[:4], shifted(1, 1)), permute_all(above[4:], shifted(1, 3))]
    right_c = permute_all(
        jnp.concatenate([right_a, right_b]), lambda zl, co, x, zh, y: (zl, 1 - co, x, zh, y)
    )
    r = rearrange(order, right_a, right_b, right_c)
    out = None
    for first, some in ((0, parts[:1]), (8, parts[1:3]), (24, parts[3:])):
        out = pair(first, place, some, r, wpair, inverse, same, chain_bias[None], out)
    return updated, out.reshape(128, 32, 128)


def solution(mesh):
    return jax.shard_map(
        body,
        mesh=mesh,
        in_specs=(P("col", "row", None),) + (P(),) * 15,
        out_specs=(P(None, ("row", "col"), None), P("row", "col", None)),
        check_vma=False,
    )
```

time: 160 us -> 126 us (0.79)
  the two profiles are of different devices: /device:TPU:38 before, /device:TPU:32 now
where the time goes in v2:
time: 126 us; the launch traced here: 125 us
  waiting for transfers between devices  46.8 us (37%)
  Pallas kernels  32.9 us (26%)
  starting transfers between devices  30.1 us (24%)
  local copies, waits for them, and re-layouts  11.2 us (9%)
  matrix products  1.51 us (1%)
  between operations  1.47 us (1%)
  other arithmetic  1.39 us (1%)
    all_to_all x1, waiting for transfers between devices, body(): lax.all_to_all(moved, 'col', split_axis=0, concat_axis=0, tiled=True)  26.1 us
    ppermute x12, waiting for transfers between devices, permute_all(): return lax.ppermute(value, ('row', 'col'), pairs)  20.7 us
    ppermute x12, starting transfers between devices, permute_all(): return lax.ppermute(value, ('row', 'col'), pairs)  17 us
    pallas_call x1, Pallas kernels, attend(): pl.pallas_call(attend_kernel, grid=(count,), in_specs=[pl.BlockSpec((grou...  16 us
    pallas_call x3, Pallas kernels, pair(): pl.pallas_call(functools.partial(pair_kernel, first, count, has_old), in_...  14.5 us
    all_to_all x1, starting transfers between devices, body(): lax.all_to_all(moved, 'col', split_axis=0, concat_axis=0, tiled=True)  13.2 us
    unnamed x37, local copies, waits for them, and re-layouts  8.44 us
  transfers between devices with their start and end apart: 13, of which 7 were waited for; matrix products, arithmetic and copies ran while one was open for 9% of the time, Pallas kernels for 10%

profile of v2, /device:TPU:32, one launch (start us, length us, event | category | flops | bytes accessed | tf_op | source)
XLA Modules:
  0.0 125.4 jit_solution(11605316616630499303)
XLA Ops:
  0.6 2.8 %copy.25 = bf16[16,128,256]{2,0,1:T(8,128)(2,1)} copy(bf16[16,128,256]{2,1,0:T(8,128)(2,1)} %param.16) | data formatting | bytes 2097152 | tf_op args[0]
  3.4 0.0 copy-start.10
  3.4 0.0 copy-start.11
  3.4 0.0 copy-start.12
  3.5 13.2 %all-to-all-start = ((bf16[32,4,16,256]{3,2,1,0:T(8,128)(2,1)}), bf16[32,4,16,256]{3,2,1,0:T(8,128)(2,1)S(1)}, u32[]{:S(2)}, u32[]{:S(2)}) async-start(bf16[32,4,16,256]{3,2,1,0:T(8,128)(2,1)} %bitcast.1), calls=%async_computation | async-start | bytes 2097152 | tf_op jit(solution)/shard_map/all_to_all | solution.py:252
  16.7 0.0 copy-start.1
  16.7 0.0 copy-start.2
  16.7 0.0 copy-start.3
  16.7 0.0 copy-start.4
  16.7 0.0 copy-start.5
  17.0 0.1 stack.176.place_ref
  17.2 0.1 iota_add_fusion
  17.2 0.1 add.495
  17.3 0.8 dynamic_slice.19
  18.1 0.8 dynamic_slice.18
  18.9 1.1 dynamic-slice_convert_fusion.2
  20.0 0.1 copy.30
  20.1 0.0 copy-done.8
  20.1 0.1 copy.27
  20.2 0.1 stack.185.order_ref
  20.3 1.3 %fusion = f32[32,128]{1,0:T(8,128)S(1)} fusion(s32[512,1024]{1,0:T(8,128)} %param.17, s32[]{:T(128)S(6)} %select_n.389, s32[]{:T(128)S(6)} %select_n.390), kind=kOutput, calls=%fused_computation.1 | convolution fusion | flops 4284416 | bytes 540680 | tf_op jit(solution)/shard_map/dot_general | solution.py:270
  21.6 0.0 copy-done.13
  21.6 0.0 copy-done.14
  21.7 0.1 pad_maximum_fusion.wqkvg_ref
  21.8 0.1 compare_convert_fusion
  21.8 0.2 fusion.1
  22.0 26.1 %all-to-all-done.parts_ref = bf16[32,4,16,256]{3,2,1,0:T(8,128)(2,1)S(1)} async-done(((bf16[32,4,16,256]{3,2,1,0:T(8,128)(2,1)}), bf16[32,4,16,256]{3,2,1,0:T(8,128)(2,1)S(1)}, u32[]{:S(2)}, u32[]{:S(2)}) %all-to-all-start) | async-done | bytes 1048608 | tf_op jit(solution)/shard_map/all_to_all | solution.py:252
  48.2 16.0 %shard_map.167 = (bf16[4,512,256]{2,1,0:T(8,128)(2,1)S(1)}, bf16[4,32,512]{2,1,0:T(8,128)(2,1)S(1)}, bf16[4,32,512]{2,1,0:T(8,128)(2,1)S(1)}) custom-call(bf16[32,4,16,256]{3,2,1,0:T(8,128)(2,1)S(1)} %all-to-all-done.parts_ref, f32[4,1,512]{2,1,0:T(1,128)S(1)} %reshape.294.mask_ref, f32[1,256]{1,0:T(1,128)S(1)} %bitcast.68, ...), custom_call_target="tpu_custom_call" | custom-call | flops 16000000000 | bytes 4000000 | tf_op jit(solution)/shard_map/pallas_call | solution.py:89
  64.1 0.0 copy-start
  64.1 1.1 collective-permute-start
  65.2 1.9 %collective-permute-start.8 = (bf16[4,32,512]{2,1,0:T(8,128)(2,1)S(1)}, bf16[4,32,512]{2,1,0:T(8,128)(2,1)S(1)}, u32[]{:S(2)}, u32[]{:S(2)}) collective-permute-start(bf16[4,32,512]{2,1,0:T(8,128)(2,1)S(1)} %get-tuple-element.22.refs_0_), channel_id=1, source_target_pairs={{0,0},{1,64},{2,128},{3,192},{4,32},{5,96},{6,160},{7,224},{8,1},{... | collective-permute-start | bytes 393224 | tf_op jit(solution)/shard_map/ppermute | solution.py:211
  67.1 8.5 %collective-permute-done.refs_1_ = bf16[4,32,512]{2,1,0:T(8,128)(2,1)S(1)} collective-permute-done((bf16[4,32,512]{2,1,0:T(8,128)(2,1)S(1)}, bf16[4,32,512]{2,1,0:T(8,128)(2,1)S(1)}, u32[]{:S(2)}, u32[]{:S(2)}) %collective-permute-start) | collective-permute-done | bytes 131104 | tf_op jit(solution)/shard_map/ppermute | solution.py:211
  75.7 0.1 collective-permute-start.1
  75.8 0.7 constant_dynamic-update-slice_fusion.4
  76.4 3.2 %collective-permute-start.2 = (bf16[2,4,32,512]{3,2,1,0:T(8,128)(2,1)S(1)}, bf16[2,4,32,512]{3,2,1,0:T(8,128)(2,1)S(1)}, u32[]{:S(2)}, u32[]{:S(2)}) collective-permute-start(bf16[2,4,32,512]{3,2,1,0:T(8,128)(2,1)S(1)} %pad_maximum_fusion.2), channel_id=1, source_target_pairs={{0,3},{1,0},{2,1},{3,2},{4,7},{5,4},{6,5},{7,6},{8,11},{9,8},{10,9... | collective-permute-start | bytes 786440 | tf_op jit(solution)/shard_map/ppermute | solution.py:211
  79.6 0.0 collective-permute-start.3
  79.6 0.0 collective-permute-done.8
  79.7 3.7 %collective-permute-start.9 = (bf16[4,32,512]{2,1,0:T(8,128)(2,1)}, bf16[4,32,512]{2,1,0:T(8,128)(2,1)S(1)}, u32[]{:S(2)}, u32[]{:S(2)}) collective-permute-start(bf16[4,32,512]{2,1,0:T(8,128)(2,1)} %shard_map.168), channel_id=1, source_target_pairs={{0,128},{1,192},{2,0},{3,64},{4,160},{5,224},{6,32},{7,96},{8,129}... | collective-permute-start | bytes 393224 | tf_op jit(solution)/shard_map/ppermute | solution.py:211
  83.4 1.6 %constant_dynamic-update-slice_fusion.3 = bf16[8,4,32,512]{3,2,1,0:T(8,128)(2,1)} fusion(bf16[8,4,32,512]{3,2,1,0:T(8,128)(2,1)} %constant_dynamic-update-slice_fusion.4, bf16[4,32,512]{2,1,0:T(8,128)(2,1)} %copy-done.7), kind=kLoop, calls=%fused_computation.21 | loop fusion | bytes 262144
  84.9 0.0 collective-permute-done.1
  84.9 0.7 constant_dynamic-update-slice_fusion.2
  85.7 0.7 collective-permute-done.2
  86.4 0.7 constant_dynamic-update-slice_fusion.1
  87.1 3.1 %collective-permute-done.3 = bf16[2,4,32,512]{3,2,1,0:T(8,128)(2,1)S(1)} collective-permute-done((bf16[2,4,32,512]{3,2,1,0:T(8,128)(2,1)S(1)}, bf16[2,4,32,512]{3,2,1,0:T(8,128)(2,1)S(1)}, u32[]{:S(2)}, u32[]{:S(2)}) %collective-permute-start.3) | collective-permute-done | bytes 262176 | tf_op jit(solution)/shard_map/ppermute | solution.py:211
  90.3 0.7 constant_dynamic-update-slice_fusion.refs_0_
  91.0 0.0 collective-permute-start.4
  91.0 3.2 %collective-permute-start.6 = (bf16[8,4,32,512]{3,2,1,0:T(8,128)(2,1)}, bf16[8,4,32,512]{3,2,1,0:T(8,128)(2,1)S(1)}, u32[]{:S(2)}, u32[]{:S(2)}) collective-permute-start(bf16[8,4,32,512]{3,2,1,0:T(8,128)(2,1)} %constant_dynamic-update-slice_fusion.refs_0_), channel_id=1, source_target_pairs={{0,24},{1,25},{2,26},{3,27},{4,28},{5,29},{6,30},{7,31},{8,0},{9,1... | collective-permute-start | bytes 3145736 | tf_op jit(solution)/shard_map/ppermute | solution.py:211
  94.2 0.0 collective-permute-done.9
  94.3 0.3 collective-permute-start.10
  94.6 6.4 %collective-permute-done.10.b_ref = bf16[2,4,32,512]{3,2,1,0:T(8,128)(2,1)S(1)} collective-permute-done((bf16[2,4,32,512]{3,2,1,0:T(8,128)(2,1)S(1)}, bf16[2,4,32,512]{3,2,1,0:T(8,128)(2,1)S(1)}, u32[]{:S(2)}, u32[]{:S(2)}) %collective-permute-start.10) | collective-permute-done | bytes 262176 | tf_op jit(solution)/shard_map/ppermute | solution.py:211
  100.9 0.1 pad_maximum_fusion.1
  101.0 0.1 collective-permute-start.11
  101.1 1.8 %copy.28 = bf16[512,4,256]{2,1,0:T(4,128)(2,1)} copy(bf16[512,4,256]{2,0,1:T(8,128)(2,1)S(1)} %bitcast.63) | data formatting | bytes 2097152
  102.9 0.1 collective-permute-done.11.c_ref
  103.0 2.4 %shard_map.169.refs_1_.refs_2_ = bf16[512,1024]{1,0:T(8,128)(2,1)S(1)} custom-call(s32[8]{0:T(128)S(1)} %stack.185.order_ref, bf16[2,4,32,512]{3,2,1,0:T(8,128)(2,1)S(1)} %pad_maximum_fusion.3.a_ref, bf16[2,4,32,512]{3,2,1,0:T(8,128)(2,1)S(1)} %collective-permute-done.10.b_ref, bf16[4,4,32,512]{3,2,1,0:T(8,128)(2,1)S(1)} %collective-permute-done.11.c_ref), custom_call_target="tpu_custom_call" | custom-call | flops 1000000 | bytes 4000000 | tf_op jit(solution)/shard_map/pallas_call | solution.py:137
  105.4 1.8 %collective-permute-done.4.refs_0_ = bf16[8,4,32,512]{3,2,1,0:T(8,128)(2,1)S(1)} collective-permute-done((bf16[8,4,32,512]{3,2,1,0:T(8,128)(2,1)}, bf16[8,4,32,512]{3,2,1,0:T(8,128)(2,1)S(1)}, u32[]{:S(2)}, u32[]{:S(2)}) %collective-permute-start.4) | collective-permute-done | bytes 1048608 | tf_op jit(solution)/shard_map/ppermute | solution.py:211
  107.3 0.1 collective-permute-start.5
  107.4 0.0 collective-permute-done.6.refs_1_
  107.4 3.3 %collective-permute-start.7 = (bf16[4,4,32,512]{3,2,1,0:T(8,128)(2,1)S(1)}, bf16[4,4,32,512]{3,2,1,0:T(8,128)(2,1)S(1)}, u32[]{:S(2)}, u32[]{:S(2)}) collective-permute-start(bf16[4,4,32,512]{3,2,1,0:T(8,128)(2,1)S(1)} %slice.19), channel_id=1, source_target_pairs={{0,24},{1,25},{2,26},{3,27},{4,28},{5,29},{6,30},{7,31},{8,0},{9,1... | collective-permute-start | bytes 1572872 | tf_op jit(solution)/shard_map/ppermute | solution.py:211
  110.7 4.6 %shard_map.170.refs_7_ = bf16[32,4,32,128]{3,2,1,0:T(8,128)(2,1)} custom-call(s32[32]{0:T(128)S(1)} %stack.176.place_ref, bf16[8,4,32,512]{3,2,1,0:T(8,128)(2,1)} %constant_dynamic-update-slice_fusion.refs_0_, bf16[512,1024]{1,0:T(8,128)(2,1)S(1)} %shard_map.169.refs_1_.refs_2_, bf16[1024,128]{1,0:T(8,128)(2,1)S(1)} %bitcast.65, ...), custom_call_target="tpu_custom_call" | custom-call | flops 2000000000 | bytes 3200000 | tf_op jit(solution)/shard_map/pallas_call | solution.py:185
  115.3 6.0 %shard_map.171.refs_7_ = bf16[32,4,32,128]{3,2,1,0:T(8,128)(2,1)} custom-call(s32[32]{0:T(128)S(1)} %stack.176.place_ref, bf16[8,4,32,512]{3,2,1,0:T(8,128)(2,1)S(1)} %collective-permute-done.4.refs_0_, bf16[8,4,32,512]{3,2,1,0:T(8,128)(2,1)S(1)} %collective-permute-done.6.refs_1_, ...), custom_call_target="tpu_custom_call", output_to_operand_aliasing={{}: (8, {})} | custom-call | flops 4000000000 | bytes 6400000 | tf_op jit(solution)/shard_map/pallas_call | solution.py:185
  121.3 0.0 collective-permute-done.5.refs_0_
  121.3 0.0 collective-permute-done.7.refs_1_
  121.3 3.9 %shard_map.172 = bf16[32,4,32,128]{3,2,1,0:T(8,128)(2,1)} custom-call(s32[32]{0:T(128)S(1)} %stack.176.place_ref, bf16[4,4,32,512]{3,2,1,0:T(8,128)(2,1)S(1)} %collective-permute-done.5.refs_0_, bf16[4,4,32,512]{3,2,1,0:T(8,128)(2,1)S(1)} %collective-permute-done.7.refs_1_, ...), custom_call_target="tpu_custom_call", output_to_operand_aliasing={{}: (8, {})} | custom-call | flops 2000000000 | bytes 3200000 | tf_op jit(solution)/shard_map/pallas_call | solution.py:185
  (27 shorter events, 0.2 us)
Async XLA Ops:
  3.4 16.7 %copy-start.8 = (bf16[1024,128]{1,0:T(8,128)(2,1)S(1)}, bf16[1024,128]{1,0:T(8,128)(2,1)}, u32[]{:S(2)}) copy-start(bf16[1024,128]{1,0:T(8,128)(2,1)} %param.30) | copy-start | bytes 786436
  3.4 18.2 %copy-start.13 = (bf16[256,32]{0,1:T(8,128)(2,1)S(1)}, bf16[256,32]{0,1:T(8,128)(2,1)}, u32[]{:S(2)}) copy-start(bf16[256,32]{0,1:T(8,128)(2,1)} %param.29) | copy-start | bytes 49156
  3.4 18.2 %copy-start.14 = (bf16[256,32]{0,1:T(8,128)(2,1)S(1)}, bf16[256,32]{0,1:T(8,128)(2,1)}, u32[]{:S(2)}) copy-start(bf16[256,32]{0,1:T(8,128)(2,1)} %param.28) | copy-start | bytes 49156
  3.4 18.3 %copy-start.9 = (bf16[256,256]{1,0:T(8,128)(2,1)S(1)}, bf16[256,256]{1,0:T(8,128)(2,1)}, u32[]{:S(2)}) copy-start(bf16[256,256]{1,0:T(8,128)(2,1)} %param.23) | copy-start | bytes 393220
  3.4 18.3 %copy-start.10 = (bf16[256,256]{1,0:T(8,128)(2,1)S(1)}, bf16[256,256]{1,0:T(8,128)(2,1)}, u32[]{:S(2)}) copy-start(bf16[256,256]{1,0:T(8,128)(2,1)} %param.22) | copy-start | bytes 393220
  3.4 18.3 %copy-start.11 = (bf16[256,256]{1,0:T(8,128)(2,1)S(1)}, bf16[256,256]{1,0:T(8,128)(2,1)}, u32[]{:S(2)}) copy-start(bf16[256,256]{1,0:T(8,128)(2,1)} %param.21) | copy-start | bytes 393220
  3.4 18.3 %copy-start.12 = (bf16[256,256]{1,0:T(8,128)(2,1)S(1)}, bf16[256,256]{1,0:T(8,128)(2,1)}, u32[]{:S(2)}) copy-start(bf16[256,256]{1,0:T(8,128)(2,1)} %param.20) | copy-start | bytes 393220
  3.5 44.7 %all-to-all-start = ((bf16[32,4,16,256]{3,2,1,0:T(8,128)(2,1)}), bf16[32,4,16,256]{3,2,1,0:T(8,128)(2,1)S(1)}, u32[]{:S(2)}, u32[]{:S(2)}) async-start(bf16[32,4,16,256]{3,2,1,0:T(8,128)(2,1)} %bitcast.1), calls=%async_computation | async-start | bytes 2097152 | tf_op jit(solution)/shard_map/all_to_all | solution.py:252
  16.7 31.5 %copy-start.1 = (bf16[256,256]{1,0:T(8,128)(2,1)S(1)}, bf16[256,256]{1,0:T(8,128)(2,1)}, u32[]{:S(2)}) copy-start(bf16[256,256]{1,0:T(8,128)(2,1)} %wo_ref.1) | copy-start | bytes 393220
  16.7 31.5 %copy-start.2 = (f32[256]{0:T(256)S(1)}, f32[256]{0:T(256)}, u32[]{:S(2)}) copy-start(f32[256]{0:T(256)} %param.19) | copy-start | bytes 3076
  16.7 31.5 %copy-start.3 = (f32[256]{0:T(256)S(1)}, f32[256]{0:T(256)}, u32[]{:S(2)}) copy-start(f32[256]{0:T(256)} %param.24) | copy-start | bytes 3076
  16.7 31.5 %copy-start.4 = (f32[256]{0:T(256)S(1)}, f32[256]{0:T(256)}, u32[]{:S(2)}) copy-start(f32[256]{0:T(256)} %param.26) | copy-start | bytes 3076
  16.7 31.4 %copy-start.5 = (f32[256]{0:T(256)S(1)}, f32[256]{0:T(256)}, u32[]{:S(2)}) copy-start(f32[256]{0:T(256)} %param.27) | copy-start | bytes 3076
  64.1 15.5 %copy-start = (bf16[4,32,512]{2,1,0:T(8,128)(2,1)}, bf16[4,32,512]{2,1,0:T(8,128)(2,1)S(1)}, u32[]{:S(2)}) copy-start(bf16[4,32,512]{2,1,0:T(8,128)(2,1)S(1)} %get-tuple-element.22.refs_0_) | copy-start | bytes 393220
  64.1 11.5 %collective-permute-start = (bf16[4,32,512]{2,1,0:T(8,128)(2,1)S(1)}, bf16[4,32,512]{2,1,0:T(8,128)(2,1)S(1)}, u32[]{:S(2)}, u32[]{:S(2)}) collective-permute-start(bf16[4,32,512]{2,1,0:T(8,128)(2,1)S(1)} %get-tuple-element.20), channel_id=1, source_target_pairs={{0,4},{1,5},{2,6},{3,7},{4,0},{5,1},{6,2},{7,3},{8,12},{9,13},{10,... | collective-permute-start | bytes 393224 | tf_op jit(solution)/shard_map/ppermute | solution.py:211
  65.2 14.4 %collective-permute-start.8 = (bf16[4,32,512]{2,1,0:T(8,128)(2,1)S(1)}, bf16[4,32,512]{2,1,0:T(8,128)(2,1)S(1)}, u32[]{:S(2)}, u32[]{:S(2)}) collective-permute-start(bf16[4,32,512]{2,1,0:T(8,128)(2,1)S(1)} %get-tuple-element.22.refs_0_), channel_id=1, source_target_pairs={{0,0},{1,64},{2,128},{3,192},{4,32},{5,96},{6,160},{7,224},{8,1},{... | collective-permute-start | bytes 393224 | tf_op jit(solution)/shard_map/ppermute | solution.py:211
  75.6 4.0 %copy-start.7 = (bf16[4,32,512]{2,1,0:T(8,128)(2,1)}, bf16[4,32,512]{2,1,0:T(8,128)(2,1)S(1)}, u32[]{:S(2)}) copy-start(bf16[4,32,512]{2,1,0:T(8,128)(2,1)S(1)} %collective-permute-done.refs_1_) | copy-start | bytes 393220
  75.7 9.3 %collective-permute-start.1 = (bf16[2,4,32,512]{3,2,1,0:T(8,128)(2,1)S(1)}, bf16[2,4,32,512]{3,2,1,0:T(8,128)(2,1)S(1)}, u32[]{:S(2)}, u32[]{:S(2)}) collective-permute-start(bf16[2,4,32,512]{3,2,1,0:T(8,128)(2,1)S(1)} %pad_maximum_fusion.2), channel_id=1, source_target_pairs={{0,1},{1,2},{2,3},{3,0},{4,5},{5,6},{6,7},{7,4},{8,9},{9,10},{10,1... | collective-permute-start | bytes 786440 | tf_op jit(solution)/shard_map/ppermute | solution.py:211
  76.4 10.0 %collective-permute-start.2 = (bf16[2,4,32,512]{3,2,1,0:T(8,128)(2,1)S(1)}, bf16[2,4,32,512]{3,2,1,0:T(8,128)(2,1)S(1)}, u32[]{:S(2)}, u32[]{:S(2)}) collective-permute-start(bf16[2,4,32,512]{3,2,1,0:T(8,128)(2,1)S(1)} %pad_maximum_fusion.2), channel_id=1, source_target_pairs={{0,3},{1,0},{2,1},{3,2},{4,7},{5,4},{6,5},{7,6},{8,11},{9,8},{10,9... | collective-permute-start | bytes 786440 | tf_op jit(solution)/shard_map/ppermute | solution.py:211
  79.6 10.6 %collective-permute-start.3 = (bf16[2,4,32,512]{3,2,1,0:T(8,128)(2,1)S(1)}, bf16[2,4,32,512]{3,2,1,0:T(8,128)(2,1)S(1)}, u32[]{:S(2)}, u32[]{:S(2)}) collective-permute-start(bf16[2,4,32,512]{3,2,1,0:T(8,128)(2,1)S(1)} %pad_maximum_fusion.2), channel_id=1, source_target_pairs={{0,2},{1,3},{2,0},{3,1},{4,6},{5,7},{6,4},{7,5},{8,10},{9,11},{10,... | collective-permute-start | bytes 786440 | tf_op jit(solution)/shard_map/ppermute | solution.py:211
  79.7 14.6 %collective-permute-start.9 = (bf16[4,32,512]{2,1,0:T(8,128)(2,1)}, bf16[4,32,512]{2,1,0:T(8,128)(2,1)S(1)}, u32[]{:S(2)}, u32[]{:S(2)}) collective-permute-start(bf16[4,32,512]{2,1,0:T(8,128)(2,1)} %shard_map.168), channel_id=1, source_target_pairs={{0,128},{1,192},{2,0},{3,64},{4,160},{5,224},{6,32},{7,96},{8,129}... | collective-permute-start | bytes 393224 | tf_op jit(solution)/shard_map/ppermute | solution.py:211
  91.0 16.2 %collective-permute-start.4 = (bf16[8,4,32,512]{3,2,1,0:T(8,128)(2,1)}, bf16[8,4,32,512]{3,2,1,0:T(8,128)(2,1)S(1)}, u32[]{:S(2)}, u32[]{:S(2)}) collective-permute-start(bf16[8,4,32,512]{3,2,1,0:T(8,128)(2,1)} %constant_dynamic-update-slice_fusion.refs_0_), channel_id=1, source_target_pairs={{0,8},{1,9},{2,10},{3,11},{4,12},{5,13},{6,14},{7,15},{8,16},{9,17... | collective-permute-start | bytes 3145736 | tf_op jit(solution)/shard_map/ppermute | solution.py:211
  91.0 16.4 %collective-permute-start.6 = (bf16[8,4,32,512]{3,2,1,0:T(8,128)(2,1)}, bf16[8,4,32,512]{3,2,1,0:T(8,128)(2,1)S(1)}, u32[]{:S(2)}, u32[]{:S(2)}) collective-permute-start(bf16[8,4,32,512]{3,2,1,0:T(8,128)(2,1)} %constant_dynamic-update-slice_fusion.refs_0_), channel_id=1, source_target_pairs={{0,24},{1,25},{2,26},{3,27},{4,28},{5,29},{6,30},{7,31},{8,0},{9,1... | collective-permute-start | bytes 3145736 | tf_op jit(solution)/shard_map/ppermute | solution.py:211
  94.3 6.6 %collective-permute-start.10 = (bf16[2,4,32,512]{3,2,1,0:T(8,128)(2,1)S(1)}, bf16[2,4,32,512]{3,2,1,0:T(8,128)(2,1)S(1)}, u32[]{:S(2)}, u32[]{:S(2)}) collective-permute-start(bf16[2,4,32,512]{3,2,1,0:T(8,128)(2,1)S(1)} %pad_maximum_fusion.3.a_ref), channel_id=1, source_target_pairs={{0,64},{1,65},{2,66},{3,67},{4,68},{5,69},{6,70},{7,71},{8,72},{9,... | collective-permute-start | bytes 786440 | tf_op jit(solution)/shard_map/ppermute | solution.py:211
  101.0 2.0 %collective-permute-start.11 = (bf16[4,4,32,512]{3,2,1,0:T(8,128)(2,1)S(1)}, bf16[4,4,32,512]{3,2,1,0:T(8,128)(2,1)S(1)}, u32[]{:S(2)}, u32[]{:S(2)}) collective-permute-start(bf16[4,4,32,512]{3,2,1,0:T(8,128)(2,1)S(1)} %pad_maximum_fusion.1), channel_id=1, source_target_pairs={{0,32},{1,33},{2,34},{3,35},{4,36},{5,37},{6,38},{7,39},{8,40},{9,... | collective-permute-start | bytes 1572872 | tf_op jit(solution)/shard_map/ppermute | solution.py:211
  102.9 7.9 %copy-start.6 = (f32[128]{0:T(128)S(1)}, f32[128]{0:T(128)}, u32[]{:S(2)}) copy-start(f32[128]{0:T(128)} %param.31) | copy-start | bytes 1540
  107.3 14.0 %collective-permute-start.5 = (bf16[4,4,32,512]{3,2,1,0:T(8,128)(2,1)S(1)}, bf16[4,4,32,512]{3,2,1,0:T(8,128)(2,1)S(1)}, u32[]{:S(2)}, u32[]{:S(2)}) collective-permute-start(bf16[4,4,32,512]{3,2,1,0:T(8,128)(2,1)S(1)} %slice.18), channel_id=1, source_target_pairs={{0,8},{1,9},{2,10},{3,11},{4,12},{5,13},{6,14},{7,15},{8,16},{9,17... | collective-permute-start | bytes 1572872 | tf_op jit(solution)/shard_map/ppermute | solution.py:211
  107.4 13.9 %collective-permute-start.7 = (bf16[4,4,32,512]{3,2,1,0:T(8,128)(2,1)S(1)}, bf16[4,4,32,512]{3,2,1,0:T(8,128)(2,1)S(1)}, u32[]{:S(2)}, u32[]{:S(2)}) collective-permute-start(bf16[4,4,32,512]{3,2,1,0:T(8,128)(2,1)S(1)} %slice.19), channel_id=1, source_target_pairs={{0,24},{1,25},{2,26},{3,27},{4,28},{5,29},{6,30},{7,31},{8,0},{9,1... | collective-permute-start | bytes 1572872 | tf_op jit(solution)/shard_map/ppermute | solution.py:211

commit v3 on v2

--- a/solution.py
+++ b/solution.py
@@ -130,7 +130,7 @@
             part = jnp.concatenate(
                 [f_ref[c, pl.ds(b * 4 + a, 32, stride=32), :] for a in range(4)], axis=0
             )
-            out_ref[c * 128:(c + 1) * 128, b * 128:(b + 1) * 128] = part.T.astype(BF16)
+            out_ref[c * 128:(c + 1) * 128, b * 128:(b + 1) * 128] = part.astype(BF16).T
 
 
 def rearrange(order, a, b, c):
@@ -149,29 +149,39 @@
     r_ref, w_ref, inv_ref, same_ref, bias_ref = refs[count:count + 5]
     out_ref, x_ref, y_ref, sems = refs[count + 5 + has_old:]
     copies = []
-    at = 0
-    for part in parts:
-        for half in range(part.shape[0] // 4):
-            outer = dot(part[half * 4:half * 4 + 4].reshape(512, 512), r_ref[...]).astype(BF16)
-            for n in range(16):
-                a = jnp.concatenate(
-                    [outer[n * 32:(n + 1) * 32, b * 128:(b + 1) * 128] for b in range(8)], axis=0
-                )
-                t = a.T
-                for q in range(4):
-                    x_ref[n * 32:(n + 1) * 32, q * 256:(q + 1) * 256] = t[q * 32:(q + 1) * 32, :]
-            y = dot(x_ref[...], w_ref[...])
-            for n in range(16):
-                lane = (first + at) * 4 + n
-                scale = jnp.broadcast_to(inv_ref[:, lane:lane + 1], (32, 128))
-                same = jnp.broadcast_to(same_ref[:, lane:lane + 1], (32, 128))
-                result = y[n * 32:(n + 1) * 32] * scale + same * bias_ref[...]
-                y_ref[at + n // 4, n % 4] = result.astype(BF16)
-            for s in range(at, at + 4):
-                copy = pltpu.make_async_copy(y_ref.at[s], out_ref.at[place_ref[first + s]], sems.at[s])
-                copy.start()
-                copies.append(copy)
-            at += 4
+    halves = [(part, n) for part in parts for n in range(0, part.shape[0], 2)]
+
+    def outer_product(part, n):
+        return dot(part[n:n + 2].reshape(256, 512), r_ref[...]).astype(BF16)
+
+    def project(at):
+        y = dot(x_ref[(at // 2) % 2], w_ref[...])
+        for n in range(8):
+            lane = (first + at) * 4 + n
+            scale = jnp.broadcast_to(inv_ref[:, lane:lane + 1], (32, 128))
+            same = jnp.broadcast_to(same_ref[:, lane:lane + 1], (32, 128))
+            result = y[n * 32:(n + 1) * 32] * scale + same * bias_ref[...]
+            y_ref[at + n // 4, n % 4] = result.astype(BF16)
+        for s in range(at, at + 2):
+            copy = pltpu.make_async_copy(y_ref.at[s], out_ref.at[place_ref[first + s]], sems.at[s])
+            copy.start()
+            copies.append(copy)
+
+    following = outer_product(*halves[0])
+    for i in range(len(halves)):
+        outer = following
+        if i + 1 < len(halves):
+            following = outer_product(*halves[i + 1])
+        for n in range(8):
+            a = jnp.concatenate(
+                [outer[n * 32:(n + 1) * 32, b * 128:(b + 1) * 128] for b in range(8)], axis=0
+            )
+            t = a.T
+            for q in range(4):
+                x_ref[i % 2, n * 32:(n + 1) * 32, q * 256:(q + 1) * 256] = t[q * 32:(q + 1) * 32, :]
+        if i:
+            project(2 * i - 2)
+    project(2 * len(halves) - 2)
     for copy in copies:
         copy.wait()
 
@@ -188,7 +198,7 @@
         out_specs=anywhere,
         out_shape=jax.ShapeDtypeStruct((32, 4, 32, 128), BF16),
         scratch_shapes=[
-            pltpu.VMEM((512, 1024), BF16),
+            pltpu.VMEM((2, 256, 1024), BF16),
             pltpu.VMEM((sources, 4, 32, 128), BF16),
             pltpu.SemaphoreType.DMA((sources,)),
         ],
@@ -298,11 +308,11 @@
     below, above = permute_all(line, shifted(1, 1)), permute_all(line, shifted(1, 3))
     parts = [line, below, above, permute_all(below[:4], shifted(1, 1)), permute_all(above[4:], shifted(1, 3))]
     right_c = permute_all(
-        jnp.concatenate([right_a, right_b]), lambda zl, co, x, zh, y: (zl, 1 - co, x, zh, y)
+        after(jnp.concatenate([right_a, right_b]), updated), lambda zl, co, x, zh, y: (zl, 1 - co, x, zh, y)
     )
     r = rearrange(order, right_a, right_b, right_c)
     out = None
-    for first, some in ((0, parts[:1]), (8, parts[1:3]), (24, parts[3:])):
+    for first, some in ((0, parts[:3]), (24, parts[3:])):
         out = pair(first, place, some, r, wpair, inverse, same, chain_bias[None], out)
     return updated, out.reshape(128, 32, 128)
 

time: 126 us -> 123 us (0.976)
  the two profiles are of different devices: /device:TPU:32 before, /device:TPU:38 now
where the time goes in v3:
time: 123 us
  waiting for transfers between devices  44.5 us (36%)
  starting transfers between devices  32.1 us (26%)
  Pallas kernels  28.5 us (23%)
  local copies, waits for them, and re-layouts  12.3 us (10%)
  other arithmetic  2.18 us (2%)
  matrix products  1.51 us (1%)
  between operations  1.43 us (1%)
    all_to_all x1, waiting for transfers between devices, body(): lax.all_to_all(moved, 'col', split_axis=0, concat_axis=0, tiled=True)  24.6 us
    ppermute x12, waiting for transfers between devices, permute_all(): return lax.ppermute(value, ('row', 'col'), pairs)  19.9 us
    ppermute x12, starting transfers between devices, permute_all(): return lax.ppermute(value, ('row', 'col'), pairs)  18.7 us
    pallas_call x1, Pallas kernels, attend(): pl.pallas_call(attend_kernel, grid=(count,), in_specs=[pl.BlockSpec((grou...  16 us
    all_to_all x1, starting transfers between devices, body(): lax.all_to_all(moved, 'col', split_axis=0, concat_axis=0, tiled=True)  13.5 us
    pallas_call x2, Pallas kernels, pair(): pl.pallas_call(functools.partial(pair_kernel, first, count, has_old), in_...  10.6 us
    unnamed x36, local copies, waits for them, and re-layouts  6.66 us
  transfers between devices with their start and end apart: 13, of which 6 were waited for; matrix products, arithmetic and copies ran while one was open for 11% of the time, Pallas kernels for 8%

profile of v3, /device:TPU:38, one launch (start us, length us, event | category | flops | bytes accessed | tf_op | source)
XLA Modules:
  0.0 122.6 jit_solution(2050551918819771581)
XLA Ops:
  0.6 2.8 %copy.25 = bf16[16,128,256]{2,0,1:T(8,128)(2,1)} copy(bf16[16,128,256]{2,1,0:T(8,128)(2,1)} %param.16) | data formatting | bytes 2097152 | tf_op args[0]
  3.4 0.0 copy-start.10
  3.4 0.0 copy-start.11
  3.4 0.0 copy-start.12
  3.5 13.5 %all-to-all-start = ((bf16[32,4,16,256]{3,2,1,0:T(8,128)(2,1)}), bf16[32,4,16,256]{3,2,1,0:T(8,128)(2,1)S(1)}, u32[]{:S(2)}, u32[]{:S(2)}) async-start(bf16[32,4,16,256]{3,2,1,0:T(8,128)(2,1)} %bitcast.1), calls=%async_computation | async-start | bytes 2097152 | tf_op jit(solution)/shard_map/all_to_all | solution.py:262
  16.9 0.0 copy-start.1
  16.9 0.0 copy-start.2
  17.0 0.0 copy-start.3
  17.0 0.0 copy-start.4
  17.0 0.0 copy-start.5
  17.3 0.1 stack.176.place_ref
  17.4 0.1 iota_add_fusion
  17.5 0.1 add.495
  17.6 0.8 dynamic_slice.19
  18.4 0.8 dynamic_slice.18
  19.2 1.1 dynamic-slice_convert_fusion.2
  20.2 0.1 copy.30
  20.4 0.0 copy-done.8
  20.4 0.1 copy.27
  20.5 0.1 stack.185.order_ref
  20.6 1.3 %fusion = f32[32,128]{1,0:T(8,128)S(1)} fusion(s32[512,1024]{1,0:T(8,128)} %param.17, s32[]{:T(128)S(6)} %select_n.389, s32[]{:T(128)S(6)} %select_n.390), kind=kOutput, calls=%fused_computation.1 | convolution fusion | flops 4284416 | bytes 540680 | tf_op jit(solution)/shard_map/dot_general | solution.py:280
  21.9 0.0 copy-done.13
  22.0 0.1 pad_maximum_fusion.wqkvg_ref
  22.1 0.1 compare_convert_fusion
  22.1 0.2 fusion.1
  22.3 24.6 %all-to-all-done.parts_ref = bf16[32,4,16,256]{3,2,1,0:T(8,128)(2,1)S(1)} async-done(((bf16[32,4,16,256]{3,2,1,0:T(8,128)(2,1)}), bf16[32,4,16,256]{3,2,1,0:T(8,128)(2,1)S(1)}, u32[]{:S(2)}, u32[]{:S(2)}) %all-to-all-start) | async-done | bytes 1048608 | tf_op jit(solution)/shard_map/all_to_all | solution.py:262
  46.9 16.0 %shard_map.167 = (bf16[4,512,256]{2,1,0:T(8,128)(2,1)S(1)}, bf16[4,32,512]{2,1,0:T(8,128)(2,1)S(1)}, bf16[4,32,512]{2,1,0:T(8,128)(2,1)S(1)}) custom-call(bf16[32,4,16,256]{3,2,1,0:T(8,128)(2,1)S(1)} %all-to-all-done.parts_ref, f32[4,1,512]{2,1,0:T(1,128)S(1)} %reshape.294.mask_ref, f32[1,256]{1,0:T(1,128)S(1)} %bitcast.68, ...), custom_call_target="tpu_custom_call" | custom-call | flops 16000000000 | bytes 4000000 | tf_op jit(solution)/shard_map/pallas_call | solution.py:89
  62.9 0.0 copy-start
  62.9 1.0 collective-permute-start
  64.0 1.9 %collective-permute-start.8 = (bf16[4,32,512]{2,1,0:T(8,128)(2,1)S(1)}, bf16[4,32,512]{2,1,0:T(8,128)(2,1)S(1)}, u32[]{:S(2)}, u32[]{:S(2)}) collective-permute-start(bf16[4,32,512]{2,1,0:T(8,128)(2,1)S(1)} %get-tuple-element.22.refs_0_), channel_id=1, source_target_pairs={{0,0},{1,64},{2,128},{3,192},{4,32},{5,96},{6,160},{7,224},{8,1},{... | collective-permute-start | bytes 393224 | tf_op jit(solution)/shard_map/ppermute | solution.py:221
  65.9 8.0 %collective-permute-done.refs_1_ = bf16[4,32,512]{2,1,0:T(8,128)(2,1)S(1)} collective-permute-done((bf16[4,32,512]{2,1,0:T(8,128)(2,1)S(1)}, bf16[4,32,512]{2,1,0:T(8,128)(2,1)S(1)}, u32[]{:S(2)}, u32[]{:S(2)}) %collective-permute-start) | collective-permute-done | bytes 131104 | tf_op jit(solution)/shard_map/ppermute | solution.py:221
  73.9 0.1 collective-permute-start.1
  74.0 0.7 constant_dynamic-update-slice_fusion.4
  74.6 3.2 %collective-permute-start.2 = (bf16[2,4,32,512]{3,2,1,0:T(8,128)(2,1)S(1)}, bf16[2,4,32,512]{3,2,1,0:T(8,128)(2,1)S(1)}, u32[]{:S(2)}, u32[]{:S(2)}) collective-permute-start(bf16[2,4,32,512]{3,2,1,0:T(8,128)(2,1)S(1)} %pad_maximum_fusion.2), channel_id=1, source_target_pairs={{0,3},{1,0},{2,1},{3,2},{4,7},{5,4},{6,5},{7,6},{8,11},{9,8},{10,9... | collective-permute-start | bytes 786440 | tf_op jit(solution)/shard_map/ppermute | solution.py:221
  77.8 0.0 collective-permute-start.3
  77.8 0.8 collective-permute-done.8
  78.7 0.0 copy-done.7
  78.7 4.9 %collective-permute-start.9 = (bf16[4,32,512]{2,1,0:T(8,128)(2,1)}, bf16[4,32,512]{2,1,0:T(8,128)(2,1)S(1)}, u32[]{:S(2)}, u32[]{:S(2)}) collective-permute-start(bf16[4,32,512]{2,1,0:T(8,128)(2,1)} %shard_map.168), channel_id=1, source_target_pairs={{0,128},{1,192},{2,0},{3,64},{4,160},{5,224},{6,32},{7,96},{8,129}... | collective-permute-start | bytes 393224 | tf_op jit(solution)/shard_map/ppermute | solution.py:221
  83.6 1.6 %constant_dynamic-update-slice_fusion.3 = bf16[8,4,32,512]{3,2,1,0:T(8,128)(2,1)} fusion(bf16[8,4,32,512]{3,2,1,0:T(8,128)(2,1)} %constant_dynamic-update-slice_fusion.4, bf16[4,32,512]{2,1,0:T(8,128)(2,1)} %copy-done.7), kind=kLoop, calls=%fused_computation.22 | loop fusion | bytes 262144
  85.2 0.0 collective-permute-done.1
  85.2 0.7 constant_dynamic-update-slice_fusion.2
  85.9 0.0 collective-permute-done.2
  85.9 0.7 constant_dynamic-update-slice_fusion.1
  86.7 0.0 collective-permute-done.3
  86.7 0.7 constant_dynamic-update-slice_fusion.refs_0_
  87.4 4.1 %collective-permute-start.4 = (bf16[8,4,32,512]{3,2,1,0:T(8,128)(2,1)}, bf16[8,4,32,512]{3,2,1,0:T(8,128)(2,1)S(1)}, u32[]{:S(2)}, u32[]{:S(2)}) collective-permute-start(bf16[8,4,32,512]{3,2,1,0:T(8,128)(2,1)} %constant_dynamic-update-slice_fusion.refs_0_), channel_id=1, source_target_pairs={{0,8},{1,9},{2,10},{3,11},{4,12},{5,13},{6,14},{7,15},{8,16},{9,17... | collective-permute-start | bytes 3145736 | tf_op jit(solution)/shard_map/ppermute | solution.py:221
  91.5 0.0 collective-permute-start.6
  91.5 0.0 collective-permute-done.9
  91.5 0.3 collective-permute-start.10
  91.8 1.8 %copy.32 = bf16[4,512,256]{2,0,1:T(4,128)(2,1)} copy(bf16[4,512,256]{2,1,0:T(8,128)(2,1)S(1)} %get-tuple-element.18) | data formatting | bytes 2097152 | tf_op jit(solution)/shard_map/pallas_call | solution.py:89
  93.6 6.2 %collective-permute-done.10.b_ref = bf16[2,4,32,512]{3,2,1,0:T(8,128)(2,1)S(1)} collective-permute-done((bf16[2,4,32,512]{3,2,1,0:T(8,128)(2,1)S(1)}, bf16[2,4,32,512]{3,2,1,0:T(8,128)(2,1)S(1)}, u32[]{:S(2)}, u32[]{:S(2)}) %collective-permute-start.10) | collective-permute-done | bytes 262176 | tf_op jit(solution)/shard_map/ppermute | solution.py:221
  99.8 0.8 pad_maximum_fusion.1.refs_0_
  100.6 0.0 collective-permute-start.11
  100.6 2.1 %collective-permute-done.11.c_ref = bf16[4,4,32,512]{3,2,1,0:T(8,128)(2,1)S(1)} collective-permute-done((bf16[4,4,32,512]{3,2,1,0:T(8,128)(2,1)}, bf16[4,4,32,512]{3,2,1,0:T(8,128)(2,1)S(1)}, u32[]{:S(2)}, u32[]{:S(2)}) %collective-permute-start.11) | collective-permute-done | bytes 524320 | tf_op jit(solution)/shard_map/ppermute | solution.py:221
  102.7 2.0 %shard_map.170.refs_3_.refs_2_ = bf16[512,1024]{1,0:T(8,128)(2,1)S(1)} custom-call(s32[8]{0:T(128)S(1)} %stack.185.order_ref, bf16[2,4,32,512]{3,2,1,0:T(8,128)(2,1)S(1)} %pad_maximum_fusion.3.a_ref, bf16[2,4,32,512]{3,2,1,0:T(8,128)(2,1)S(1)} %collective-permute-done.10.b_ref, bf16[4,4,32,512]{3,2,1,0:T(8,128)(2,1)S(1)} %collective-permute-done.11.c_ref), custom_call_target="tpu_custom_call" | custom-call | flops 1000000 | bytes 4000000 | tf_op jit(solution)/shard_map/pallas_call | solution.py:137
  104.7 0.0 collective-permute-done.4.refs_1_
  104.8 3.1 %collective-permute-start.5 = (bf16[4,4,32,512]{3,2,1,0:T(8,128)(2,1)S(1)}, bf16[4,4,32,512]{3,2,1,0:T(8,128)(2,1)S(1)}, u32[]{:S(2)}, u32[]{:S(2)}) collective-permute-start(bf16[4,4,32,512]{3,2,1,0:T(8,128)(2,1)S(1)} %slice.18), channel_id=1, source_target_pairs={{0,8},{1,9},{2,10},{3,11},{4,12},{5,13},{6,14},{7,15},{8,16},{9,17... | collective-permute-start | bytes 1572872 | tf_op jit(solution)/shard_map/ppermute | solution.py:221
  107.8 0.0 collective-permute-done.6.refs_2_
  107.8 1.1 slice.19
  108.9 0.1 collective-permute-start.7
  109.0 7.5 %shard_map.171.refs_7_ = bf16[32,4,32,128]{3,2,1,0:T(8,128)(2,1)} custom-call(s32[32]{0:T(128)S(1)} %stack.176.place_ref, bf16[8,4,32,512]{3,2,1,0:T(8,128)(2,1)} %constant_dynamic-update-slice_fusion.refs_0_, bf16[8,4,32,512]{3,2,1,0:T(8,128)(2,1)S(1)} %collective-permute-done.4.refs_1_, bf16[8,4,32,512]{3,2,1,0:T(8,128)(2,1)} %collective-permute-done.6.refs_2_, ...), custom_call_target="tpu_custom_call" | custom-call | flops 6000000000 | bytes 9600000 | tf_op jit(solution)/shard_map/pallas_call | solution.py:195
  116.6 0.0 collective-permute-done.5.refs_0_
  116.6 2.8 %collective-permute-done.7.refs_1_ = bf16[4,4,32,512]{3,2,1,0:T(8,128)(2,1)S(1)} collective-permute-done((bf16[4,4,32,512]{3,2,1,0:T(8,128)(2,1)S(1)}, bf16[4,4,32,512]{3,2,1,0:T(8,128)(2,1)S(1)}, u32[]{:S(2)}, u32[]{:S(2)}) %collective-permute-start.7) | collective-permute-done | bytes 524320 | tf_op jit(solution)/shard_map/ppermute | solution.py:221
  119.4 3.1 %shard_map.172 = bf16[32,4,32,128]{3,2,1,0:T(8,128)(2,1)} custom-call(s32[32]{0:T(128)S(1)} %stack.176.place_ref, bf16[4,4,32,512]{3,2,1,0:T(8,128)(2,1)S(1)} %collective-permute-done.5.refs_0_, bf16[4,4,32,512]{3,2,1,0:T(8,128)(2,1)S(1)} %collective-permute-done.7.refs_1_, ...), custom_call_target="tpu_custom_call", output_to_operand_aliasing={{}: (8, {})} | custom-call | flops 2000000000 | bytes 3200000 | tf_op jit(solution)/shard_map/pallas_call | solution.py:195
  (27 shorter events, 0.1 us)
Async XLA Ops:
  3.4 17.0 %copy-start.8 = (bf16[1024,128]{1,0:T(8,128)(2,1)S(1)}, bf16[1024,128]{1,0:T(8,128)(2,1)}, u32[]{:S(2)}) copy-start(bf16[1024,128]{1,0:T(8,128)(2,1)} %param.30) | copy-start | bytes 786436
  3.4 18.5 %copy-start.13 = (bf16[256,32]{0,1:T(8,128)(2,1)S(1)}, bf16[256,32]{0,1:T(8,128)(2,1)}, u32[]{:S(2)}) copy-start(bf16[256,32]{0,1:T(8,128)(2,1)} %param.29) | copy-start | bytes 49156
  3.4 18.5 %copy-start.14 = (bf16[256,32]{0,1:T(8,128)(2,1)S(1)}, bf16[256,32]{0,1:T(8,128)(2,1)}, u32[]{:S(2)}) copy-start(bf16[256,32]{0,1:T(8,128)(2,1)} %param.28) | copy-start | bytes 49156
  3.4 18.5 %copy-start.9 = (bf16[256,256]{1,0:T(8,128)(2,1)S(1)}, bf16[256,256]{1,0:T(8,128)(2,1)}, u32[]{:S(2)}) copy-start(bf16[256,256]{1,0:T(8,128)(2,1)} %param.23) | copy-start | bytes 393220
  3.4 18.5 %copy-start.10 = (bf16[256,256]{1,0:T(8,128)(2,1)S(1)}, bf16[256,256]{1,0:T(8,128)(2,1)}, u32[]{:S(2)}) copy-start(bf16[256,256]{1,0:T(8,128)(2,1)} %param.22) | copy-start | bytes 393220
  3.4 18.5 %copy-start.11 = (bf16[256,256]{1,0:T(8,128)(2,1)S(1)}, bf16[256,256]{1,0:T(8,128)(2,1)}, u32[]{:S(2)}) copy-start(bf16[256,256]{1,0:T(8,128)(2,1)} %param.21) | copy-start | bytes 393220
  3.4 18.5 %copy-start.12 = (bf16[256,256]{1,0:T(8,128)(2,1)S(1)}, bf16[256,256]{1,0:T(8,128)(2,1)}, u32[]{:S(2)}) copy-start(bf16[256,256]{1,0:T(8,128)(2,1)} %param.20) | copy-start | bytes 393220
  3.5 43.5 %all-to-all-start = ((bf16[32,4,16,256]{3,2,1,0:T(8,128)(2,1)}), bf16[32,4,16,256]{3,2,1,0:T(8,128)(2,1)S(1)}, u32[]{:S(2)}, u32[]{:S(2)}) async-start(bf16[32,4,16,256]{3,2,1,0:T(8,128)(2,1)} %bitcast.1), calls=%async_computation | async-start | bytes 2097152 | tf_op jit(solution)/shard_map/all_to_all | solution.py:262
  16.9 30.0 %copy-start.1 = (bf16[256,256]{1,0:T(8,128)(2,1)S(1)}, bf16[256,256]{1,0:T(8,128)(2,1)}, u32[]{:S(2)}) copy-start(bf16[256,256]{1,0:T(8,128)(2,1)} %wo_ref.1) | copy-start | bytes 393220
  16.9 30.0 %copy-start.2 = (f32[256]{0:T(256)S(1)}, f32[256]{0:T(256)}, u32[]{:S(2)}) copy-start(f32[256]{0:T(256)} %param.19) | copy-start | bytes 3076
  17.0 30.0 %copy-start.3 = (f32[256]{0:T(256)S(1)}, f32[256]{0:T(256)}, u32[]{:S(2)}) copy-start(f32[256]{0:T(256)} %param.24) | copy-start | bytes 3076
  17.0 30.0 %copy-start.4 = (f32[256]{0:T(256)S(1)}, f32[256]{0:T(256)}, u32[]{:S(2)}) copy-start(f32[256]{0:T(256)} %param.26) | copy-start | bytes 3076
  17.0 30.0 %copy-start.5 = (f32[256]{0:T(256)S(1)}, f32[256]{0:T(256)}, u32[]{:S(2)}) copy-start(f32[256]{0:T(256)} %param.27) | copy-start | bytes 3076
  62.9 15.8 %copy-start = (bf16[4,32,512]{2,1,0:T(8,128)(2,1)}, bf16[4,32,512]{2,1,0:T(8,128)(2,1)S(1)}, u32[]{:S(2)}) copy-start(bf16[4,32,512]{2,1,0:T(8,128)(2,1)S(1)} %get-tuple-element.22.refs_0_) | copy-start | bytes 393220
  62.9 10.9 %collective-permute-start = (bf16[4,32,512]{2,1,0:T(8,128)(2,1)S(1)}, bf16[4,32,512]{2,1,0:T(8,128)(2,1)S(1)}, u32[]{:S(2)}, u32[]{:S(2)}) collective-permute-start(bf16[4,32,512]{2,1,0:T(8,128)(2,1)S(1)} %get-tuple-element.20), channel_id=1, source_target_pairs={{0,4},{1,5},{2,6},{3,7},{4,0},{5,1},{6,2},{7,3},{8,12},{9,13},{10,... | collective-permute-start | bytes 393224 | tf_op jit(solution)/shard_map/ppermute | solution.py:221
  64.0 14.7 %collective-permute-start.8 = (bf16[4,32,512]{2,1,0:T(8,128)(2,1)S(1)}, bf16[4,32,512]{2,1,0:T(8,128)(2,1)S(1)}, u32[]{:S(2)}, u32[]{:S(2)}) collective-permute-start(bf16[4,32,512]{2,1,0:T(8,128)(2,1)S(1)} %get-tuple-element.22.refs_0_), channel_id=1, source_target_pairs={{0,0},{1,64},{2,128},{3,192},{4,32},{5,96},{6,160},{7,224},{8,1},{... | collective-permute-start | bytes 393224 | tf_op jit(solution)/shard_map/ppermute | solution.py:221
  73.8 4.9 %copy-start.7 = (bf16[4,32,512]{2,1,0:T(8,128)(2,1)}, bf16[4,32,512]{2,1,0:T(8,128)(2,1)S(1)}, u32[]{:S(2)}) copy-start(bf16[4,32,512]{2,1,0:T(8,128)(2,1)S(1)} %collective-permute-done.refs_1_) | copy-start | bytes 393220
  73.9 11.3 %collective-permute-start.1 = (bf16[2,4,32,512]{3,2,1,0:T(8,128)(2,1)S(1)}, bf16[2,4,32,512]{3,2,1,0:T(8,128)(2,1)S(1)}, u32[]{:S(2)}, u32[]{:S(2)}) collective-permute-start(bf16[2,4,32,512]{3,2,1,0:T(8,128)(2,1)S(1)} %pad_maximum_fusion.2), channel_id=1, source_target_pairs={{0,1},{1,2},{2,3},{3,0},{4,5},{5,6},{6,7},{7,4},{8,9},{9,10},{10,1... | collective-permute-start | bytes 786440 | tf_op jit(solution)/shard_map/ppermute | solution.py:221
  74.6 11.3 %collective-permute-start.2 = (bf16[2,4,32,512]{3,2,1,0:T(8,128)(2,1)S(1)}, bf16[2,4,32,512]{3,2,1,0:T(8,128)(2,1)S(1)}, u32[]{:S(2)}, u32[]{:S(2)}) collective-permute-start(bf16[2,4,32,512]{3,2,1,0:T(8,128)(2,1)S(1)} %pad_maximum_fusion.2), channel_id=1, source_target_pairs={{0,3},{1,0},{2,1},{3,2},{4,7},{5,4},{6,5},{7,6},{8,11},{9,8},{10,9... | collective-permute-start | bytes 786440 | tf_op jit(solution)/shard_map/ppermute | solution.py:221
  77.8 8.8 %collective-permute-start.3 = (bf16[2,4,32,512]{3,2,1,0:T(8,128)(2,1)S(1)}, bf16[2,4,32,512]{3,2,1,0:T(8,128)(2,1)S(1)}, u32[]{:S(2)}, u32[]{:S(2)}) collective-permute-start(bf16[2,4,32,512]{3,2,1,0:T(8,128)(2,1)S(1)} %pad_maximum_fusion.2), channel_id=1, source_target_pairs={{0,2},{1,3},{2,0},{3,1},{4,6},{5,7},{6,4},{7,5},{8,10},{9,11},{10,... | collective-permute-start | bytes 786440 | tf_op jit(solution)/shard_map/ppermute | solution.py:221
  78.7 12.8 %collective-permute-start.9 = (bf16[4,32,512]{2,1,0:T(8,128)(2,1)}, bf16[4,32,512]{2,1,0:T(8,128)(2,1)S(1)}, u32[]{:S(2)}, u32[]{:S(2)}) collective-permute-start(bf16[4,32,512]{2,1,0:T(8,128)(2,1)} %shard_map.168), channel_id=1, source_target_pairs={{0,128},{1,192},{2,0},{3,64},{4,160},{5,224},{6,32},{7,96},{8,129}... | collective-permute-start | bytes 393224 | tf_op jit(solution)/shard_map/ppermute | solution.py:221
  87.4 17.3 %collective-permute-start.4 = (bf16[8,4,32,512]{3,2,1,0:T(8,128)(2,1)}, bf16[8,4,32,512]{3,2,1,0:T(8,128)(2,1)S(1)}, u32[]{:S(2)}, u32[]{:S(2)}) collective-permute-start(bf16[8,4,32,512]{3,2,1,0:T(8,128)(2,1)} %constant_dynamic-update-slice_fusion.refs_0_), channel_id=1, source_target_pairs={{0,8},{1,9},{2,10},{3,11},{4,12},{5,13},{6,14},{7,15},{8,16},{9,17... | collective-permute-start | bytes 3145736 | tf_op jit(solution)/shard_map/ppermute | solution.py:221
  91.5 16.3 %collective-permute-start.6 = (bf16[8,4,32,512]{3,2,1,0:T(8,128)(2,1)}, bf16[8,4,32,512]{3,2,1,0:T(8,128)(2,1)}, u32[]{:S(2)}, u32[]{:S(2)}) collective-permute-start(bf16[8,4,32,512]{3,2,1,0:T(8,128)(2,1)} %constant_dynamic-update-slice_fusion.refs_0_), channel_id=1, source_target_pairs={{0,24},{1,25},{2,26},{3,27},{4,28},{5,29},{6,30},{7,31},{8,0},{9,1... | collective-permute-start | bytes 3145736 | tf_op jit(solution)/shard_map/ppermute | solution.py:221
  91.5 8.3 %collective-permute-start.10 = (bf16[2,4,32,512]{3,2,1,0:T(8,128)(2,1)S(1)}, bf16[2,4,32,512]{3,2,1,0:T(8,128)(2,1)S(1)}, u32[]{:S(2)}, u32[]{:S(2)}) collective-permute-start(bf16[2,4,32,512]{3,2,1,0:T(8,128)(2,1)S(1)} %pad_maximum_fusion.3.a_ref), channel_id=1, source_target_pairs={{0,64},{1,65},{2,66},{3,67},{4,68},{5,69},{6,70},{7,71},{8,72},{9,... | collective-permute-start | bytes 786440 | tf_op jit(solution)/shard_map/ppermute | solution.py:221
  100.6 8.4 %copy-start.6 = (f32[128]{0:T(128)S(1)}, f32[128]{0:T(128)}, u32[]{:S(2)}) copy-start(f32[128]{0:T(128)} %param.31) | copy-start | bytes 1540
  100.6 2.1 %collective-permute-start.11 = (bf16[4,4,32,512]{3,2,1,0:T(8,128)(2,1)}, bf16[4,4,32,512]{3,2,1,0:T(8,128)(2,1)S(1)}, u32[]{:S(2)}, u32[]{:S(2)}) collective-permute-start(bf16[4,4,32,512]{3,2,1,0:T(8,128)(2,1)} %shard_map.169), channel_id=1, source_target_pairs={{0,32},{1,33},{2,34},{3,35},{4,36},{5,37},{6,38},{7,39},{8,40},{9,... | collective-permute-start | bytes 1572872 | tf_op jit(solution)/shard_map/ppermute | solution.py:221
  104.8 11.8 %collective-permute-start.5 = (bf16[4,4,32,512]{3,2,1,0:T(8,128)(2,1)S(1)}, bf16[4,4,32,512]{3,2,1,0:T(8,128)(2,1)S(1)}, u32[]{:S(2)}, u32[]{:S(2)}) collective-permute-start(bf16[4,4,32,512]{3,2,1,0:T(8,128)(2,1)S(1)} %slice.18), channel_id=1, source_target_pairs={{0,8},{1,9},{2,10},{3,11},{4,12},{5,13},{6,14},{7,15},{8,16},{9,17... | collective-permute-start | bytes 1572872 | tf_op jit(solution)/shard_map/ppermute | solution.py:221
  108.9 10.5 %collective-permute-start.7 = (bf16[4,4,32,512]{3,2,1,0:T(8,128)(2,1)S(1)}, bf16[4,4,32,512]{3,2,1,0:T(8,128)(2,1)S(1)}, u32[]{:S(2)}, u32[]{:S(2)}) collective-permute-start(bf16[4,4,32,512]{3,2,1,0:T(8,128)(2,1)S(1)} %slice.19), channel_id=1, source_target_pairs={{0,24},{1,25},{2,26},{3,27},{4,28},{5,29},{6,30},{7,31},{8,0},{9,1... | collective-permute-start | bytes 1572872 | tf_op jit(solution)/shard_map/ppermute | solution.py:221

commit v4 on v3

--- a/solution.py
+++ b/solution.py
@@ -36,7 +36,6 @@
     @pl.when(pl.program_id(0) == 0)
     def _():
         ka_ref[...] = jnp.zeros_like(ka_ref)
-        va_ref[...] = jnp.zeros_like(va_ref)
         ones = jnp.broadcast_to(jnp.where(lane == 0, 1.0, 0.0).astype(BF16), (rows, 128))
         for g in range(2):
             qa_ref[g, :, 128:] = ones

time: 123 us -> 123 us (level)
  no operation moved by 1% of the time
where the time goes in v4:
time: 123 us; the launch traced here: 122 us
  waiting for transfers between devices  44.5 us (36%)
  starting transfers between devices  32.1 us (26%)
  Pallas kernels  28.4 us (23%)
  local copies, waits for them, and re-layouts  12.3 us (10%)
  other arithmetic  2.18 us (2%)
  matrix products  1.51 us (1%)
  between operations  1.43 us (1%)
    all_to_all x1, waiting for transfers between devices, body(): lax.all_to_all(moved, 'col', split_axis=0, concat_axis=0, tiled=True)  24.6 us
    ppermute x12, waiting for transfers between devices, permute_all(): return lax.ppermute(value, ('row', 'col'), pairs)  19.9 us
    ppermute x12, starting transfers between devices, permute_all(): return lax.ppermute(value, ('row', 'col'), pairs)  18.7 us
    pallas_call x1, Pallas kernels, attend(): pl.pallas_call(attend_kernel, grid=(count,), in_specs=[pl.BlockSpec((grou...  15.8 us
    all_to_all x1, starting transfers between devices, body(): lax.all_to_all(moved, 'col', split_axis=0, concat_axis=0, tiled=True)  13.5 us
    pallas_call x2, Pallas kernels, pair(): pl.pallas_call(functools.partial(pair_kernel, first, count, has_old), in_...  10.6 us
    unnamed x36, local copies, waits for them, and re-layouts  6.66 us
  transfers between devices with their start and end apart: 13, of which 6 were waited for; matrix products, arithmetic and copies ran while one was open for 11% of the time, Pallas kernels for 8%

profile of v4, /device:TPU:38, one launch (start us, length us, event | category | flops | bytes accessed | tf_op | source)
XLA Modules:
  0.0 122.5 jit_solution(2644549153181457935)
XLA Ops:
  0.6 2.8 %copy.25 = bf16[16,128,256]{2,0,1:T(8,128)(2,1)} copy(bf16[16,128,256]{2,1,0:T(8,128)(2,1)} %param.16) | data formatting | bytes 2097152 | tf_op args[0]
  3.4 0.0 copy-start.10
  3.4 0.0 copy-start.11
  3.4 0.0 copy-start.12
  3.5 13.5 %all-to-all-start = ((bf16[32,4,16,256]{3,2,1,0:T(8,128)(2,1)}), bf16[32,4,16,256]{3,2,1,0:T(8,128)(2,1)S(1)}, u32[]{:S(2)}, u32[]{:S(2)}) async-start(bf16[32,4,16,256]{3,2,1,0:T(8,128)(2,1)} %bitcast.1), calls=%async_computation | async-start | bytes 2097152 | tf_op jit(solution)/shard_map/all_to_all | solution.py:261
  16.9 0.0 copy-start.1
  16.9 0.0 copy-start.2
  17.0 0.0 copy-start.3
  17.0 0.0 copy-start.4
  17.0 0.0 copy-start.5
  17.3 0.1 stack.176.place_ref
  17.4 0.1 iota_add_fusion
  17.5 0.1 add.495
  17.6 0.8 dynamic_slice.19
  18.4 0.8 dynamic_slice.18
  19.2 1.1 dynamic-slice_convert_fusion.2
  20.2 0.1 copy.30
  20.4 0.0 copy-done.8
  20.4 0.1 copy.27
  20.5 0.1 stack.185.order_ref
  20.6 1.3 %fusion = f32[32,128]{1,0:T(8,128)S(1)} fusion(s32[512,1024]{1,0:T(8,128)} %param.17, s32[]{:T(128)S(6)} %select_n.389, s32[]{:T(128)S(6)} %select_n.390), kind=kOutput, calls=%fused_computation.1 | convolution fusion | flops 4284416 | bytes 540680 | tf_op jit(solution)/shard_map/dot_general | solution.py:279
  21.9 0.0 copy-done.13
  21.9 0.0 copy-done.14
  22.0 0.1 pad_maximum_fusion.wqkvg_ref
  22.1 0.1 compare_convert_fusion
  22.1 0.2 fusion.1
  22.3 24.6 %all-to-all-done.parts_ref = bf16[32,4,16,256]{3,2,1,0:T(8,128)(2,1)S(1)} async-done(((bf16[32,4,16,256]{3,2,1,0:T(8,128)(2,1)}), bf16[32,4,16,256]{3,2,1,0:T(8,128)(2,1)S(1)}, u32[]{:S(2)}, u32[]{:S(2)}) %all-to-all-start) | async-done | bytes 1048608 | tf_op jit(solution)/shard_map/all_to_all | solution.py:261
  46.9 15.8 %shard_map.167 = (bf16[4,512,256]{2,1,0:T(8,128)(2,1)S(1)}, bf16[4,32,512]{2,1,0:T(8,128)(2,1)S(1)}, bf16[4,32,512]{2,1,0:T(8,128)(2,1)S(1)}) custom-call(bf16[32,4,16,256]{3,2,1,0:T(8,128)(2,1)S(1)} %all-to-all-done.parts_ref, f32[4,1,512]{2,1,0:T(1,128)S(1)} %reshape.294.mask_ref, f32[1,256]{1,0:T(1,128)S(1)} %bitcast.68, ...), custom_call_target="tpu_custom_call" | custom-call | flops 16000000000 | bytes 4000000 | tf_op jit(solution)/shard_map/pallas_call | solution.py:88
  62.8 0.0 copy-start
  62.8 1.0 collective-permute-start
  63.8 1.9 %collective-permute-start.8 = (bf16[4,32,512]{2,1,0:T(8,128)(2,1)S(1)}, bf16[4,32,512]{2,1,0:T(8,128)(2,1)S(1)}, u32[]{:S(2)}, u32[]{:S(2)}) collective-permute-start(bf16[4,32,512]{2,1,0:T(8,128)(2,1)S(1)} %get-tuple-element.22.refs_0_), channel_id=1, source_target_pairs={{0,0},{1,64},{2,128},{3,192},{4,32},{5,96},{6,160},{7,224},{8,1},{... | collective-permute-start | bytes 393224 | tf_op jit(solution)/shard_map/ppermute | solution.py:220
  65.7 8.0 %collective-permute-done.refs_1_ = bf16[4,32,512]{2,1,0:T(8,128)(2,1)S(1)} collective-permute-done((bf16[4,32,512]{2,1,0:T(8,128)(2,1)S(1)}, bf16[4,32,512]{2,1,0:T(8,128)(2,1)S(1)}, u32[]{:S(2)}, u32[]{:S(2)}) %collective-permute-start) | collective-permute-done | bytes 131104 | tf_op jit(solution)/shard_map/ppermute | solution.py:220
  73.7 0.1 collective-permute-start.1
  73.8 0.7 constant_dynamic-update-slice_fusion.4
  74.5 3.2 %collective-permute-start.2 = (bf16[2,4,32,512]{3,2,1,0:T(8,128)(2,1)S(1)}, bf16[2,4,32,512]{3,2,1,0:T(8,128)(2,1)S(1)}, u32[]{:S(2)}, u32[]{:S(2)}) collective-permute-start(bf16[2,4,32,512]{3,2,1,0:T(8,128)(2,1)S(1)} %pad_maximum_fusion.2), channel_id=1, source_target_pairs={{0,3},{1,0},{2,1},{3,2},{4,7},{5,4},{6,5},{7,6},{8,11},{9,8},{10,9... | collective-permute-start | bytes 786440 | tf_op jit(solution)/shard_map/ppermute | solution.py:220
  77.7 0.0 collective-permute-start.3
  77.7 0.8 collective-permute-done.8
  78.6 4.9 %collective-permute-start.9 = (bf16[4,32,512]{2,1,0:T(8,128)(2,1)}, bf16[4,32,512]{2,1,0:T(8,128)(2,1)S(1)}, u32[]{:S(2)}, u32[]{:S(2)}) collective-permute-start(bf16[4,32,512]{2,1,0:T(8,128)(2,1)} %shard_map.168), channel_id=1, source_target_pairs={{0,128},{1,192},{2,0},{3,64},{4,160},{5,224},{6,32},{7,96},{8,129}... | collective-permute-start | bytes 393224 | tf_op jit(solution)/shard_map/ppermute | solution.py:220
  83.5 1.6 %constant_dynamic-update-slice_fusion.3 = bf16[8,4,32,512]{3,2,1,0:T(8,128)(2,1)} fusion(bf16[8,4,32,512]{3,2,1,0:T(8,128)(2,1)} %constant_dynamic-update-slice_fusion.4, bf16[4,32,512]{2,1,0:T(8,128)(2,1)} %copy-done.7), kind=kLoop, calls=%fused_computation.22 | loop fusion | bytes 262144
  85.0 0.0 collective-permute-done.1
  85.1 0.7 constant_dynamic-update-slice_fusion.2
  85.8 0.0 collective-permute-done.2
  85.8 0.7 constant_dynamic-update-slice_fusion.1
  86.5 0.0 collective-permute-done.3
  86.5 0.7 constant_dynamic-update-slice_fusion.refs_0_
  87.3 4.1 %collective-permute-start.4 = (bf16[8,4,32,512]{3,2,1,0:T(8,128)(2,1)}, bf16[8,4,32,512]{3,2,1,0:T(8,128)(2,1)S(1)}, u32[]{:S(2)}, u32[]{:S(2)}) collective-permute-start(bf16[8,4,32,512]{3,2,1,0:T(8,128)(2,1)} %constant_dynamic-update-slice_fusion.refs_0_), channel_id=1, source_target_pairs={{0,8},{1,9},{2,10},{3,11},{4,12},{5,13},{6,14},{7,15},{8,16},{9,17... | collective-permute-start | bytes 3145736 | tf_op jit(solution)/shard_map/ppermute | solution.py:220
  91.4 0.0 collective-permute-start.6
  91.4 0.0 collective-permute-done.9
  91.4 0.3 collective-permute-start.10
  91.7 1.8 %copy.32 = bf16[4,512,256]{2,0,1:T(4,128)(2,1)} copy(bf16[4,512,256]{2,1,0:T(8,128)(2,1)S(1)} %get-tuple-element.18) | data formatting | bytes 2097152 | tf_op jit(solution)/shard_map/pallas_call | solution.py:88
  93.5 6.2 %collective-permute-done.10.b_ref = bf16[2,4,32,512]{3,2,1,0:T(8,128)(2,1)S(1)} collective-permute-done((bf16[2,4,32,512]{3,2,1,0:T(8,128)(2,1)S(1)}, bf16[2,4,32,512]{3,2,1,0:T(8,128)(2,1)S(1)}, u32[]{:S(2)}, u32[]{:S(2)}) %collective-permute-start.10) | collective-permute-done | bytes 262176 | tf_op jit(solution)/shard_map/ppermute | solution.py:220
  99.6 0.8 pad_maximum_fusion.1.refs_0_
  100.5 0.0 collective-permute-start.11
  100.5 2.1 %collective-permute-done.11.c_ref = bf16[4,4,32,512]{3,2,1,0:T(8,128)(2,1)S(1)} collective-permute-done((bf16[4,4,32,512]{3,2,1,0:T(8,128)(2,1)}, bf16[4,4,32,512]{3,2,1,0:T(8,128)(2,1)S(1)}, u32[]{:S(2)}, u32[]{:S(2)}) %collective-permute-start.11) | collective-permute-done | bytes 524320 | tf_op jit(solution)/shard_map/ppermute | solution.py:220
  102.6 2.0 %shard_map.170.refs_3_.refs_2_ = bf16[512,1024]{1,0:T(8,128)(2,1)S(1)} custom-call(s32[8]{0:T(128)S(1)} %stack.185.order_ref, bf16[2,4,32,512]{3,2,1,0:T(8,128)(2,1)S(1)} %pad_maximum_fusion.3.a_ref, bf16[2,4,32,512]{3,2,1,0:T(8,128)(2,1)S(1)} %collective-permute-done.10.b_ref, bf16[4,4,32,512]{3,2,1,0:T(8,128)(2,1)S(1)} %collective-permute-done.11.c_ref), custom_call_target="tpu_custom_call" | custom-call | flops 1000000 | bytes 4000000 | tf_op jit(solution)/shard_map/pallas_call | solution.py:136
  104.6 0.0 collective-permute-done.4.refs_1_
  104.6 3.1 %collective-permute-start.5 = (bf16[4,4,32,512]{3,2,1,0:T(8,128)(2,1)S(1)}, bf16[4,4,32,512]{3,2,1,0:T(8,128)(2,1)S(1)}, u32[]{:S(2)}, u32[]{:S(2)}) collective-permute-start(bf16[4,4,32,512]{3,2,1,0:T(8,128)(2,1)S(1)} %slice.18), channel_id=1, source_target_pairs={{0,8},{1,9},{2,10},{3,11},{4,12},{5,13},{6,14},{7,15},{8,16},{9,17... | collective-permute-start | bytes 1572872 | tf_op jit(solution)/shard_map/ppermute | solution.py:220
  107.7 0.0 collective-permute-done.6.refs_2_
  107.7 1.1 slice.19
  108.8 0.1 collective-permute-start.7
  108.9 7.5 %shard_map.171.refs_7_ = bf16[32,4,32,128]{3,2,1,0:T(8,128)(2,1)} custom-call(s32[32]{0:T(128)S(1)} %stack.176.place_ref, bf16[8,4,32,512]{3,2,1,0:T(8,128)(2,1)} %constant_dynamic-update-slice_fusion.refs_0_, bf16[8,4,32,512]{3,2,1,0:T(8,128)(2,1)S(1)} %collective-permute-done.4.refs_1_, bf16[8,4,32,512]{3,2,1,0:T(8,128)(2,1)} %collective-permute-done.6.refs_2_, ...), custom_call_target="tpu_custom_call" | custom-call | flops 6000000000 | bytes 9600000 | tf_op jit(solution)/shard_map/pallas_call | solution.py:194
  116.4 0.0 collective-permute-done.5.refs_0_
  116.4 2.8 %collective-permute-done.7.refs_1_ = bf16[4,4,32,512]{3,2,1,0:T(8,128)(2,1)S(1)} collective-permute-done((bf16[4,4,32,512]{3,2,1,0:T(8,128)(2,1)S(1)}, bf16[4,4,32,512]{3,2,1,0:T(8,128)(2,1)S(1)}, u32[]{:S(2)}, u32[]{:S(2)}) %collective-permute-start.7) | collective-permute-done | bytes 524320 | tf_op jit(solution)/shard_map/ppermute | solution.py:220
  119.3 3.1 %shard_map.172 = bf16[32,4,32,128]{3,2,1,0:T(8,128)(2,1)} custom-call(s32[32]{0:T(128)S(1)} %stack.176.place_ref, bf16[4,4,32,512]{3,2,1,0:T(8,128)(2,1)S(1)} %collective-permute-done.5.refs_0_, bf16[4,4,32,512]{3,2,1,0:T(8,128)(2,1)S(1)} %collective-permute-done.7.refs_1_, ...), custom_call_target="tpu_custom_call", output_to_operand_aliasing={{}: (8, {})} | custom-call | flops 2000000000 | bytes 3200000 | tf_op jit(solution)/shard_map/pallas_call | solution.py:194
  (27 shorter events, 0.1 us)
Async XLA Ops:
  3.4 17.0 %copy-start.8 = (bf16[1024,128]{1,0:T(8,128)(2,1)S(1)}, bf16[1024,128]{1,0:T(8,128)(2,1)}, u32[]{:S(2)}) copy-start(bf16[1024,128]{1,0:T(8,128)(2,1)} %param.30) | copy-start | bytes 786436
  3.4 18.5 %copy-start.13 = (bf16[256,32]{0,1:T(8,128)(2,1)S(1)}, bf16[256,32]{0,1:T(8,128)(2,1)}, u32[]{:S(2)}) copy-start(bf16[256,32]{0,1:T(8,128)(2,1)} %param.29) | copy-start | bytes 49156
  3.4 18.5 %copy-start.14 = (bf16[256,32]{0,1:T(8,128)(2,1)S(1)}, bf16[256,32]{0,1:T(8,128)(2,1)}, u32[]{:S(2)}) copy-start(bf16[256,32]{0,1:T(8,128)(2,1)} %param.28) | copy-start | bytes 49156
  3.4 18.5 %copy-start.9 = (bf16[256,256]{1,0:T(8,128)(2,1)S(1)}, bf16[256,256]{1,0:T(8,128)(2,1)}, u32[]{:S(2)}) copy-start(bf16[256,256]{1,0:T(8,128)(2,1)} %param.23) | copy-start | bytes 393220
  3.4 18.5 %copy-start.10 = (bf16[256,256]{1,0:T(8,128)(2,1)S(1)}, bf16[256,256]{1,0:T(8,128)(2,1)}, u32[]{:S(2)}) copy-start(bf16[256,256]{1,0:T(8,128)(2,1)} %param.22) | copy-start | bytes 393220
  3.4 18.5 %copy-start.11 = (bf16[256,256]{1,0:T(8,128)(2,1)S(1)}, bf16[256,256]{1,0:T(8,128)(2,1)}, u32[]{:S(2)}) copy-start(bf16[256,256]{1,0:T(8,128)(2,1)} %param.21) | copy-start | bytes 393220
  3.4 18.5 %copy-start.12 = (bf16[256,256]{1,0:T(8,128)(2,1)S(1)}, bf16[256,256]{1,0:T(8,128)(2,1)}, u32[]{:S(2)}) copy-start(bf16[256,256]{1,0:T(8,128)(2,1)} %param.20) | copy-start | bytes 393220
  3.5 43.5 %all-to-all-start = ((bf16[32,4,16,256]{3,2,1,0:T(8,128)(2,1)}), bf16[32,4,16,256]{3,2,1,0:T(8,128)(2,1)S(1)}, u32[]{:S(2)}, u32[]{:S(2)}) async-start(bf16[32,4,16,256]{3,2,1,0:T(8,128)(2,1)} %bitcast.1), calls=%async_computation | async-start | bytes 2097152 | tf_op jit(solution)/shard_map/all_to_all | solution.py:261
  16.9 30.0 %copy-start.1 = (bf16[256,256]{1,0:T(8,128)(2,1)S(1)}, bf16[256,256]{1,0:T(8,128)(2,1)}, u32[]{:S(2)}) copy-start(bf16[256,256]{1,0:T(8,128)(2,1)} %wo_ref.1) | copy-start | bytes 393220
  16.9 30.0 %copy-start.2 = (f32[256]{0:T(256)S(1)}, f32[256]{0:T(256)}, u32[]{:S(2)}) copy-start(f32[256]{0:T(256)} %param.19) | copy-start | bytes 3076
  17.0 30.0 %copy-start.3 = (f32[256]{0:T(256)S(1)}, f32[256]{0:T(256)}, u32[]{:S(2)}) copy-start(f32[256]{0:T(256)} %param.24) | copy-start | bytes 3076
  17.0 30.0 %copy-start.4 = (f32[256]{0:T(256)S(1)}, f32[256]{0:T(256)}, u32[]{:S(2)}) copy-start(f32[256]{0:T(256)} %param.26) | copy-start | bytes 3076
  17.0 30.0 %copy-start.5 = (f32[256]{0:T(256)S(1)}, f32[256]{0:T(256)}, u32[]{:S(2)}) copy-start(f32[256]{0:T(256)} %param.27) | copy-start | bytes 3076
  62.8 15.8 %copy-start = (bf16[4,32,512]{2,1,0:T(8,128)(2,1)}, bf16[4,32,512]{2,1,0:T(8,128)(2,1)S(1)}, u32[]{:S(2)}) copy-start(bf16[4,32,512]{2,1,0:T(8,128)(2,1)S(1)} %get-tuple-element.22.refs_0_) | copy-start | bytes 393220
  62.8 10.9 %collective-permute-start = (bf16[4,32,512]{2,1,0:T(8,128)(2,1)S(1)}, bf16[4,32,512]{2,1,0:T(8,128)(2,1)S(1)}, u32[]{:S(2)}, u32[]{:S(2)}) collective-permute-start(bf16[4,32,512]{2,1,0:T(8,128)(2,1)S(1)} %get-tuple-element.20), channel_id=1, source_target_pairs={{0,4},{1,5},{2,6},{3,7},{4,0},{5,1},{6,2},{7,3},{8,12},{9,13},{10,... | collective-permute-start | bytes 393224 | tf_op jit(solution)/shard_map/ppermute | solution.py:220
  63.8 14.7 %collective-permute-start.8 = (bf16[4,32,512]{2,1,0:T(8,128)(2,1)S(1)}, bf16[4,32,512]{2,1,0:T(8,128)(2,1)S(1)}, u32[]{:S(2)}, u32[]{:S(2)}) collective-permute-start(bf16[4,32,512]{2,1,0:T(8,128)(2,1)S(1)} %get-tuple-element.22.refs_0_), channel_id=1, source_target_pairs={{0,0},{1,64},{2,128},{3,192},{4,32},{5,96},{6,160},{7,224},{8,1},{... | collective-permute-start | bytes 393224 | tf_op jit(solution)/shard_map/ppermute | solution.py:220
  73.7 4.9 %copy-start.7 = (bf16[4,32,512]{2,1,0:T(8,128)(2,1)}, bf16[4,32,512]{2,1,0:T(8,128)(2,1)S(1)}, u32[]{:S(2)}) copy-start(bf16[4,32,512]{2,1,0:T(8,128)(2,1)S(1)} %collective-permute-done.refs_1_) | copy-start | bytes 393220
  73.7 11.3 %collective-permute-start.1 = (bf16[2,4,32,512]{3,2,1,0:T(8,128)(2,1)S(1)}, bf16[2,4,32,512]{3,2,1,0:T(8,128)(2,1)S(1)}, u32[]{:S(2)}, u32[]{:S(2)}) collective-permute-start(bf16[2,4,32,512]{3,2,1,0:T(8,128)(2,1)S(1)} %pad_maximum_fusion.2), channel_id=1, source_target_pairs={{0,1},{1,2},{2,3},{3,0},{4,5},{5,6},{6,7},{7,4},{8,9},{9,10},{10,1... | collective-permute-start | bytes 786440 | tf_op jit(solution)/shard_map/ppermute | solution.py:220
  74.5 11.3 %collective-permute-start.2 = (bf16[2,4,32,512]{3,2,1,0:T(8,128)(2,1)S(1)}, bf16[2,4,32,512]{3,2,1,0:T(8,128)(2,1)S(1)}, u32[]{:S(2)}, u32[]{:S(2)}) collective-permute-start(bf16[2,4,32,512]{3,2,1,0:T(8,128)(2,1)S(1)} %pad_maximum_fusion.2), channel_id=1, source_target_pairs={{0,3},{1,0},{2,1},{3,2},{4,7},{5,4},{6,5},{7,6},{8,11},{9,8},{10,9... | collective-permute-start | bytes 786440 | tf_op jit(solution)/shard_map/ppermute | solution.py:220
  77.7 8.8 %collective-permute-start.3 = (bf16[2,4,32,512]{3,2,1,0:T(8,128)(2,1)S(1)}, bf16[2,4,32,512]{3,2,1,0:T(8,128)(2,1)S(1)}, u32[]{:S(2)}, u32[]{:S(2)}) collective-permute-start(bf16[2,4,32,512]{3,2,1,0:T(8,128)(2,1)S(1)} %pad_maximum_fusion.2), channel_id=1, source_target_pairs={{0,2},{1,3},{2,0},{3,1},{4,6},{5,7},{6,4},{7,5},{8,10},{9,11},{10,... | collective-permute-start | bytes 786440 | tf_op jit(solution)/shard_map/ppermute | solution.py:220
  78.6 12.8 %collective-permute-start.9 = (bf16[4,32,512]{2,1,0:T(8,128)(2,1)}, bf16[4,32,512]{2,1,0:T(8,128)(2,1)S(1)}, u32[]{:S(2)}, u32[]{:S(2)}) collective-permute-start(bf16[4,32,512]{2,1,0:T(8,128)(2,1)} %shard_map.168), channel_id=1, source_target_pairs={{0,128},{1,192},{2,0},{3,64},{4,160},{5,224},{6,32},{7,96},{8,129}... | collective-permute-start | bytes 393224 | tf_op jit(solution)/shard_map/ppermute | solution.py:220
  87.3 17.3 %collective-permute-start.4 = (bf16[8,4,32,512]{3,2,1,0:T(8,128)(2,1)}, bf16[8,4,32,512]{3,2,1,0:T(8,128)(2,1)S(1)}, u32[]{:S(2)}, u32[]{:S(2)}) collective-permute-start(bf16[8,4,32,512]{3,2,1,0:T(8,128)(2,1)} %constant_dynamic-update-slice_fusion.refs_0_), channel_id=1, source_target_pairs={{0,8},{1,9},{2,10},{3,11},{4,12},{5,13},{6,14},{7,15},{8,16},{9,17... | collective-permute-start | bytes 3145736 | tf_op jit(solution)/shard_map/ppermute | solution.py:220
  91.4 16.3 %collective-permute-start.6 = (bf16[8,4,32,512]{3,2,1,0:T(8,128)(2,1)}, bf16[8,4,32,512]{3,2,1,0:T(8,128)(2,1)}, u32[]{:S(2)}, u32[]{:S(2)}) collective-permute-start(bf16[8,4,32,512]{3,2,1,0:T(8,128)(2,1)} %constant_dynamic-update-slice_fusion.refs_0_), channel_id=1, source_target_pairs={{0,24},{1,25},{2,26},{3,27},{4,28},{5,29},{6,30},{7,31},{8,0},{9,1... | collective-permute-start | bytes 3145736 | tf_op jit(solution)/shard_map/ppermute | solution.py:220
  91.4 8.3 %collective-permute-start.10 = (bf16[2,4,32,512]{3,2,1,0:T(8,128)(2,1)S(1)}, bf16[2,4,32,512]{3,2,1,0:T(8,128)(2,1)S(1)}, u32[]{:S(2)}, u32[]{:S(2)}) collective-permute-start(bf16[2,4,32,512]{3,2,1,0:T(8,128)(2,1)S(1)} %pad_maximum_fusion.3.a_ref), channel_id=1, source_target_pairs={{0,64},{1,65},{2,66},{3,67},{4,68},{5,69},{6,70},{7,71},{8,72},{9,... | collective-permute-start | bytes 786440 | tf_op jit(solution)/shard_map/ppermute | solution.py:220
  100.5 8.4 %copy-start.6 = (f32[128]{0:T(128)S(1)}, f32[128]{0:T(128)}, u32[]{:S(2)}) copy-start(f32[128]{0:T(128)} %param.31) | copy-start | bytes 1540
  100.5 2.1 %collective-permute-start.11 = (bf16[4,4,32,512]{3,2,1,0:T(8,128)(2,1)}, bf16[4,4,32,512]{3,2,1,0:T(8,128)(2,1)S(1)}, u32[]{:S(2)}, u32[]{:S(2)}) collective-permute-start(bf16[4,4,32,512]{3,2,1,0:T(8,128)(2,1)} %shard_map.169), channel_id=1, source_target_pairs={{0,32},{1,33},{2,34},{3,35},{4,36},{5,37},{6,38},{7,39},{8,40},{9,... | collective-permute-start | bytes 1572872 | tf_op jit(solution)/shard_map/ppermute | solution.py:220
  104.6 11.8 %collective-permute-start.5 = (bf16[4,4,32,512]{3,2,1,0:T(8,128)(2,1)S(1)}, bf16[4,4,32,512]{3,2,1,0:T(8,128)(2,1)S(1)}, u32[]{:S(2)}, u32[]{:S(2)}) collective-permute-start(bf16[4,4,32,512]{3,2,1,0:T(8,128)(2,1)S(1)} %slice.18), channel_id=1, source_target_pairs={{0,8},{1,9},{2,10},{3,11},{4,12},{5,13},{6,14},{7,15},{8,16},{9,17... | collective-permute-start | bytes 1572872 | tf_op jit(solution)/shard_map/ppermute | solution.py:220
  108.8 10.5 %collective-permute-start.7 = (bf16[4,4,32,512]{3,2,1,0:T(8,128)(2,1)S(1)}, bf16[4,4,32,512]{3,2,1,0:T(8,128)(2,1)S(1)}, u32[]{:S(2)}, u32[]{:S(2)}) collective-permute-start(bf16[4,4,32,512]{3,2,1,0:T(8,128)(2,1)S(1)} %slice.19), channel_id=1, source_target_pairs={{0,24},{1,25},{2,26},{3,27},{4,28},{5,29},{6,30},{7,31},{8,0},{9,1... | collective-permute-start | bytes 1572872 | tf_op jit(solution)/shard_map/ppermute | solution.py:220

commit v5 on v4

--- a/solution.py
+++ b/solution.py
@@ -11,7 +11,7 @@
 
 HEAD_FEATURES = 32
 F32, BF16 = jnp.float32, jnp.bfloat16
-SB = 256
+SB = 128
 VMEM_LIMIT = 40 * 1024 * 1024
 
 def norm_rows(x, gain):

time: 123 us -> 123 us (level)
  no operation moved by 1% of the time
where the time goes in v5:
time: 123 us; the launch traced here: 122 us
  waiting for transfers between devices  44.6 us (36%)
  starting transfers between devices  32.1 us (26%)
  Pallas kernels  28.3 us (23%)
  local copies, waits for them, and re-layouts  12.3 us (10%)
  other arithmetic  2.18 us (2%)
  matrix products  1.51 us (1%)
  between operations  1.43 us (1%)
    all_to_all x1, waiting for transfers between devices, body(): lax.all_to_all(moved, 'col', split_axis=0, concat_axis=0, tiled=True)  24.6 us
    ppermute x12, waiting for transfers between devices, permute_all(): return lax.ppermute(value, ('row', 'col'), pairs)  20 us
    ppermute x12, starting transfers between devices, permute_all(): return lax.ppermute(value, ('row', 'col'), pairs)  18.6 us
    pallas_call x1, Pallas kernels, attend(): pl.pallas_call(attend_kernel, grid=(count,), in_specs=[pl.BlockSpec((grou...  15.8 us
    all_to_all x1, starting transfers between devices, body(): lax.all_to_all(moved, 'col', split_axis=0, concat_axis=0, tiled=True)  13.5 us
    pallas_call x2, Pallas kernels, pair(): pl.pallas_call(functools.partial(pair_kernel, first, count, has_old), in_...  10.6 us
    unnamed x36, local copies, waits for them, and re-layouts  6.66 us
  transfers between devices with their start and end apart: 13, of which 6 were waited for; matrix products, arithmetic and copies ran while one was open for 11% of the time, Pallas kernels for 8%

profile of v5, /device:TPU:38, one launch (start us, length us, event | category | flops | bytes accessed | tf_op | source)
XLA Modules:
  0.0 122.4 jit_solution(18247677777367270196)
XLA Ops:
  0.6 2.8 %copy.25 = bf16[16,128,256]{2,0,1:T(8,128)(2,1)} copy(bf16[16,128,256]{2,1,0:T(8,128)(2,1)} %param.16) | data formatting | bytes 2097152 | tf_op args[0]
  3.4 0.0 copy-start.10
  3.4 0.0 copy-start.11
  3.4 0.0 copy-start.12
  3.5 13.5 %all-to-all-start = ((bf16[32,4,16,256]{3,2,1,0:T(8,128)(2,1)}), bf16[32,4,16,256]{3,2,1,0:T(8,128)(2,1)S(1)}, u32[]{:S(2)}, u32[]{:S(2)}) async-start(bf16[32,4,16,256]{3,2,1,0:T(8,128)(2,1)} %bitcast.1), calls=%async_computation | async-start | bytes 2097152 | tf_op jit(solution)/shard_map/all_to_all | solution.py:261
  16.9 0.0 copy-start.1
  16.9 0.0 copy-start.2
  17.0 0.0 copy-start.3
  17.0 0.0 copy-start.4
  17.0 0.0 copy-start.5
  17.3 0.1 stack.176.place_ref
  17.4 0.1 iota_add_fusion
  17.5 0.1 add.495
  17.6 0.8 dynamic_slice.19
  18.4 0.8 dynamic_slice.18
  19.2 1.1 dynamic-slice_convert_fusion.2
  20.2 0.1 copy.30
  20.4 0.0 copy-done.8
  20.4 0.1 copy.27
  20.5 0.1 stack.185.order_ref
  20.6 1.3 %fusion = f32[32,128]{1,0:T(8,128)S(1)} fusion(s32[512,1024]{1,0:T(8,128)} %param.17, s32[]{:T(128)S(6)} %select_n.389, s32[]{:T(128)S(6)} %select_n.390), kind=kOutput, calls=%fused_computation.1 | convolution fusion | flops 4284416 | bytes 540680 | tf_op jit(solution)/shard_map/dot_general | solution.py:279
  21.9 0.0 copy-done.13
  22.0 0.1 pad_maximum_fusion.wqkvg_ref
  22.1 0.1 compare_convert_fusion
  22.1 0.2 fusion.1
  22.3 24.6 %all-to-all-done.parts_ref = bf16[32,4,16,256]{3,2,1,0:T(8,128)(2,1)S(1)} async-done(((bf16[32,4,16,256]{3,2,1,0:T(8,128)(2,1)}), bf16[32,4,16,256]{3,2,1,0:T(8,128)(2,1)S(1)}, u32[]{:S(2)}, u32[]{:S(2)}) %all-to-all-start) | async-done | bytes 1048608 | tf_op jit(solution)/shard_map/all_to_all | solution.py:261
  46.9 15.8 %shard_map.167 = (bf16[4,512,256]{2,1,0:T(8,128)(2,1)S(1)}, bf16[4,32,512]{2,1,0:T(8,128)(2,1)S(1)}, bf16[4,32,512]{2,1,0:T(8,128)(2,1)S(1)}) custom-call(bf16[32,4,16,256]{3,2,1,0:T(8,128)(2,1)S(1)} %all-to-all-done.parts_ref, f32[4,1,512]{2,1,0:T(1,128)S(1)} %reshape.294.mask_ref, f32[1,256]{1,0:T(1,128)S(1)} %bitcast.68, ...), custom_call_target="tpu_custom_call" | custom-call | flops 16000000000 | bytes 4000000 | tf_op jit(solution)/shard_map/pallas_call | solution.py:88
  62.7 0.0 copy-start
  62.8 1.0 collective-permute-start
  63.8 1.9 %collective-permute-start.8 = (bf16[4,32,512]{2,1,0:T(8,128)(2,1)S(1)}, bf16[4,32,512]{2,1,0:T(8,128)(2,1)S(1)}, u32[]{:S(2)}, u32[]{:S(2)}) collective-permute-start(bf16[4,32,512]{2,1,0:T(8,128)(2,1)S(1)} %get-tuple-element.22.refs_0_), channel_id=1, source_target_pairs={{0,0},{1,64},{2,128},{3,192},{4,32},{5,96},{6,160},{7,224},{8,1},{... | collective-permute-start | bytes 393224 | tf_op jit(solution)/shard_map/ppermute | solution.py:220
  65.7 8.0 %collective-permute-done.refs_1_ = bf16[4,32,512]{2,1,0:T(8,128)(2,1)S(1)} collective-permute-done((bf16[4,32,512]{2,1,0:T(8,128)(2,1)S(1)}, bf16[4,32,512]{2,1,0:T(8,128)(2,1)S(1)}, u32[]{:S(2)}, u32[]{:S(2)}) %collective-permute-start) | collective-permute-done | bytes 131104 | tf_op jit(solution)/shard_map/ppermute | solution.py:220
  73.7 0.1 collective-permute-start.1
  73.8 0.7 constant_dynamic-update-slice_fusion.4
  74.4 3.2 %collective-permute-start.2 = (bf16[2,4,32,512]{3,2,1,0:T(8,128)(2,1)S(1)}, bf16[2,4,32,512]{3,2,1,0:T(8,128)(2,1)S(1)}, u32[]{:S(2)}, u32[]{:S(2)}) collective-permute-start(bf16[2,4,32,512]{3,2,1,0:T(8,128)(2,1)S(1)} %pad_maximum_fusion.2), channel_id=1, source_target_pairs={{0,3},{1,0},{2,1},{3,2},{4,7},{5,4},{6,5},{7,6},{8,11},{9,8},{10,9... | collective-permute-start | bytes 786440 | tf_op jit(solution)/shard_map/ppermute | solution.py:220
  77.7 0.0 collective-permute-start.3
  77.7 0.9 collective-permute-done.8
  78.5 0.0 copy-done.7
  78.5 4.9 %collective-permute-start.9 = (bf16[4,32,512]{2,1,0:T(8,128)(2,1)}, bf16[4,32,512]{2,1,0:T(8,128)(2,1)S(1)}, u32[]{:S(2)}, u32[]{:S(2)}) collective-permute-start(bf16[4,32,512]{2,1,0:T(8,128)(2,1)} %shard_map.168), channel_id=1, source_target_pairs={{0,128},{1,192},{2,0},{3,64},{4,160},{5,224},{6,32},{7,96},{8,129}... | collective-permute-start | bytes 393224 | tf_op jit(solution)/shard_map/ppermute | solution.py:220
  83.5 1.6 %constant_dynamic-update-slice_fusion.3 = bf16[8,4,32,512]{3,2,1,0:T(8,128)(2,1)} fusion(bf16[8,4,32,512]{3,2,1,0:T(8,128)(2,1)} %constant_dynamic-update-slice_fusion.4, bf16[4,32,512]{2,1,0:T(8,128)(2,1)} %copy-done.7), kind=kLoop, calls=%fused_computation.22 | loop fusion | bytes 262144
  85.0 0.0 collective-permute-done.1
  85.0 0.7 constant_dynamic-update-slice_fusion.2
  85.8 0.0 collective-permute-done.2
  85.8 0.7 constant_dynamic-update-slice_fusion.1
  86.5 0.0 collective-permute-done.3
  86.5 0.7 constant_dynamic-update-slice_fusion.refs_0_
  87.2 4.1 %collective-permute-start.4 = (bf16[8,4,32,512]{3,2,1,0:T(8,128)(2,1)}, bf16[8,4,32,512]{3,2,1,0:T(8,128)(2,1)S(1)}, u32[]{:S(2)}, u32[]{:S(2)}) collective-permute-start(bf16[8,4,32,512]{3,2,1,0:T(8,128)(2,1)} %constant_dynamic-update-slice_fusion.refs_0_), channel_id=1, source_target_pairs={{0,8},{1,9},{2,10},{3,11},{4,12},{5,13},{6,14},{7,15},{8,16},{9,17... | collective-permute-start | bytes 3145736 | tf_op jit(solution)/shard_map/ppermute | solution.py:220
  91.3 0.0 collective-permute-start.6
  91.3 0.0 collective-permute-done.9
  91.3 0.3 collective-permute-start.10
  91.6 1.8 %copy.32 = bf16[4,512,256]{2,0,1:T(4,128)(2,1)} copy(bf16[4,512,256]{2,1,0:T(8,128)(2,1)S(1)} %get-tuple-element.18) | data formatting | bytes 2097152 | tf_op jit(solution)/shard_map/pallas_call | solution.py:88
  93.4 6.2 %collective-permute-done.10.b_ref = bf16[2,4,32,512]{3,2,1,0:T(8,128)(2,1)S(1)} collective-permute-done((bf16[2,4,32,512]{3,2,1,0:T(8,128)(2,1)S(1)}, bf16[2,4,32,512]{3,2,1,0:T(8,128)(2,1)S(1)}, u32[]{:S(2)}, u32[]{:S(2)}) %collective-permute-start.10) | collective-permute-done | bytes 262176 | tf_op jit(solution)/shard_map/ppermute | solution.py:220
  99.6 0.8 pad_maximum_fusion.1.refs_0_
  100.5 0.0 collective-permute-start.11
  100.5 2.1 %collective-permute-done.11.c_ref = bf16[4,4,32,512]{3,2,1,0:T(8,128)(2,1)S(1)} collective-permute-done((bf16[4,4,32,512]{3,2,1,0:T(8,128)(2,1)}, bf16[4,4,32,512]{3,2,1,0:T(8,128)(2,1)S(1)}, u32[]{:S(2)}, u32[]{:S(2)}) %collective-permute-start.11) | collective-permute-done | bytes 524320 | tf_op jit(solution)/shard_map/ppermute | solution.py:220
  102.6 2.0 %shard_map.170.refs_3_.refs_2_ = bf16[512,1024]{1,0:T(8,128)(2,1)S(1)} custom-call(s32[8]{0:T(128)S(1)} %stack.185.order_ref, bf16[2,4,32,512]{3,2,1,0:T(8,128)(2,1)S(1)} %pad_maximum_fusion.3.a_ref, bf16[2,4,32,512]{3,2,1,0:T(8,128)(2,1)S(1)} %collective-permute-done.10.b_ref, bf16[4,4,32,512]{3,2,1,0:T(8,128)(2,1)S(1)} %collective-permute-done.11.c_ref), custom_call_target="tpu_custom_call" | custom-call | flops 1000000 | bytes 4000000 | tf_op jit(solution)/shard_map/pallas_call | solution.py:136
  104.5 0.0 collective-permute-done.4.refs_1_
  104.6 3.1 %collective-permute-start.5 = (bf16[4,4,32,512]{3,2,1,0:T(8,128)(2,1)S(1)}, bf16[4,4,32,512]{3,2,1,0:T(8,128)(2,1)S(1)}, u32[]{:S(2)}, u32[]{:S(2)}) collective-permute-start(bf16[4,4,32,512]{3,2,1,0:T(8,128)(2,1)S(1)} %slice.18), channel_id=1, source_target_pairs={{0,8},{1,9},{2,10},{3,11},{4,12},{5,13},{6,14},{7,15},{8,16},{9,17... | collective-permute-start | bytes 1572872 | tf_op jit(solution)/shard_map/ppermute | solution.py:220
  107.6 0.0 collective-permute-done.6.refs_2_
  107.7 1.1 slice.19
  108.7 0.1 collective-permute-start.7
  108.8 7.5 %shard_map.171.refs_7_ = bf16[32,4,32,128]{3,2,1,0:T(8,128)(2,1)} custom-call(s32[32]{0:T(128)S(1)} %stack.176.place_ref, bf16[8,4,32,512]{3,2,1,0:T(8,128)(2,1)} %constant_dynamic-update-slice_fusion.refs_0_, bf16[8,4,32,512]{3,2,1,0:T(8,128)(2,1)S(1)} %collective-permute-done.4.refs_1_, bf16[8,4,32,512]{3,2,1,0:T(8,128)(2,1)} %collective-permute-done.6.refs_2_, ...), custom_call_target="tpu_custom_call" | custom-call | flops 6000000000 | bytes 9600000 | tf_op jit(solution)/shard_map/pallas_call | solution.py:194
  116.4 0.0 collective-permute-done.5.refs_0_
  116.4 2.8 %collective-permute-done.7.refs_1_ = bf16[4,4,32,512]{3,2,1,0:T(8,128)(2,1)S(1)} collective-permute-done((bf16[4,4,32,512]{3,2,1,0:T(8,128)(2,1)S(1)}, bf16[4,4,32,512]{3,2,1,0:T(8,128)(2,1)S(1)}, u32[]{:S(2)}, u32[]{:S(2)}) %collective-permute-start.7) | collective-permute-done | bytes 524320 | tf_op jit(solution)/shard_map/ppermute | solution.py:220
  119.2 3.1 %shard_map.172 = bf16[32,4,32,128]{3,2,1,0:T(8,128)(2,1)} custom-call(s32[32]{0:T(128)S(1)} %stack.176.place_ref, bf16[4,4,32,512]{3,2,1,0:T(8,128)(2,1)S(1)} %collective-permute-done.5.refs_0_, bf16[4,4,32,512]{3,2,1,0:T(8,128)(2,1)S(1)} %collective-permute-done.7.refs_1_, ...), custom_call_target="tpu_custom_call", output_to_operand_aliasing={{}: (8, {})} | custom-call | flops 2000000000 | bytes 3200000 | tf_op jit(solution)/shard_map/pallas_call | solution.py:194
  (27 shorter events, 0.1 us)
Async XLA Ops:
  3.4 17.0 %copy-start.8 = (bf16[1024,128]{1,0:T(8,128)(2,1)S(1)}, bf16[1024,128]{1,0:T(8,128)(2,1)}, u32[]{:S(2)}) copy-start(bf16[1024,128]{1,0:T(8,128)(2,1)} %param.30) | copy-start | bytes 786436
  3.4 18.5 %copy-start.13 = (bf16[256,32]{0,1:T(8,128)(2,1)S(1)}, bf16[256,32]{0,1:T(8,128)(2,1)}, u32[]{:S(2)}) copy-start(bf16[256,32]{0,1:T(8,128)(2,1)} %param.29) | copy-start | bytes 49156
  3.4 18.5 %copy-start.14 = (bf16[256,32]{0,1:T(8,128)(2,1)S(1)}, bf16[256,32]{0,1:T(8,128)(2,1)}, u32[]{:S(2)}) copy-start(bf16[256,32]{0,1:T(8,128)(2,1)} %param.28) | copy-start | bytes 49156
  3.4 18.5 %copy-start.9 = (bf16[256,256]{1,0:T(8,128)(2,1)S(1)}, bf16[256,256]{1,0:T(8,128)(2,1)}, u32[]{:S(2)}) copy-start(bf16[256,256]{1,0:T(8,128)(2,1)} %param.23) | copy-start | bytes 393220
  3.4 18.5 %copy-start.10 = (bf16[256,256]{1,0:T(8,128)(2,1)S(1)}, bf16[256,256]{1,0:T(8,128)(2,1)}, u32[]{:S(2)}) copy-start(bf16[256,256]{1,0:T(8,128)(2,1)} %param.22) | copy-start | bytes 393220
  3.4 18.5 %copy-start.11 = (bf16[256,256]{1,0:T(8,128)(2,1)S(1)}, bf16[256,256]{1,0:T(8,128)(2,1)}, u32[]{:S(2)}) copy-start(bf16[256,256]{1,0:T(8,128)(2,1)} %param.21) | copy-start | bytes 393220
  3.4 18.5 %copy-start.12 = (bf16[256,256]{1,0:T(8,128)(2,1)S(1)}, bf16[256,256]{1,0:T(8,128)(2,1)}, u32[]{:S(2)}) copy-start(bf16[256,256]{1,0:T(8,128)(2,1)} %param.20) | copy-start | bytes 393220
  3.5 43.5 %all-to-all-start = ((bf16[32,4,16,256]{3,2,1,0:T(8,128)(2,1)}), bf16[32,4,16,256]{3,2,1,0:T(8,128)(2,1)S(1)}, u32[]{:S(2)}, u32[]{:S(2)}) async-start(bf16[32,4,16,256]{3,2,1,0:T(8,128)(2,1)} %bitcast.1), calls=%async_computation | async-start | bytes 2097152 | tf_op jit(solution)/shard_map/all_to_all | solution.py:261
  16.9 30.0 %copy-start.1 = (bf16[256,256]{1,0:T(8,128)(2,1)S(1)}, bf16[256,256]{1,0:T(8,128)(2,1)}, u32[]{:S(2)}) copy-start(bf16[256,256]{1,0:T(8,128)(2,1)} %wo_ref.1) | copy-start | bytes 393220
  16.9 30.0 %copy-start.2 = (f32[256]{0:T(256)S(1)}, f32[256]{0:T(256)}, u32[]{:S(2)}) copy-start(f32[256]{0:T(256)} %param.19) | copy-start | bytes 3076
  17.0 30.0 %copy-start.3 = (f32[256]{0:T(256)S(1)}, f32[256]{0:T(256)}, u32[]{:S(2)}) copy-start(f32[256]{0:T(256)} %param.24) | copy-start | bytes 3076
  17.0 30.0 %copy-start.4 = (f32[256]{0:T(256)S(1)}, f32[256]{0:T(256)}, u32[]{:S(2)}) copy-start(f32[256]{0:T(256)} %param.26) | copy-start | bytes 3076
  17.0 30.0 %copy-start.5 = (f32[256]{0:T(256)S(1)}, f32[256]{0:T(256)}, u32[]{:S(2)}) copy-start(f32[256]{0:T(256)} %param.27) | copy-start | bytes 3076
  62.7 15.8 %copy-start = (bf16[4,32,512]{2,1,0:T(8,128)(2,1)}, bf16[4,32,512]{2,1,0:T(8,128)(2,1)S(1)}, u32[]{:S(2)}) copy-start(bf16[4,32,512]{2,1,0:T(8,128)(2,1)S(1)} %get-tuple-element.22.refs_0_) | copy-start | bytes 393220
  62.8 10.9 %collective-permute-start = (bf16[4,32,512]{2,1,0:T(8,128)(2,1)S(1)}, bf16[4,32,512]{2,1,0:T(8,128)(2,1)S(1)}, u32[]{:S(2)}, u32[]{:S(2)}) collective-permute-start(bf16[4,32,512]{2,1,0:T(8,128)(2,1)S(1)} %get-tuple-element.20), channel_id=1, source_target_pairs={{0,4},{1,5},{2,6},{3,7},{4,0},{5,1},{6,2},{7,3},{8,12},{9,13},{10,... | collective-permute-start | bytes 393224 | tf_op jit(solution)/shard_map/ppermute | solution.py:220
  63.8 14.8 %collective-permute-start.8 = (bf16[4,32,512]{2,1,0:T(8,128)(2,1)S(1)}, bf16[4,32,512]{2,1,0:T(8,128)(2,1)S(1)}, u32[]{:S(2)}, u32[]{:S(2)}) collective-permute-start(bf16[4,32,512]{2,1,0:T(8,128)(2,1)S(1)} %get-tuple-element.22.refs_0_), channel_id=1, source_target_pairs={{0,0},{1,64},{2,128},{3,192},{4,32},{5,96},{6,160},{7,224},{8,1},{... | collective-permute-start | bytes 393224 | tf_op jit(solution)/shard_map/ppermute | solution.py:220
  73.7 4.9 %copy-start.7 = (bf16[4,32,512]{2,1,0:T(8,128)(2,1)}, bf16[4,32,512]{2,1,0:T(8,128)(2,1)S(1)}, u32[]{:S(2)}) copy-start(bf16[4,32,512]{2,1,0:T(8,128)(2,1)S(1)} %collective-permute-done.refs_1_) | copy-start | bytes 393220
  73.7 11.3 %collective-permute-start.1 = (bf16[2,4,32,512]{3,2,1,0:T(8,128)(2,1)S(1)}, bf16[2,4,32,512]{3,2,1,0:T(8,128)(2,1)S(1)}, u32[]{:S(2)}, u32[]{:S(2)}) collective-permute-start(bf16[2,4,32,512]{3,2,1,0:T(8,128)(2,1)S(1)} %pad_maximum_fusion.2), channel_id=1, source_target_pairs={{0,1},{1,2},{2,3},{3,0},{4,5},{5,6},{6,7},{7,4},{8,9},{9,10},{10,1... | collective-permute-start | bytes 786440 | tf_op jit(solution)/shard_map/ppermute | solution.py:220
  74.4 11.3 %collective-permute-start.2 = (bf16[2,4,32,512]{3,2,1,0:T(8,128)(2,1)S(1)}, bf16[2,4,32,512]{3,2,1,0:T(8,128)(2,1)S(1)}, u32[]{:S(2)}, u32[]{:S(2)}) collective-permute-start(bf16[2,4,32,512]{3,2,1,0:T(8,128)(2,1)S(1)} %pad_maximum_fusion.2), channel_id=1, source_target_pairs={{0,3},{1,0},{2,1},{3,2},{4,7},{5,4},{6,5},{7,6},{8,11},{9,8},{10,9... | collective-permute-start | bytes 786440 | tf_op jit(solution)/shard_map/ppermute | solution.py:220
  77.7 8.8 %collective-permute-start.3 = (bf16[2,4,32,512]{3,2,1,0:T(8,128)(2,1)S(1)}, bf16[2,4,32,512]{3,2,1,0:T(8,128)(2,1)S(1)}, u32[]{:S(2)}, u32[]{:S(2)}) collective-permute-start(bf16[2,4,32,512]{3,2,1,0:T(8,128)(2,1)S(1)} %pad_maximum_fusion.2), channel_id=1, source_target_pairs={{0,2},{1,3},{2,0},{3,1},{4,6},{5,7},{6,4},{7,5},{8,10},{9,11},{10,... | collective-permute-start | bytes 786440 | tf_op jit(solution)/shard_map/ppermute | solution.py:220
  78.5 12.8 %collective-permute-start.9 = (bf16[4,32,512]{2,1,0:T(8,128)(2,1)}, bf16[4,32,512]{2,1,0:T(8,128)(2,1)S(1)}, u32[]{:S(2)}, u32[]{:S(2)}) collective-permute-start(bf16[4,32,512]{2,1,0:T(8,128)(2,1)} %shard_map.168), channel_id=1, source_target_pairs={{0,128},{1,192},{2,0},{3,64},{4,160},{5,224},{6,32},{7,96},{8,129}... | collective-permute-start | bytes 393224 | tf_op jit(solution)/shard_map/ppermute | solution.py:220
  87.2 17.3 %collective-permute-start.4 = (bf16[8,4,32,512]{3,2,1,0:T(8,128)(2,1)}, bf16[8,4,32,512]{3,2,1,0:T(8,128)(2,1)S(1)}, u32[]{:S(2)}, u32[]{:S(2)}) collective-permute-start(bf16[8,4,32,512]{3,2,1,0:T(8,128)(2,1)} %constant_dynamic-update-slice_fusion.refs_0_), channel_id=1, source_target_pairs={{0,8},{1,9},{2,10},{3,11},{4,12},{5,13},{6,14},{7,15},{8,16},{9,17... | collective-permute-start | bytes 3145736 | tf_op jit(solution)/shard_map/ppermute | solution.py:220
  91.3 16.3 %collective-permute-start.6 = (bf16[8,4,32,512]{3,2,1,0:T(8,128)(2,1)}, bf16[8,4,32,512]{3,2,1,0:T(8,128)(2,1)}, u32[]{:S(2)}, u32[]{:S(2)}) collective-permute-start(bf16[8,4,32,512]{3,2,1,0:T(8,128)(2,1)} %constant_dynamic-update-slice_fusion.refs_0_), channel_id=1, source_target_pairs={{0,24},{1,25},{2,26},{3,27},{4,28},{5,29},{6,30},{7,31},{8,0},{9,1... | collective-permute-start | bytes 3145736 | tf_op jit(solution)/shard_map/ppermute | solution.py:220
  91.3 8.3 %collective-permute-start.10 = (bf16[2,4,32,512]{3,2,1,0:T(8,128)(2,1)S(1)}, bf16[2,4,32,512]{3,2,1,0:T(8,128)(2,1)S(1)}, u32[]{:S(2)}, u32[]{:S(2)}) collective-permute-start(bf16[2,4,32,512]{3,2,1,0:T(8,128)(2,1)S(1)} %pad_maximum_fusion.3.a_ref), channel_id=1, source_target_pairs={{0,64},{1,65},{2,66},{3,67},{4,68},{5,69},{6,70},{7,71},{8,72},{9,... | collective-permute-start | bytes 786440 | tf_op jit(solution)/shard_map/ppermute | solution.py:220
  100.5 8.4 %copy-start.6 = (f32[128]{0:T(128)S(1)}, f32[128]{0:T(128)}, u32[]{:S(2)}) copy-start(f32[128]{0:T(128)} %param.31) | copy-start | bytes 1540
  100.5 2.1 %collective-permute-start.11 = (bf16[4,4,32,512]{3,2,1,0:T(8,128)(2,1)}, bf16[4,4,32,512]{3,2,1,0:T(8,128)(2,1)S(1)}, u32[]{:S(2)}, u32[]{:S(2)}) collective-permute-start(bf16[4,4,32,512]{3,2,1,0:T(8,128)(2,1)} %shard_map.169), channel_id=1, source_target_pairs={{0,32},{1,33},{2,34},{3,35},{4,36},{5,37},{6,38},{7,39},{8,40},{9,... | collective-permute-start | bytes 1572872 | tf_op jit(solution)/shard_map/ppermute | solution.py:220
  104.6 11.8 %collective-permute-start.5 = (bf16[4,4,32,512]{3,2,1,0:T(8,128)(2,1)S(1)}, bf16[4,4,32,512]{3,2,1,0:T(8,128)(2,1)S(1)}, u32[]{:S(2)}, u32[]{:S(2)}) collective-permute-start(bf16[4,4,32,512]{3,2,1,0:T(8,128)(2,1)S(1)} %slice.18), channel_id=1, source_target_pairs={{0,8},{1,9},{2,10},{3,11},{4,12},{5,13},{6,14},{7,15},{8,16},{9,17... | collective-permute-start | bytes 1572872 | tf_op jit(solution)/shard_map/ppermute | solution.py:220
  108.7 10.5 %collective-permute-start.7 = (bf16[4,4,32,512]{3,2,1,0:T(8,128)(2,1)S(1)}, bf16[4,4,32,512]{3,2,1,0:T(8,128)(2,1)S(1)}, u32[]{:S(2)}, u32[]{:S(2)}) collective-permute-start(bf16[4,4,32,512]{3,2,1,0:T(8,128)(2,1)S(1)} %slice.19), channel_id=1, source_target_pairs={{0,24},{1,25},{2,26},{3,27},{4,28},{5,29},{6,30},{7,31},{8,0},{9,1... | collective-permute-start | bytes 1572872 | tf_op jit(solution)/shard_map/ppermute | solution.py:220
